TPU v7x, 512 devices: a whole 4x8x8 slice. The times are simulated.
512 devices in a mesh: seq: 32 (over y, x), section: 16 (over z, core).
Axes of the slice: x: 4, y: 8, z: 8, core: 2. Of those that a mesh axis runs over, the one named last changes fastest.
Arguments:
- fwd_input: bfloat16 [16, 2048, 1024], P('section', 'seq'), may hold values from -6 to 6
- bwd_input: bfloat16 [16, 2048, 1024], P('section', 'seq'), may hold values from -6 to 6
- bwd_grad: float32 [16, 2048, 1024], P('section', 'seq'), may hold values from -6 to 6
- norm_gain: float32 [16, 1024], P('section'), may hold values from 0.5 to 2.5
- w_query: bfloat16 [16, 1024, 1024], P('section', 'seq'), may hold values from -1 to 1
- w_key: bfloat16 [16, 1024, 1024], P('section', 'seq'), may hold values from -1 to 1
- w_value: bfloat16 [16, 1024, 1024], P('section', 'seq'), may hold values from -0.1875 to 0.1875
- w_out: bfloat16 [16, 1024, 1024], P('section', 'seq'), may hold values from -0.1875 to 0.1875
Outputs:
- next_input: bfloat16 [16, 2048, 1024], P('section', 'seq')
- prev_grad: float32 [16, 2048, 1024], P('section', 'seq')
All inputs are finite; a program needn't handle non-finite values.
Results may differ from a plain program's by a relative error of at most 0.024.
Values may be sent and summed in bfloat16 or wider, within the bound.
No kernel may reach another device: no remote copies, remote signals or barrier semaphores. Data moves between devices by JAX's collectives and lax.ppermute only.
A program may use at most 64 MiB of HBM per device.

v0:
```python
import jax
import jax.numpy as jnp
from jax import lax
from jax.sharding import PartitionSpec as P

HEADS = 16
HEAD = 64
INNER = 1024
LEVELS = 3


NEG = -1e30
EPS = 1e-06


def swapped(value, axis, distance):
    mask = 2**distance
    pairs = [(source, source ^ mask) for source in range(lax.axis_size(axis))]
    return lax.ppermute(value, axis, pairs)


def from_behind(value, axis, steps):
    count = lax.axis_size(axis)
    pairs = [(source, (source + steps) % count) for source in range(count)]
    return lax.ppermute(value, axis, pairs)


def normalize(x, gain):
    xf = x.astype(jnp.float32)
    inv = lax.rsqrt(jnp.mean(xf * xf, axis=-1, keepdims=True) + EPS)
    return ((xf * inv * gain).astype(jnp.bfloat16), xf, inv)


def project(normed, weights):
    outputs = []
    for matrix in weights[:3]:
        outputs.append(
            jnp.dot(normed, matrix, preferred_element_type=jnp.float32).astype(jnp.bfloat16)
        )
    return outputs


def choose(array, rate):
    rows = array.shape[0]
    shaped = array.reshape(rows // rate, rate, HEADS, array.shape[1] // HEADS)
    hit = (jnp.arange(rate)[:, None] == (jnp.arange(HEADS) % rate)[None, :])[None, :, :, None]
    return jnp.sum(jnp.where(hit, shaped, jnp.zeros((), array.dtype)), axis=1)


def choose_stats(array, rate):
    rows = array.shape[0]
    shaped = array.reshape(rows // rate, rate, HEADS)
    hit = (jnp.arange(rate)[:, None] == (jnp.arange(HEADS) % rate)[None, :])[None]
    return jnp.sum(jnp.where(hit, shaped, 0.0), axis=1)


def expand(array, rate, fill):
    hit = jnp.arange(rate)[:, None] == (jnp.arange(HEADS) % rate)[None, :]
    hit = hit.reshape((1, rate, HEADS) + (1,) * (array.ndim - 2))
    full = jnp.where(hit, array[:, None], fill)
    return full.reshape((array.shape[0] * rate,) + array.shape[1:])


def merge_halves(mine, other, bit, position):
    lower = position // 2**bit % 2 == 0
    return jnp.where(lower, jnp.concatenate((mine, other), 1), jnp.concatenate((other, mine), 1))


def gather_keys(pieces, position):
    result = []
    for index, block in enumerate(pieces):
        for bit in range(index + 1):
            other = swapped(block, "seq", bit)
            block = merge_halves(block, other, bit, position)
        result.append(block)
    return result


def gather_queries(pieces, stats, position):
    blocks, extras = ([], [])
    for index in range(len(pieces)):
        block, extra = (pieces[index], stats[index])
        for bit in range(index + 1):
            other, other_stats = (
                swapped(block, "seq", bit),
                swapped(extra.astype(jnp.bfloat16), "seq", bit).astype(extra.dtype),
            )
            block = merge_halves(block, other, bit, position)
            extra = merge_halves(extra, other_stats, bit, position)
        blocks.append(block)
        extras.append(extra)
    return (blocks, extras)


def attend(query, keys, values, position):
    rows = query.shape[0]
    scale = HEAD ** (-0.5)
    pieces = []
    for level in range(1, LEVELS):
        rate = 2**level
        pieces.append(
            jnp.stack((choose(keys, rate), choose(values, rate))).reshape(2, rows // rate, INNER)
        )
    gathered = [jnp.stack((keys, values))] + gather_keys(pieces, position)
    for level in range(LEVELS):
        rate = 2**level
        count = rows // rate
        mine = choose(query, rate)
        group_k = gathered[level][0].reshape(rows, HEADS, HEAD)
        group_v = gathered[level][1].reshape(rows, HEADS, HEAD)
        start = position % rate * count
        causal = (start + jnp.arange(count))[:, None] >= jnp.arange(rows)[None, :]
        scores = (
            jnp.einsum("thd,uhd->htu", mine, group_k, preferred_element_type=jnp.float32) * scale
        )
        scores = jnp.where(causal, scores, NEG)
        top = jnp.max(scores, axis=-1)
        weights = jnp.where(causal, jnp.exp(scores - top[..., None]), 0.0)
        total = jnp.sum(weights, axis=-1)
        accum = jnp.einsum(
            "htu,uhd->thd",
            weights.astype(jnp.bfloat16),
            group_v,
            preferred_element_type=jnp.float32,
        )
        top = expand(top.T, rate, NEG)
        total = expand(total.T, rate, 0.0)
        accum = expand(accum, rate, 0.0)
        if level == 0:
            biggest, denom, numer = (top, total, accum)
        else:
            newest = jnp.maximum(biggest, top)
            old_factor = jnp.exp(biggest - newest)
            new_factor = jnp.exp(top - newest)
            denom = old_factor * denom + new_factor * total
            numer = old_factor[..., None] * numer + new_factor[..., None] * accum
            biggest = newest
    attended = (numer / denom[..., None]).astype(jnp.bfloat16).reshape(rows, INNER)
    return (attended, biggest + jnp.log(denom), gathered)


def backward_layer(x, grad, gain, weights, position):
    rows = x.shape[0]
    scale = HEAD ** (-0.5)
    normed, xf, inv = normalize(x, gain)
    query, keys, values = project(normed, weights)
    attended, lse, gathered = attend(query, keys, values, position)
    contract = (((1,), (1,)), ((), ()))
    d_att = lax.dot_general(
        grad.astype(jnp.bfloat16), weights[3], contract, preferred_element_type=jnp.float32
    ).astype(jnp.bfloat16)
    delta = jnp.sum(
        (d_att.astype(jnp.float32) * attended.astype(jnp.float32)).reshape(rows, HEADS, HEAD),
        axis=-1,
    )
    pieces, stats = ([], [])
    for level in range(1, LEVELS):
        rate = 2**level
        pieces.append(
            jnp.stack((choose(query, rate), choose(d_att, rate))).reshape(2, rows // rate, INNER)
        )
        stats.append(jnp.stack((choose_stats(lse, rate), choose_stats(delta, rate))))
    blocks, extras = gather_queries(pieces, stats, position)
    blocks = [jnp.stack((query, d_att))] + blocks
    extras = [jnp.stack((lse, delta))] + extras
    grad_q = jnp.zeros((rows, HEADS, HEAD), jnp.float32)
    grad_k = jnp.zeros((rows, HEADS, HEAD), jnp.float32)
    grad_v = jnp.zeros((rows, HEADS, HEAD), jnp.float32)
    for level in range(LEVELS):
        rate = 2**level
        count = rows // rate
        start = position % rate * count
        mine_q, mine_d = (choose(query, rate), choose(d_att, rate))
        mine_l, mine_e = (
            choose_stats(lse, rate).T[..., None],
            choose_stats(delta, rate).T[..., None],
        )
        group_k = gathered[level][0].reshape(rows, HEADS, HEAD)
        group_v = gathered[level][1].reshape(rows, HEADS, HEAD)
        causal = (start + jnp.arange(count))[:, None] >= jnp.arange(rows)[None, :]
        scores = (
            jnp.einsum("thd,uhd->htu", mine_q, group_k, preferred_element_type=jnp.float32) * scale
        )
        prob = jnp.where(causal, jnp.exp(jnp.where(causal, scores, NEG) - mine_l), 0.0)
        dprob = jnp.einsum("thd,uhd->htu", mine_d, group_v, preferred_element_type=jnp.float32)
        dscore = (prob * (dprob - mine_e)).astype(jnp.bfloat16)
        part_q = (
            jnp.einsum("htu,uhd->thd", dscore, group_k, preferred_element_type=jnp.float32) * scale
        )
        grad_q = grad_q + expand(part_q, rate, 0.0)
        own_k, own_v = (choose(keys, rate), choose(values, rate))
        group_q = blocks[level][0].reshape(rows, HEADS, HEAD)
        group_d = blocks[level][1].reshape(rows, HEADS, HEAD)
        group_l, group_e = (extras[level][0].T[..., None], extras[level][1].T[..., None])
        reach = jnp.arange(rows)[:, None] >= (start + jnp.arange(count))[None, :]
        scores_k = (
            jnp.einsum("thd,uhd->htu", group_q, own_k, preferred_element_type=jnp.float32) * scale
        )
        prob_k = jnp.where(reach, jnp.exp(jnp.where(reach, scores_k, NEG) - group_l), 0.0)
        dprob_k = jnp.einsum("thd,uhd->htu", group_d, own_v, preferred_element_type=jnp.float32)
        dscore_k = (prob_k * (dprob_k - group_e)).astype(jnp.bfloat16)
        part_v = jnp.einsum(
            "htu,thd->uhd", prob_k.astype(jnp.bfloat16), group_d, preferred_element_type=jnp.float32
        )
        part_k = (
            jnp.einsum("htu,thd->uhd", dscore_k, group_q, preferred_element_type=jnp.float32)
            * scale
        )
        grad_v = grad_v + expand(part_v, rate, 0.0)
        grad_k = grad_k + expand(part_k, rate, 0.0)
    grad_n = jnp.zeros((rows, x.shape[1]), jnp.float32)
    for part, matrix in zip((grad_q, grad_k, grad_v), weights[:3]):
        flat = part.astype(jnp.bfloat16).reshape(rows, INNER)
        grad_n = grad_n + lax.dot_general(
            flat, matrix, contract, preferred_element_type=jnp.float32
        )
    scaled = grad_n * gain
    nhat = xf * inv
    return grad + inv * (scaled - nhat * jnp.mean(scaled * nhat, axis=-1, keepdims=True))


def per_device(fwd_input, bwd_input, bwd_grad, norm_gain, w_query, w_key, w_value, w_out):
    position = lax.axis_index("seq")
    whole = (
        lax.all_gather(w_query, "seq", axis=1, tiled=True),
        lax.all_gather(w_key, "seq", axis=1, tiled=True),
        lax.all_gather(w_value, "seq", axis=1, tiled=True),
        lax.all_gather(w_out, "seq", axis=1, tiled=True),
    )
    weights = tuple((matrix[0] for matrix in whole))
    gain = norm_gain[0]
    normed, xf, inv = normalize(fwd_input[0], gain)
    query, keys, values = project(normed, weights)
    attended, lse, gathered = attend(query, keys, values, position)
    mixed = jnp.dot(attended, weights[3], preferred_element_type=jnp.float32)
    layer_out = (xf + mixed).astype(jnp.bfloat16)
    input_grad = backward_layer(bwd_input[0], bwd_grad[0], gain, weights, position)
    next_input = from_behind(layer_out[None], "section", 1)
    prev_grad = from_behind(input_grad[None].astype(jnp.bfloat16), "section", -1).astype(
        jnp.float32
    )
    return (next_input, prev_grad)


def solution(mesh):
    placed = (
        P("section", "seq", None),
        P("section", "seq", None),
        P("section", "seq", None),
        P("section", None),
        P("section", "seq", None),
        P("section", "seq", None),
        P("section", "seq", None),
        P("section", "seq", None),
    )
    return jax.shard_map(
        per_device,
        mesh=mesh,
        in_specs=placed,
        out_specs=(P("section", "seq", None), P("section", "seq", None)),
        check_vma=False,
    )
```

profile of v0, /device:TPU:1, one launch (start us, length us, event | category | flops | bytes accessed | tf_op | source)
XLA Modules:
  0.0 649.2 jit_solution(9043209634404523814)
XLA Ops:
  19.5 76.8 %all-gather.9.cloned.1.call-done = bf16[1,1024,1024]{2,1,0:T(8,128)(2,1)} async-done(((bf16[1,32,1024]{2,1,0:T(8,128)(2,1)}), bf16[1,1024,1024]{2,1,0:T(8,128)(2,1)}) %all-gather.9.cloned.1.call-update) | async-done | bytes 2097168 | tf_op jit(solution)/shard_map/all_gather | solution.py:227
  100.2 79.9 %all-gather.11.cloned.1.call-done = bf16[1,1024,1024]{2,1,0:T(8,128)(2,1)} async-done(((bf16[1,32,1024]{2,1,0:T(8,128)(2,1)}), bf16[1,1024,1024]{2,1,0:T(8,128)(2,1)}) %all-gather.11.cloned.1.call-update) | async-done | bytes 2097168 | tf_op jit(solution)/shard_map/all_gather | solution.py:228
  180.1 2.3 fusion.89
  183.6 80.5 %all-gather.7.cloned.1.call-done = bf16[1,1024,1024]{2,1,0:T(8,128)(2,1)} async-done(((bf16[1,32,1024]{2,1,0:T(8,128)(2,1)}), bf16[1,1024,1024]{2,1,0:T(8,128)(2,1)}) %all-gather.7.cloned.1.call-update) | async-done | bytes 2097168 | tf_op jit(solution)/shard_map/all_gather | solution.py:226
  268.9 78.9 %all-gather.5.cloned.1.call-done = bf16[1,1024,1024]{2,1,0:T(8,128)(2,1)} async-done(((bf16[1,32,1024]{2,1,0:T(8,128)(2,1)}), bf16[1,1024,1024]{2,1,0:T(8,128)(2,1)}) %all-gather.5.cloned.1.call-update) | async-done | bytes 2097168 | tf_op jit(solution)/shard_map/all_gather | solution.py:225
  365.9 2.8 select_reduce_fusion.2
  373.4 3.0 select_reduce_fusion.1
  379.8 3.3 collective-permute-start
  389.8 3.3 collective-permute-start.5
  411.9 3.3 collective-permute-start.7
  416.8 2.7 collective-permute-start.2
  421.2 4.2 collective-permute-start.6
  427.1 2.7 collective-permute-start.10
  429.8 2.2 maximum_select_fusion
  483.9 2.5 fusion.286
  511.3 2.3 fusion.43
  516.3 2.8 fusion.92
  519.1 8.4 %collective-permute-start.3 = (bf16[1,64,1024]{2,1,0:T(8,128)(2,1)}, bf16[1,64,1024]{2,1,0:T(8,128)(2,1)}, u32[]{:S(2)}, u32[]{:S(2)}) collective-permute-start(bf16[1,64,1024]{2,1,0:T(8,128)(2,1)} %fusion.92), channel_id=1, source_target_pairs={{0,1},{1,2},{2,3},{3,4},{4,5},{5,6},{6,7},{7,8},{8,9},{9,10},{10,1... | collective-permute-start | bytes 393224 | tf_op jit(solution)/shard_map/ppermute | solution.py:25
  568.3 2.4 convert_multiply_fusion.2
  586.4 2.4 collective-permute-start.11
  590.1 3.0 collective-permute-start.8
  609.6 3.9 collective-permute-start.12
  617.6 2.3 fusion.56
  636.1 4.4 collective-permute-done.13
  (336 shorter events, 254.0 us)
Async XLA Ops:
  7.2 89.1 %all-gather.9.cloned.1.call-start = ((), (), s32[]{:S(2)}) async-start(), calls=%async_computation.2 | async-start | bytes 2162688 | tf_op jit(solution)/shard_map/all_gather | solution.py:227
  7.9 172.2 %all-gather.11.cloned.1.call-start = ((), (), s32[]{:S(2)}) async-start(), calls=%async_computation.3 | async-start | bytes 2162688 | tf_op jit(solution)/shard_map/all_gather | solution.py:228
  8.6 255.4 %all-gather.7.cloned.1.call-start = ((), (), s32[]{:S(2)}) async-start(), calls=%async_computation.1 | async-start | bytes 2162688 | tf_op jit(solution)/shard_map/all_gather | solution.py:226
  9.4 338.5 %all-gather.5.cloned.1.call-start = ((), (), s32[]{:S(2)}) async-start(), calls=%async_computation | async-start | bytes 2162688 | tf_op jit(solution)/shard_map/all_gather | solution.py:225
  11.3 168.9 %copy-start.10 = (f32[1,64,1024]{2,1,0:T(8,128)S(1)}, f32[1,64,1024]{2,1,0:T(8,128)}, u32[]{:S(2)}) copy-start(f32[1,64,1024]{2,1,0:T(8,128)} %param.10) | copy-start | bytes 786436
  16.8 247.3 %copy-start.42 = (f32[64]{0:T(128)}, f32[64]{0:T(128)S(1)}, u32[]{:S(2)}) copy-start(f32[64]{0:T(128)S(1)} %add_rsqrt_fusion.1) | copy-start | bytes 772
  16.9 338.9 %copy-start.36 = (f32[64]{0:T(128)}, f32[64]{0:T(128)S(1)}, u32[]{:S(2)}) copy-start(f32[64]{0:T(128)S(1)} %add_rsqrt_fusion) | copy-start | bytes 772
  98.4 165.7 %copy-start.4 = (bf16[1,64,1024]{2,1,0:T(8,128)(2,1)S(1)}, bf16[1,64,1024]{2,1,0:T(8,128)(2,1)}, u32[]{:S(2)}) copy-start(bf16[1,64,1024]{2,1,0:T(8,128)(2,1)} %param.8) | copy-start | bytes 393220
  98.4 165.6 %copy-start.22 = (f32[1,1024]{1,0:T(1,128)S(1)}, f32[1,1024]{1,0:T(1,128)}, u32[]{:S(2)}) copy-start(f32[1,1024]{1,0:T(1,128)} %param.11) | copy-start | bytes 12292
  182.5 165.4 %copy-start.3 = (bf16[1,64,1024]{2,1,0:T(8,128)(2,1)S(1)}, bf16[1,64,1024]{2,1,0:T(8,128)(2,1)}, u32[]{:S(2)}) copy-start(bf16[1,64,1024]{2,1,0:T(8,128)(2,1)} %param.9) | copy-start | bytes 393220
  371.5 40.4 %collective-permute-start.1 = (bf16[2,16,1024]{2,1,0:T(8,128)(2,1)}, bf16[2,16,1024]{2,1,0:T(8,128)(2,1)}, u32[]{:S(2)}, u32[]{:S(2)}) collective-permute-start(bf16[2,16,1024]{2,1,0:T(8,128)(2,1)} %constant_dynamic-update-slice_fusion.2), channel_id=1, source_target_pairs={{0,16},{16,0},{32,48},{48,32},{64,80},{80,64},{96,112},{112,96},{1... | collective-permute-start | bytes 196616 | tf_op jit(solution)/shard_map/ppermute | solution.py:19
  379.8 47.3 %collective-permute-start = (bf16[2,32,1024]{2,1,0:T(8,128)(2,1)}, bf16[2,32,1024]{2,1,0:T(8,128)(2,1)}, u32[]{:S(2)}, u32[]{:S(2)}) collective-permute-start(bf16[2,32,1024]{2,1,0:T(8,128)(2,1)} %constant_dynamic-update-slice_fusion), channel_id=1, source_target_pairs={{0,16},{16,0},{32,48},{48,32},{64,80},{80,64},{96,112},{112,96},{1... | collective-permute-start | bytes 393224 | tf_op jit(solution)/shard_map/ppermute | solution.py:19
  385.6 44.2 %collective-permute-start.4 = (bf16[2,32,1024]{2,1,0:T(8,128)(2,1)}, bf16[2,32,1024]{2,1,0:T(8,128)(2,1)}, u32[]{:S(2)}, u32[]{:S(2)}) collective-permute-start(bf16[2,32,1024]{2,1,0:T(8,128)(2,1)} %constant_dynamic-update-slice_fusion.4), channel_id=1, source_target_pairs={{0,16},{16,0},{32,48},{48,32},{64,80},{80,64},{96,112},{112,96},{1... | collective-permute-start | bytes 393224 | tf_op jit(solution)/shard_map/ppermute | solution.py:19
  389.8 27.0 %collective-permute-start.5 = (bf16[2,16,1024]{2,1,0:T(8,128)(2,1)}, bf16[2,16,1024]{2,1,0:T(8,128)(2,1)}, u32[]{:S(2)}, u32[]{:S(2)}) collective-permute-start(bf16[2,16,1024]{2,1,0:T(8,128)(2,1)} %constant_dynamic-update-slice_fusion.6), channel_id=1, source_target_pairs={{0,16},{16,0},{32,48},{48,32},{64,80},{80,64},{96,112},{112,96},{1... | collective-permute-start | bytes 196616 | tf_op jit(solution)/shard_map/ppermute | solution.py:19
  395.4 25.8 %collective-permute-start.9 = (bf16[2,16,1024]{2,1,0:T(8,128)(2,1)}, bf16[2,16,1024]{2,1,0:T(8,128)(2,1)}, u32[]{:S(2)}, u32[]{:S(2)}) collective-permute-start(bf16[2,16,1024]{2,1,0:T(8,128)(2,1)} %constant_dynamic-update-slice_fusion.10), channel_id=1, source_target_pairs={{0,16},{16,0},{32,48},{48,32},{64,80},{80,64},{96,112},{112,96},{1... | collective-permute-start | bytes 196616 | tf_op jit(solution)/shard_map/ppermute | solution.py:19
  411.9 55.2 %collective-permute-start.7 = (bf16[2,32,1024]{2,1,0:T(8,128)(2,1)}, bf16[2,32,1024]{2,1,0:T(8,128)(2,1)}, u32[]{:S(2)}, u32[]{:S(2)}) collective-permute-start(bf16[2,32,1024]{2,1,0:T(8,128)(2,1)} %constant_dynamic-update-slice_fusion.8), channel_id=1, source_target_pairs={{0,16},{16,0},{32,48},{48,32},{64,80},{80,64},{96,112},{112,96},{1... | collective-permute-start | bytes 393224 | tf_op jit(solution)/shard_map/ppermute | solution.py:19
  416.8 57.8 %collective-permute-start.2 = (bf16[2,32,1024]{2,1,0:T(8,128)(2,1)}, bf16[2,32,1024]{2,1,0:T(8,128)(2,1)}, u32[]{:S(2)}, u32[]{:S(2)}) collective-permute-start(bf16[2,32,1024]{2,1,0:T(8,128)(2,1)} %maximum_select_fusion.6), channel_id=1, source_target_pairs={{0,32},{16,48},{32,0},{48,16},{64,96},{80,112},{96,64},{112,80},{1... | collective-permute-start | bytes 393224 | tf_op jit(solution)/shard_map/ppermute | solution.py:19
  421.2 59.0 %collective-permute-start.6 = (bf16[2,32,1024]{2,1,0:T(8,128)(2,1)}, bf16[2,32,1024]{2,1,0:T(8,128)(2,1)}, u32[]{:S(2)}, u32[]{:S(2)}) collective-permute-start(bf16[2,32,1024]{2,1,0:T(8,128)(2,1)} %maximum_select_fusion.7), channel_id=1, source_target_pairs={{0,32},{16,48},{32,0},{48,16},{64,96},{80,112},{96,64},{112,80},{1... | collective-permute-start | bytes 393224 | tf_op jit(solution)/shard_map/ppermute | solution.py:19
  427.1 100.4 %collective-permute-start.10 = (bf16[2,32,1024]{2,1,0:T(8,128)(2,1)}, bf16[2,32,1024]{2,1,0:T(8,128)(2,1)}, u32[]{:S(2)}, u32[]{:S(2)}) collective-permute-start(bf16[2,32,1024]{2,1,0:T(8,128)(2,1)} %maximum_select_fusion.8), channel_id=1, source_target_pairs={{0,32},{16,48},{32,0},{48,16},{64,96},{80,112},{96,64},{112,80},{1... | collective-permute-start | bytes 393224 | tf_op jit(solution)/shard_map/ppermute | solution.py:19
  519.1 117.0 %collective-permute-start.3 = (bf16[1,64,1024]{2,1,0:T(8,128)(2,1)}, bf16[1,64,1024]{2,1,0:T(8,128)(2,1)}, u32[]{:S(2)}, u32[]{:S(2)}) collective-permute-start(bf16[1,64,1024]{2,1,0:T(8,128)(2,1)} %fusion.92), channel_id=1, source_target_pairs={{0,1},{1,2},{2,3},{3,4},{4,5},{5,6},{6,7},{7,8},{8,9},{9,10},{10,1... | collective-permute-start | bytes 393224 | tf_op jit(solution)/shard_map/ppermute | solution.py:25
  586.4 21.1 %collective-permute-start.11 = (bf16[2,16,16]{1,2,0:T(8,128)(2,1)}, bf16[2,16,16]{1,2,0:T(8,128)(2,1)}, u32[]{:S(2)}, u32[]{:S(2)}) collective-permute-start(bf16[2,16,16]{1,2,0:T(8,128)(2,1)} %maximum_convert_fusion.1), channel_id=1, source_target_pairs={{0,16},{16,0},{32,48},{48,32},{64,80},{80,64},{96,112},{112,96},{1... | collective-permute-start | bytes 3080 | tf_op jit(solution)/shard_map/ppermute | solution.py:19
  590.1 23.3 %collective-permute-start.8 = (bf16[2,32,16]{1,2,0:T(8,128)(2,1)}, bf16[2,32,16]{1,2,0:T(8,128)(2,1)}, u32[]{:S(2)}, u32[]{:S(2)}) collective-permute-start(bf16[2,32,16]{1,2,0:T(8,128)(2,1)} %maximum_convert_fusion), channel_id=1, source_target_pairs={{0,16},{16,0},{32,48},{48,32},{64,80},{80,64},{96,112},{112,96},{1... | collective-permute-start | bytes 6152 | tf_op jit(solution)/shard_map/ppermute | solution.py:19
  609.6 11.5 %collective-permute-start.12 = (bf16[2,32,16]{1,2,0:T(8,128)(2,1)}, bf16[2,32,16]{1,2,0:T(8,128)(2,1)}, u32[]{:S(2)}, u32[]{:S(2)}) collective-permute-start(bf16[2,32,16]{1,2,0:T(8,128)(2,1)} %get-tuple-element.32), channel_id=1, source_target_pairs={{0,32},{16,48},{32,0},{48,16},{64,96},{80,112},{96,64},{112,80},{1... | collective-permute-start | bytes 6152 | tf_op jit(solution)/shard_map/ppermute | solution.py:19
  636.0 4.4 collective-permute-start.13
  (38 other events, 261.3 us)
Sparse Core Ops, SparseCore 0:
  11.2 85.0 all-gather.8
  99.4 80.7 all-gather.10
  183.3 80.7 all-gather.6
  267.1 80.7 all-gather.4
where the time goes:
time: 655 us; the launch traced here: 649 us
  waiting for transfers between devices  323 us (49%)
  local copies, waits for them, and re-layouts  168 us (26%)
  matrix products  55.3 us (8%)
  other arithmetic  44.7 us (7%)
  starting transfers between devices  43.4 us (7%)
  between operations  14.8 us (2%)
    all_gather x1, waiting for transfers between devices, per_device(): lax.all_gather(w_key, 'seq', axis=1, tiled=True)  80.5 us
    all_gather x1, waiting for transfers between devices, per_device(): lax.all_gather(w_out, 'seq', axis=1, tiled=True)  79.9 us
    all_gather x1, waiting for transfers between devices, per_device(): lax.all_gather(w_query, 'seq', axis=1, tiled=True)  78.9 us
    all_gather x1, waiting for transfers between devices, per_device(): lax.all_gather(w_value, 'seq', axis=1, tiled=True)  76.8 us
    broadcast_in_dim x37, local copies, waits for them, and re-layouts, expand(): full = jnp.where(hit, array[:, None], fill)  38.5 us
    ppermute x12, starting transfers between devices, swapped(): return lax.ppermute(value, axis, pairs)  34.8 us
    reshape x17, local copies, waits for them, and re-layouts, choose(): shaped = array.reshape(rows // rate, rate, HEADS, array.shape[1] // HEADS)  13.8 us
    select_n x10, other arithmetic, merge_halves(): jnp.where(lower, jnp.concatenate((mine, other), 1), jnp.concatenate((othe...  13.5 us
  transfers between devices with their start and end apart: 18, of which 5 were waited for; matrix products, arithmetic and copies ran while one was open for 37% of the time, Pallas kernels for 0%

commit v1 on v0

v1 whole, which is shorter than its diff:
```python
import functools
import math

import jax
import jax.numpy as jnp
from jax import lax
from jax.experimental import pallas as pl
from jax.experimental.pallas import tpu as pltpu
from jax.sharding import PartitionSpec as P

HEAD = 64
EPS = 1e-06
NEG = -1e30
GROUP = 4
HEADS = 4

F32 = jnp.float32
BF16 = jnp.bfloat16
NT = (((1,), (1,)), ((), ()))
NN = (((1,), (0,)), ((), ()))
TN = (((0,), (0,)), ((), ()))


def mm(a, b, dims):
    return lax.dot_general(a, b, dims, preferred_element_type=F32)


def pair_bias(rows):
    t = lax.broadcasted_iota(jnp.int32, (rows, rows), 0)
    u = lax.broadcasted_iota(jnp.int32, (rows, rows), 1)
    causal = u <= t
    apart = t ^ u
    one = causal & (apart < 64)
    two = causal & (apart < 128) & ((apart & 1) == 0)
    three = causal & (apart < 256) & ((apart & 3) == 0)
    biases = []
    for head in range(HEADS):
        count = one.astype(jnp.int32)
        count = count + (two & ((t & 1) == head % 2)).astype(jnp.int32)
        count = count + (three & ((t & 3) == head)).astype(jnp.int32)
        bias = jnp.where(count == 1, 0.0, NEG)
        bias = jnp.where(count == 2, math.log(2.0), bias)
        bias = jnp.where(count == 3, math.log(3.0), bias)
        biases.append(bias)
    return biases


def head_masks(rows):
    lane = lax.broadcasted_iota(jnp.int32, (rows, HEADS * HEAD), 1)
    return [(lane // HEAD) == head for head in range(HEADS)]


def only(mask, value):
    return jnp.where(mask, value, jnp.zeros((), value.dtype))


def pack(q_hbm, k_hbm, v_hbm, o_hbm, fwd_hbm, bwd_hbm, grad_hbm, qkv_out, own_out, tok_out, *scratch):
    grad_ref, sems, more = scratch
    copies = []

    def begin(source, target, sem):
        copies.append(pltpu.make_async_copy(source, target, sem))
        copies[-1].start()

    for block in range(GROUP):
        columns = slice(256 * block, 256 * block + 256)
        for i, ref in enumerate((q_hbm, k_hbm, v_hbm, o_hbm)):
            target = own_out.at[block, 0] if i == 3 else qkv_out.at[block, i]
            begin(ref.at[:, columns], target, sems.at[block, i])
    begin(fwd_hbm, tok_out.at[0], more.at[0])
    begin(bwd_hbm, tok_out.at[1], more.at[1])
    begin(grad_hbm, grad_ref, more.at[2])
    for copy in copies:
        copy.wait()
    tok_out[2] = grad_ref[...].astype(BF16)


def finish(parts_ref, fwd_ref, grad_ref, next_ref, prev_ref):
    for which, own, out in ((0, fwd_ref, next_ref), (1, grad_ref, prev_ref)):
        total = own[...].astype(F32)
        for part in range(GROUP):
            total = total + parts_ref[part, which].astype(F32)
        out[...] = total.astype(BF16)


def layer(me_ref, qkv_hbm, own_hbm, gain_ref, *refs):
    tok_hbm = refs[:GROUP]
    out_hbm, tok_ref, out_ref, w_ref, bias_ref, sems = refs[GROUP:]
    rows = GROUP * 64
    order = {}

    def begin(name, source, target, sem):
        order.setdefault(name, []).append(pltpu.make_async_copy(source, target, sem))
        order[name][-1].start()

    def wait(name):
        for copy in order[name]:
            copy.wait()

    def load_tokens(which, name):
        for k in range(GROUP):
            place = (me_ref[0] + GROUP - k) % GROUP
            begin(name, tok_hbm[k].at[which], tok_ref.at[which, place], sems.at[which, k])

    load_tokens(0, "x")
    begin("q", qkv_hbm.at[:, :, 0], w_ref.at[0], sems.at[3, 0])
    begin("k", qkv_hbm.at[:, :, 1], w_ref.at[1], sems.at[3, 1])
    begin("v", qkv_hbm.at[:, :, 2], w_ref.at[2], sems.at[3, 2])
    begin("o", own_hbm, w_ref.at[3], sems.at[3, 3])
    load_tokens(1, "y")
    load_tokens(2, "g")

    for head, bias in enumerate(pair_bias(rows)):
        bias_ref[head] = bias
    heads = head_masks(rows)
    scale = jnp.asarray(HEAD**-0.5, BF16)

    def weight(i):
        return w_ref[i].reshape(1024, 256)

    def out_weight(c):
        return w_ref[3, :, c].reshape(256, 256)

    def normed_of(which):
        xf = tok_ref[which].reshape(rows, 1024).astype(F32)
        inv = lax.rsqrt(jnp.mean(xf * xf, axis=-1, keepdims=True) + EPS)
        return (xf * inv * gain_ref[...]).astype(BF16), inv

    def prob_of(q_head, k, head):
        s = mm(q_head, k, NT) + bias_ref[head]
        top = jnp.max(s, axis=-1, keepdims=True)
        p = jnp.exp(s - top)
        return p * (1.0 / jnp.sum(p, axis=-1, keepdims=True))

    wait("x")
    normed, _ = normed_of(0)
    wait("q")
    q = mm(normed, weight(0), NN).astype(BF16) * scale
    wait("k")
    k = mm(normed, weight(1), NN).astype(BF16)
    wait("v")
    v = mm(normed, weight(2), NN).astype(BF16)
    attended = jnp.zeros((rows, 256), F32)
    for head in range(HEADS):
        p = prob_of(only(heads[head], q), k, head).astype(BF16)
        attended = attended + mm(p, only(heads[head], v), NN)
    attended = attended.astype(BF16)
    wait("o")
    for c in range(4):
        part = mm(attended, out_weight(c), NN).astype(BF16)
        for to in range(GROUP):
            out_ref[to, 0, :, 256 * c : 256 * c + 256] = part[64 * to : 64 * to + 64]
    begin("out", out_ref.at[:, 0], out_hbm.at[:, 0], sems.at[4, 0])

    wait("y")
    normed, inv = normed_of(1)
    q, k, v = [mm(normed, weight(i), NN).astype(BF16) for i in range(3)]
    q = q * scale
    wait("g")
    grads = tok_ref[2].reshape(rows, 1024)
    d_att = jnp.zeros((rows, 256), F32)
    for c in range(4):
        d_att = d_att + mm(grads[:, 256 * c : 256 * c + 256], out_weight(c), NT)
    d_att = d_att.astype(BF16)
    dq = jnp.zeros((rows, 256), F32)
    dk = jnp.zeros((rows, 256), F32)
    dv = jnp.zeros((rows, 256), F32)
    for head in range(HEADS):
        mask = heads[head]
        q_head = only(mask, q)
        p = prob_of(q_head, k, head)
        d_head = only(mask, d_att)
        dp = mm(d_head, v, NT)
        delta = jnp.sum(p * dp, axis=-1, keepdims=True)
        ds = (p * (dp - delta)).astype(BF16)
        dq = dq + mm(ds, only(mask, k), NN)
        dk = dk + mm(ds, q_head, TN)
        dv = dv + mm(p.astype(BF16), d_head, TN)
    dq = (dq * HEAD**-0.5).astype(BF16)
    dk = dk.astype(BF16)
    dv = dv.astype(BF16)
    dn = mm(dq, weight(0), NT) + mm(dk, weight(1), NT) + mm(dv, weight(2), NT)
    for to in range(GROUP):
        part = slice(64 * to, 64 * to + 64)
        scaled = dn[part] * gain_ref[...]
        nhat = tok_ref[1, to].astype(F32) * inv[part]
        dx = inv[part] * (scaled - nhat * jnp.mean(scaled * nhat, axis=-1, keepdims=True))
        out_ref[to, 1] = dx.astype(BF16)
    begin("out", out_ref.at[:, 1], out_hbm.at[:, 1], sems.at[4, 1])
    wait("out")


VMEM = pl.BlockSpec(memory_space=pltpu.VMEM)
HBM = pl.BlockSpec(memory_space=pltpu.HBM)
SMEM = pl.BlockSpec(memory_space=pltpu.SMEM)


def call(body, shapes, inputs, name, in_specs=None, scratch=(), flops=10**6, mib=40, out=VMEM):
    return pl.pallas_call(
        body,
        out_shape=[jax.ShapeDtypeStruct(shape, kind) for shape, kind in shapes],
        in_specs=[VMEM] * len(inputs) if in_specs is None else in_specs,
        out_specs=[out] * len(shapes),
        scratch_shapes=list(scratch),
        compiler_params=pltpu.CompilerParams(vmem_limit_bytes=mib * 2**20),
        cost_estimate=pl.CostEstimate(flops=flops, bytes_accessed=10**6, transcendentals=0),
        name=name,
    )(*inputs)


def per_device(fwd_input, bwd_input, bwd_grad, norm_gain, w_query, w_key, w_value, w_out):
    seqs = lax.axis_size("seq")
    sections = lax.axis_size("section")
    deep = seqs // GROUP
    row_groups = [[GROUP * y + x for x in range(GROUP)] for y in range(deep)]
    columns = [[GROUP * y + x for y in range(deep)] for x in range(GROUP)]
    me = (lax.axis_index("seq") % GROUP).reshape(1)

    qkv, own, tokens = call(
        pack,
        [((GROUP, 3, 32, 256), BF16), ((GROUP, 1, 32, 256), BF16), ((3, 64, 1024), BF16)],
        (w_query[0], w_key[0], w_value[0], w_out[0], fwd_input[0], bwd_input[0], bwd_grad[0]),
        "pack",
        in_specs=[HBM] * 7,
        scratch=(
            pltpu.VMEM((64, 1024), F32),
            pltpu.SemaphoreType.DMA((GROUP, 4)),
            pltpu.SemaphoreType.DMA((3,)),
        ),
        mib=62,
    )
    qkv = lax.all_to_all(qkv, "seq", 0, 0, axis_index_groups=row_groups, tiled=True)
    own = lax.ppermute(own, "seq", [(s, GROUP * (s % deep) + s // deep) for s in range(seqs)])

    qkv, tokens = lax.optimization_barrier((qkv, tokens))
    qkv = lax.all_gather(qkv, "seq", axis_index_groups=columns)
    own = jnp.broadcast_to(own.reshape(1, GROUP, 32, 256), (deep, GROUP, 32, 256))
    own = lax.all_to_all(own, "seq", 0, 0, axis_index_groups=columns, tiled=True)

    all_tokens = [tokens]
    for step in range(1, GROUP):
        pairs = [(s, s - s % GROUP + (s + step) % GROUP) for s in range(seqs)]
        all_tokens.append(lax.ppermute(tokens, "seq", pairs))
    parts, = call(
        layer,
        [((GROUP, 2, 64, 1024), BF16)],
        (me, qkv, own, norm_gain, *all_tokens),
        "layer",
        in_specs=[SMEM, HBM, HBM, VMEM] + [HBM] * GROUP,
        scratch=(
            pltpu.VMEM((3, GROUP, 64, 1024), BF16),
            pltpu.VMEM((GROUP, 2, 64, 1024), BF16),
            pltpu.VMEM((4, deep, GROUP, 32, 256), BF16),
            pltpu.VMEM((HEADS, 256, 256), F32),
            pltpu.SemaphoreType.DMA((5, 4)),
        ),
        flops=15 * 10**8,
        mib=60,
        out=HBM,
    )
    parts = lax.all_to_all(parts, "seq", 0, 0, axis_index_groups=row_groups, tiled=True)
    layer_out, input_grad = call(
        finish,
        [((64, 1024), BF16)] * 2,
        (parts, fwd_input[0], bwd_grad[0]),
        "finish",
    )
    ring = [(c, (c + 1) % sections) for c in range(sections)]
    next_input = lax.ppermute(layer_out, "section", ring)
    prev_grad = lax.ppermute(input_grad, "section", [(b, a) for a, b in ring])
    return next_input[None], prev_grad.astype(F32)[None]


def solution(mesh):
    placed = (
        P("section", "seq", None),
        P("section", "seq", None),
        P("section", "seq", None),
        P("section", None),
        P("section", "seq", None),
        P("section", "seq", None),
        P("section", "seq", None),
        P("section", "seq", None),
    )
    return jax.shard_map(
        per_device,
        mesh=mesh,
        in_specs=placed,
        out_specs=(P("section", "seq", None), P("section", "seq", None)),
        check_vma=False,
    )
```

time: 655 us -> 115 us (0.18)
  waiting for transfers between devices: 323 us -> 30.2 us
  local copies, waits for them, and re-layouts: 168 us -> 1.58 us
  matrix products: 55.3 us -> 0 us
  other arithmetic: 44.7 us -> 0.72 us
  blocking collectives: 0 us -> 26.5 us
  starting transfers between devices: 43.4 us -> 29.6 us
  Pallas kernels: 0 us -> 11.3 us
    all_gather x4 -> x1, waiting for transfers between devices: 316 us -> 11.6 us  [per_device(): qkv = lax.all_gather(qkv, 'seq', axis_index_groups=columns)]
    dot_general x35 -> x0, matrix products: 55.3 us -> none  [the longest x6 11.2 us: project(): jnp.dot(normed, matrix, preferred_element_type=jnp.float32)]
    broadcast_in_dim x41 -> x1, local copies, waits for them, and re-layouts: 40.5 us -> 0.89 us  [per_device(): jnp.broadcast_to(own.reshape(1, GROUP, 32, 256), (deep, GROUP, 32, 256))]
    another operation x34 -> x0, local copies, waits for them, and re-layouts: 38.9 us -> none  [the longest x5 8.22 us: attend(): group_k = gathered[level][0].reshape(rows, HEADS, HEAD)]
    ppermute x14 -> x6, starting transfers between devices: 43.2 us -> 14.9 us  [the longest x3 7.75 us: per_device(): all_tokens.append(lax.ppermute(tokens, 'seq', pairs))]
    all_to_all x0 -> x2, blocking collectives: none -> 26.5 us  [the longest x1 16.3 us: per_device(): lax.all_to_all(parts, 'seq', 0, 0, axis_index_groups=row_groups, tiled=True)]
    reshape x21 -> x0, local copies, waits for them, and re-layouts: 20 us -> none  [the longest x17 13.8 us: choose(): shaped = array.reshape(rows // rate, rate, HEADS, array.shape[1] // HEADS)]
    reduce_sum x10 -> x0, other arithmetic: 17.7 us -> none  [the longest x2 5.82 us: choose(): return jnp.sum(jnp.where(hit, shaped, jnp.zeros((), array.dtype)), axis=1)]
  transfers between devices with their start and end apart: 18 -> 8, of which waited for: 5 -> 6; matrix products, arithmetic and copies ran while one was open for 37% -> 1% of each run, Pallas kernels for 0% -> 0%
where the time goes in v1:
time: 115 us; the launch traced here: 114 us
  waiting for transfers between devices  30.2 us (26%)
  starting transfers between devices  29.6 us (26%)
  blocking collectives  26.5 us (23%)
  between operations  14.1 us (12%)
  Pallas kernels  11.3 us (10%)
  local copies, waits for them, and re-layouts  1.58 us (1%)
    all_to_all x1, blocking collectives, per_device(): lax.all_to_all(parts, 'seq', 0, 0, axis_index_groups=row_groups, tiled=True)  16.3 us
    all_to_all x1, starting transfers between devices, per_device(): lax.all_to_all(own, 'seq', 0, 0, axis_index_groups=columns, tiled=True)  14.7 us
    ppermute x3, waiting for transfers between devices, per_device(): all_tokens.append(lax.ppermute(tokens, 'seq', pairs))  14.2 us
    all_gather x1, waiting for transfers between devices, per_device(): qkv = lax.all_gather(qkv, 'seq', axis_index_groups=columns)  11.6 us
    pallas_call x3, Pallas kernels, call(): pl.pallas_call(body, out_shape=[jax.ShapeDtypeStruct(shape, kind) for sha...  11.3 us
    all_to_all x1, blocking collectives, per_device(): lax.all_to_all(qkv, 'seq', 0, 0, axis_index_groups=row_groups, tiled=True)  10.3 us
    ppermute x3, starting transfers between devices, per_device(): all_tokens.append(lax.ppermute(tokens, 'seq', pairs))  7.75 us
    ppermute x1, starting transfers between devices, per_device(): next_input = lax.ppermute(layer_out, 'section', ring)  5.68 us
  transfers between devices with their start and end apart: 8, of which 6 were waited for; matrix products, arithmetic and copies ran while one was open for 1% of the time, Pallas kernels for 0%

profile of v1, /device:TPU:1, one launch (start us, length us, event | category | flops | bytes accessed | tf_op | source)
XLA Modules:
  0.0 114.1 jit_solution(7463091671976382826)
XLA Ops:
  7.2 0.0 all-gather.3.cloned.1.call-start
  7.2 2.3 %pack.1 = (bf16[4,3,32,256]{3,2,1,0:T(8,128)(2,1)}, bf16[4,1,32,256]{3,2,1,0:T(8,128)(2,1)}, bf16[3,64,1024]{2,1,0:T(8,128)(2,1)}) custom-call(bf16[32,1024]{1,0:T(8,128)(2,1)} %bitcast.20, bf16[32,1024]{1,0:T(8,128)(2,1)} %bitcast.21, bf16[32,1024]{1,0:T(8,128)(2,1)} %bitcast.22, bf16[32,1024]{1,0:T(8,128)(2,1)} %bitcast.23, bf16[64,1024]{1,0:T(8,128)(2,1)} %bitcast.16, ...), custom_call_target="tpu_custom_call" | custom-call | flops 1000000 | bytes 1000000 | tf_op jit(solution)/shard_map/pack/pallas_call | solution.py:199
  9.5 10.3 %all_to_all.15 = bf16[4,3,32,256]{3,2,1,0:T(8,128)(2,1)} all-to-all(bf16[4,3,32,256]{3,2,1,0:T(8,128)(2,1)} %get-tuple-element.9), channel_id=1, replica_groups={{0,16,32,48},{64,80,96,112},{128,144,160,176},{192,208,224,240},{256,27..., dimensions={0} | all-to-all | bytes 393216 | tf_op jit(solution)/shard_map/all_to_all | solution.py:232
  19.8 0.0 all-gather.3.cloned.1.call-update
  19.8 1.5 %collective-permute-start = (bf16[4,1,32,256]{3,2,1,0:T(8,128)(2,1)}, bf16[4,1,32,256]{3,2,1,0:T(8,128)(2,1)S(1)}, u32[]{:S(2)}, u32[]{:S(2)}) collective-permute-start(bf16[4,1,32,256]{3,2,1,0:T(8,128)(2,1)} %get-tuple-element.12), channel_id=1, source_target_pairs={{0,0},{16,64},{32,128},{48,192},{64,256},{80,320},{96,384},{112,44... | collective-permute-start | bytes 196616 | tf_op jit(solution)/shard_map/ppermute | solution.py:233
  21.3 0.9 broadcast_in_dim.17
  22.2 14.7 %all-to-all-start.1 = ((bf16[8,4,32,256]{3,2,1,0:T(8,128)(2,1)}), bf16[8,4,32,256]{3,2,1,0:T(8,128)(2,1)S(1)}, u32[]{:S(2)}, u32[]{:S(2)}) async-start(bf16[8,4,32,256]{3,2,1,0:T(8,128)(2,1)} %broadcast_in_dim.17), calls=%async_computation.1 | async-start | bytes 1048576 | tf_op jit(solution)/shard_map/all_to_all | solution.py:238
  36.9 2.6 %collective-permute-start.3 = (bf16[3,64,1024]{2,1,0:T(8,128)(2,1)S(1)}, bf16[3,64,1024]{2,1,0:T(8,128)(2,1)S(1)}, u32[]{:S(2)}, u32[]{:S(2)}) collective-permute-start(bf16[3,64,1024]{2,1,0:T(8,128)(2,1)S(1)} %copy-done.3), channel_id=1, source_target_pairs={{0,48},{16,0},{32,16},{48,32},{64,112},{80,64},{96,80},{112,96},{1... | collective-permute-start | bytes 1179656 | tf_op jit(solution)/shard_map/ppermute | solution.py:243
  39.5 3.2 %collective-permute-start.2 = (bf16[3,64,1024]{2,1,0:T(8,128)(2,1)S(1)}, bf16[3,64,1024]{2,1,0:T(8,128)(2,1)S(1)}, u32[]{:S(2)}, u32[]{:S(2)}) collective-permute-start(bf16[3,64,1024]{2,1,0:T(8,128)(2,1)S(1)} %copy-done.3), channel_id=1, source_target_pairs={{0,32},{16,48},{32,0},{48,16},{64,96},{80,112},{96,64},{112,80},{1... | collective-permute-start | bytes 1179656 | tf_op jit(solution)/shard_map/ppermute | solution.py:243
  42.7 1.9 %collective-permute-start.1 = (bf16[3,64,1024]{2,1,0:T(8,128)(2,1)S(1)}, bf16[3,64,1024]{2,1,0:T(8,128)(2,1)S(1)}, u32[]{:S(2)}, u32[]{:S(2)}) collective-permute-start(bf16[3,64,1024]{2,1,0:T(8,128)(2,1)S(1)} %copy-done.3), channel_id=1, source_target_pairs={{0,16},{16,32},{32,48},{48,0},{64,80},{80,96},{96,112},{112,64},{1... | collective-permute-start | bytes 1179656 | tf_op jit(solution)/shard_map/ppermute | solution.py:243
  44.7 1.4 %collective-permute-done.3.refs_3_ = bf16[3,64,1024]{2,1,0:T(8,128)(2,1)S(1)} collective-permute-done((bf16[3,64,1024]{2,1,0:T(8,128)(2,1)S(1)}, bf16[3,64,1024]{2,1,0:T(8,128)(2,1)S(1)}, u32[]{:S(2)}, u32[]{:S(2)}) %collective-permute-start.3) | collective-permute-done | bytes 393248 | tf_op jit(solution)/shard_map/ppermute | solution.py:243
  46.1 3.7 %collective-permute-done.2.refs_2_ = bf16[3,64,1024]{2,1,0:T(8,128)(2,1)S(1)} collective-permute-done((bf16[3,64,1024]{2,1,0:T(8,128)(2,1)S(1)}, bf16[3,64,1024]{2,1,0:T(8,128)(2,1)S(1)}, u32[]{:S(2)}, u32[]{:S(2)}) %collective-permute-start.2) | collective-permute-done | bytes 393248 | tf_op jit(solution)/shard_map/ppermute | solution.py:243
  49.8 9.1 %collective-permute-done.1.refs_1_ = bf16[3,64,1024]{2,1,0:T(8,128)(2,1)S(1)} collective-permute-done((bf16[3,64,1024]{2,1,0:T(8,128)(2,1)S(1)}, bf16[3,64,1024]{2,1,0:T(8,128)(2,1)S(1)}, u32[]{:S(2)}, u32[]{:S(2)}) %collective-permute-start.1) | collective-permute-done | bytes 393248 | tf_op jit(solution)/shard_map/ppermute | solution.py:243
  58.9 11.6 %all-gather.3.cloned.1.call-done = bf16[32,3,32,256]{3,2,1,0:T(8,128)(2,1)} async-done(((bf16[4,3,32,256]{3,2,1,0:T(8,128)(2,1)}), bf16[32,3,32,256]{3,2,1,0:T(8,128)(2,1)}) %all-gather.3.cloned.1.call-update) | async-done | bytes 1572880 | tf_op jit(solution)/shard_map/all_gather | solution.py:236
  70.5 8.9 %layer.1 = bf16[4,2,64,1024]{3,2,1,0:T(8,128)(2,1)} custom-call(s32[1]{0:T(128)} %bitcast.me_ref, bf16[8,4,3,32,256]{4,3,2,1,0:T(8,128)(2,1)} %bitcast.25, bf16[8,4,32,256]{3,2,1,0:T(8,128)(2,1)} %copy-done.2, f32[1,1024]{1,0:T(1,128)} %gain_ref.1, bf16[3,64,1024]{2,1,0:T(8,128)(2,1)} %get-tuple-element.13.refs_0_, bf16[3,64,1024]{2,1,0:T(8,128)(2,1)} %copy-done.6, ...), custom_call_target="tpu_custom_call" | custom-call | flops 1500000000 | bytes 1000000 | tf_op jit(solution)/shard_map/layer/pallas_call | solution.py:199
  79.4 0.0 copy-start
  79.4 0.0 copy-start.1
  79.4 16.3 %all_to_all.16.parts_ref = bf16[4,2,64,1024]{3,2,1,0:T(8,128)(2,1)S(1)} all-to-all(bf16[4,2,64,1024]{3,2,1,0:T(8,128)(2,1)} %layer.1), channel_id=1, replica_groups={{0,16,32,48},{64,80,96,112},{128,144,160,176},{192,208,224,240},{256,27..., dimensions={0} | all-to-all | bytes 2097152 | tf_op jit(solution)/shard_map/all_to_all | solution.py:261
  95.7 0.2 finish.1
  95.8 5.7 %collective-permute-start.4 = (bf16[64,1024]{1,0:T(8,128)(2,1)S(1)}, bf16[64,1024]{1,0:T(8,128)(2,1)S(1)}, u32[]{:S(2)}, u32[]{:S(2)}) collective-permute-start(bf16[64,1024]{1,0:T(8,128)(2,1)S(1)} %get-tuple-element.14), channel_id=1, source_target_pairs={{0,1},{1,2},{2,3},{3,4},{4,5},{5,6},{6,7},{7,8},{8,9},{9,10},{10,1... | collective-permute-start | bytes 393224 | tf_op jit(solution)/shard_map/ppermute | solution.py:269
  101.5 1.9 %collective-permute-done.4 = bf16[64,1024]{1,0:T(8,128)(2,1)S(1)} collective-permute-done((bf16[64,1024]{1,0:T(8,128)(2,1)S(1)}, bf16[64,1024]{1,0:T(8,128)(2,1)S(1)}, u32[]{:S(2)}, u32[]{:S(2)}) %collective-permute-start.4) | collective-permute-done | bytes 131104 | tf_op jit(solution)/shard_map/ppermute | solution.py:269
  103.5 2.4 %collective-permute-done.5 = bf16[64,1024]{1,0:T(8,128)(2,1)S(1)} collective-permute-done((bf16[64,1024]{1,0:T(8,128)(2,1)S(1)}, bf16[64,1024]{1,0:T(8,128)(2,1)S(1)}, u32[]{:S(2)}, u32[]{:S(2)}) %collective-permute-start.5) | collective-permute-done | bytes 131104 | tf_op jit(solution)/shard_map/ppermute | solution.py:270
  105.9 0.7 bitcast_convert_fusion
  106.6 0.7 copy.11
  (15 shorter events, 0.0 us)
Async XLA Ops:
  7.2 63.3 %all-gather.3.cloned.1.call-start = ((), (), s32[]{:S(2)}) async-start(), calls=%async_computation.3 | async-start | bytes 1769472 | tf_op jit(solution)/shard_map/all_gather | solution.py:236
  9.5 27.4 %copy-start.3 = (bf16[3,64,1024]{2,1,0:T(8,128)(2,1)S(1)}, bf16[3,64,1024]{2,1,0:T(8,128)(2,1)}, u32[]{:S(2)}) copy-start(bf16[3,64,1024]{2,1,0:T(8,128)(2,1)} %get-tuple-element.13.refs_0_) | copy-start | bytes 1179652
  19.8 1.5 %collective-permute-start = (bf16[4,1,32,256]{3,2,1,0:T(8,128)(2,1)}, bf16[4,1,32,256]{3,2,1,0:T(8,128)(2,1)S(1)}, u32[]{:S(2)}, u32[]{:S(2)}) collective-permute-start(bf16[4,1,32,256]{3,2,1,0:T(8,128)(2,1)} %get-tuple-element.12), channel_id=1, source_target_pairs={{0,0},{16,64},{32,128},{48,192},{64,256},{80,320},{96,384},{112,44... | collective-permute-start | bytes 196616 | tf_op jit(solution)/shard_map/ppermute | solution.py:233
  22.2 36.6 %all-to-all-start.1 = ((bf16[8,4,32,256]{3,2,1,0:T(8,128)(2,1)}), bf16[8,4,32,256]{3,2,1,0:T(8,128)(2,1)S(1)}, u32[]{:S(2)}, u32[]{:S(2)}) async-start(bf16[8,4,32,256]{3,2,1,0:T(8,128)(2,1)} %broadcast_in_dim.17), calls=%async_computation.1 | async-start | bytes 1048576 | tf_op jit(solution)/shard_map/all_to_all | solution.py:238
  36.9 9.2 %collective-permute-start.3 = (bf16[3,64,1024]{2,1,0:T(8,128)(2,1)S(1)}, bf16[3,64,1024]{2,1,0:T(8,128)(2,1)S(1)}, u32[]{:S(2)}, u32[]{:S(2)}) collective-permute-start(bf16[3,64,1024]{2,1,0:T(8,128)(2,1)S(1)} %copy-done.3), channel_id=1, source_target_pairs={{0,48},{16,0},{32,16},{48,32},{64,112},{80,64},{96,80},{112,96},{1... | collective-permute-start | bytes 1179656 | tf_op jit(solution)/shard_map/ppermute | solution.py:243
  39.5 10.3 %collective-permute-start.2 = (bf16[3,64,1024]{2,1,0:T(8,128)(2,1)S(1)}, bf16[3,64,1024]{2,1,0:T(8,128)(2,1)S(1)}, u32[]{:S(2)}, u32[]{:S(2)}) collective-permute-start(bf16[3,64,1024]{2,1,0:T(8,128)(2,1)S(1)} %copy-done.3), channel_id=1, source_target_pairs={{0,32},{16,48},{32,0},{48,16},{64,96},{80,112},{96,64},{112,80},{1... | collective-permute-start | bytes 1179656 | tf_op jit(solution)/shard_map/ppermute | solution.py:243
  42.7 16.1 %collective-permute-start.1 = (bf16[3,64,1024]{2,1,0:T(8,128)(2,1)S(1)}, bf16[3,64,1024]{2,1,0:T(8,128)(2,1)S(1)}, u32[]{:S(2)}, u32[]{:S(2)}) collective-permute-start(bf16[3,64,1024]{2,1,0:T(8,128)(2,1)S(1)} %copy-done.3), channel_id=1, source_target_pairs={{0,16},{16,32},{32,48},{48,0},{64,80},{80,96},{96,112},{112,64},{1... | collective-permute-start | bytes 1179656 | tf_op jit(solution)/shard_map/ppermute | solution.py:243
  46.1 24.5 %copy-start.4 = (bf16[3,64,1024]{2,1,0:T(8,128)(2,1)}, bf16[3,64,1024]{2,1,0:T(8,128)(2,1)S(1)}, u32[]{:S(2)}) copy-start(bf16[3,64,1024]{2,1,0:T(8,128)(2,1)S(1)} %collective-permute-done.3.refs_3_) | copy-start | bytes 1179652
  49.8 20.7 %copy-start.5 = (bf16[3,64,1024]{2,1,0:T(8,128)(2,1)}, bf16[3,64,1024]{2,1,0:T(8,128)(2,1)S(1)}, u32[]{:S(2)}) copy-start(bf16[3,64,1024]{2,1,0:T(8,128)(2,1)S(1)} %collective-permute-done.2.refs_2_) | copy-start | bytes 1179652
  58.9 11.7 %copy-start.6 = (bf16[3,64,1024]{2,1,0:T(8,128)(2,1)}, bf16[3,64,1024]{2,1,0:T(8,128)(2,1)S(1)}, u32[]{:S(2)}) copy-start(bf16[3,64,1024]{2,1,0:T(8,128)(2,1)S(1)} %collective-permute-done.1.refs_1_) | copy-start | bytes 1179652
  58.9 11.7 %copy-start.2 = (bf16[8,4,32,256]{3,2,1,0:T(8,128)(2,1)}, bf16[8,4,32,256]{3,2,1,0:T(8,128)(2,1)S(1)}, u32[]{:S(2)}) copy-start(bf16[8,4,32,256]{3,2,1,0:T(8,128)(2,1)S(1)} %all-to-all-done.1.own_hbm) | copy-start | bytes 1572868
  79.4 16.3 %copy-start = (f32[1,64,1024]{2,1,0:T(8,128)S(1)}, f32[1,64,1024]{2,1,0:T(8,128)}, u32[]{:S(2)}) copy-start(f32[1,64,1024]{2,1,0:T(8,128)} %param.10) | copy-start | bytes 786436
  79.4 16.3 %copy-start.1 = (bf16[1,64,1024]{2,1,0:T(8,128)(2,1)S(1)}, bf16[1,64,1024]{2,1,0:T(8,128)(2,1)}, u32[]{:S(2)}) copy-start(bf16[1,64,1024]{2,1,0:T(8,128)(2,1)} %param.8) | copy-start | bytes 393220
  95.8 7.6 %collective-permute-start.4 = (bf16[64,1024]{1,0:T(8,128)(2,1)S(1)}, bf16[64,1024]{1,0:T(8,128)(2,1)S(1)}, u32[]{:S(2)}, u32[]{:S(2)}) collective-permute-start(bf16[64,1024]{1,0:T(8,128)(2,1)S(1)} %get-tuple-element.14), channel_id=1, source_target_pairs={{0,1},{1,2},{2,3},{3,4},{4,5},{5,6},{6,7},{7,8},{8,9},{9,10},{10,1... | collective-permute-start | bytes 393224 | tf_op jit(solution)/shard_map/ppermute | solution.py:269
  101.5 4.4 %collective-permute-start.5 = (bf16[64,1024]{1,0:T(8,128)(2,1)S(1)}, bf16[64,1024]{1,0:T(8,128)(2,1)S(1)}, u32[]{:S(2)}, u32[]{:S(2)}) collective-permute-start(bf16[64,1024]{1,0:T(8,128)(2,1)S(1)} %get-tuple-element.15), channel_id=1, source_target_pairs={{1,0},{2,1},{3,2},{4,3},{5,4},{6,5},{7,6},{8,7},{9,8},{10,9},{11,1... | collective-permute-start | bytes 393224 | tf_op jit(solution)/shard_map/ppermute | solution.py:270
Sparse Core Ops, SparseCore 0:
  19.9 50.5 all-gather.2

commit v2 on v1

v2 whole, which is shorter than its diff:
```python
import functools
import math

import jax
import jax.numpy as jnp
from jax import lax
from jax.experimental import pallas as pl
from jax.experimental.pallas import tpu as pltpu
from jax.sharding import PartitionSpec as P

HEAD = 64
EPS = 1e-06
NEG = -1e30
GROUP = 4
HEADS = 4

F32 = jnp.float32
BF16 = jnp.bfloat16
NT = (((1,), (1,)), ((), ()))
NN = (((1,), (0,)), ((), ()))
TN = (((0,), (0,)), ((), ()))


def mm(a, b, dims):
    return lax.dot_general(a, b, dims, preferred_element_type=F32)


def pair_bias(rows):
    t = lax.broadcasted_iota(jnp.int32, (rows, rows), 0)
    u = lax.broadcasted_iota(jnp.int32, (rows, rows), 1)
    causal = u <= t
    apart = t ^ u
    one = causal & (apart < 64)
    two = causal & (apart < 128) & ((apart & 1) == 0)
    three = causal & (apart < 256) & ((apart & 3) == 0)
    biases = []
    for head in range(HEADS):
        count = one.astype(jnp.int32)
        count = count + (two & ((t & 1) == head % 2)).astype(jnp.int32)
        count = count + (three & ((t & 3) == head)).astype(jnp.int32)
        bias = jnp.where(count == 1, 0.0, NEG)
        bias = jnp.where(count == 2, math.log(2.0), bias)
        bias = jnp.where(count == 3, math.log(3.0), bias)
        biases.append(bias)
    return biases


def head_masks(rows):
    lane = lax.broadcasted_iota(jnp.int32, (rows, HEADS * HEAD), 1)
    return [(lane // HEAD) == head for head in range(HEADS)]


def only(mask, value):
    return jnp.where(mask, value, jnp.zeros((), value.dtype))


def pack_weights(q_hbm, k_hbm, v_hbm, o_hbm, qkv_out, own_out, sems):
    copies = []
    for block in range(GROUP):
        columns = slice(256 * block, 256 * block + 256)
        for i, ref in enumerate((q_hbm, k_hbm, v_hbm, o_hbm)):
            target = own_out.at[block, 0] if i == 3 else qkv_out.at[block, i]
            copies.append(pltpu.make_async_copy(ref.at[:, columns], target, sems.at[block, i]))
            copies[-1].start()
    for copy in copies:
        copy.wait()


def pack_tokens(fwd_hbm, bwd_hbm, grad_hbm, out_ref, grad_ref, sems, grad_sem):
    first = pltpu.make_async_copy(grad_hbm, grad_ref, grad_sem)
    first.start()
    copies = []
    for to in range(GROUP):
        for i, ref in enumerate((fwd_hbm, bwd_hbm)):
            copies.append(pltpu.make_async_copy(ref, out_ref.at[to, i], sems.at[to, i]))
            copies[-1].start()
    first.wait()
    for to in range(GROUP):
        out_ref[to, 2] = grad_ref[...].astype(BF16)
    for copy in copies:
        copy.wait()


def finish(parts_ref, fwd_ref, grad_ref, next_ref, prev_ref):
    for which, own, out in ((0, fwd_ref, next_ref), (1, grad_ref, prev_ref)):
        total = own[...].astype(F32)
        for part in range(GROUP):
            total = total + parts_ref[part, which].astype(F32)
        out[...] = total.astype(BF16)


def prepare(tok_ref, gain_ref, normed_ref, inv_ref, bias_ref):
    for which in range(2):
        for part in range(GROUP):
            xf = tok_ref[part, which].astype(F32)
            inv = lax.rsqrt(jnp.mean(xf * xf, axis=-1, keepdims=True) + EPS)
            rows = slice(64 * part, 64 * part + 64)
            normed_ref[which, rows, :] = (xf * inv * gain_ref[...]).astype(BF16)
            if which == 1:
                inv_ref[rows, :] = jnp.broadcast_to(inv, (64, 128))
    for head, bias in enumerate(pair_bias(GROUP * 64)):
        bias_ref[head] = bias


def layer(row_ref, tok_ref, normed_ref, inv_ref, bias_ref, gain_ref, qkv_ref, *refs):
    pieces, (out_ref, own_ref) = refs[:-2], refs[-2:]
    rows = GROUP * 64
    deep = 2 * len(pieces)
    for k in range(deep):
        own_ref[(row_ref[0] + k) % deep] = pieces[k // 2][k % 2]
    heads = head_masks(rows)
    scale = jnp.asarray(HEAD**-0.5, BF16)

    def weight(i):
        return qkv_ref[:, :, i].reshape(1024, 256)

    def out_weight(c):
        return own_ref[:, c].reshape(256, 256)

    def projected(which):
        normed = normed_ref[which]
        q, k, v = [mm(normed, weight(i), NN).astype(BF16) for i in range(3)]
        return q * scale, k, v

    def prob_of(q_head, k, head):
        s = mm(q_head, k, NT) + bias_ref[head]
        top = jnp.max(s, axis=-1, keepdims=True)
        p = jnp.exp(s - top)
        return p * (1.0 / jnp.sum(p, axis=-1, keepdims=True))

    q, k, v = projected(0)
    attended = jnp.zeros((rows, 256), F32)
    for head in range(HEADS):
        p = prob_of(only(heads[head], q), k, head).astype(BF16)
        attended = attended + mm(p, only(heads[head], v), NN)
    attended = attended.astype(BF16)
    for c in range(4):
        part = mm(attended, out_weight(c), NN).astype(BF16)
        for to in range(GROUP):
            out_ref[to, 0, :, 256 * c : 256 * c + 256] = part[64 * to : 64 * to + 64]

    q, k, v = projected(1)
    grads = tok_ref[:, 2].reshape(rows, 1024)
    d_att = jnp.zeros((rows, 256), F32)
    for c in range(4):
        d_att = d_att + mm(grads[:, 256 * c : 256 * c + 256], out_weight(c), NT)
    d_att = d_att.astype(BF16)
    dq = jnp.zeros((rows, 256), F32)
    dk = jnp.zeros((rows, 256), F32)
    dv = jnp.zeros((rows, 256), F32)
    for head in range(HEADS):
        mask = heads[head]
        q_head = only(mask, q)
        p = prob_of(q_head, k, head)
        d_head = only(mask, d_att)
        dp = mm(d_head, v, NT)
        delta = jnp.sum(p * dp, axis=-1, keepdims=True)
        ds = (p * (dp - delta)).astype(BF16)
        dq = dq + mm(ds, only(mask, k), NN)
        dk = dk + mm(ds, q_head, TN)
        dv = dv + mm(p.astype(BF16), d_head, TN)
    dq = (dq * HEAD**-0.5).astype(BF16)
    dk = dk.astype(BF16)
    dv = dv.astype(BF16)
    dn = mm(dq, weight(0), NT) + mm(dk, weight(1), NT) + mm(dv, weight(2), NT)
    for to in range(GROUP):
        part = slice(64 * to, 64 * to + 64)
        inv = inv_ref[part, 0:1]
        scaled = dn[part] * gain_ref[...]
        nhat = tok_ref[to, 1].astype(F32) * inv
        dx = inv * (scaled - nhat * jnp.mean(scaled * nhat, axis=-1, keepdims=True))
        out_ref[to, 1] = dx.astype(BF16)


VMEM = pl.BlockSpec(memory_space=pltpu.VMEM)
HBM = pl.BlockSpec(memory_space=pltpu.HBM)
SMEM = pl.BlockSpec(memory_space=pltpu.SMEM)


def call(body, shapes, inputs, name, in_specs=None, scratch=(), flops=10**6, mib=40, out=VMEM):
    return pl.pallas_call(
        body,
        out_shape=[jax.ShapeDtypeStruct(shape, kind) for shape, kind in shapes],
        in_specs=[VMEM] * len(inputs) if in_specs is None else in_specs,
        out_specs=[out] * len(shapes),
        scratch_shapes=list(scratch),
        compiler_params=pltpu.CompilerParams(vmem_limit_bytes=mib * 2**20),
        cost_estimate=pl.CostEstimate(flops=flops, bytes_accessed=10**6, transcendentals=0),
        name=name,
    )(*inputs)


def per_device(fwd_input, bwd_input, bwd_grad, norm_gain, w_query, w_key, w_value, w_out):
    seqs = lax.axis_size("seq")
    sections = lax.axis_size("section")
    deep = seqs // GROUP
    row_groups = [[GROUP * y + x for x in range(GROUP)] for y in range(deep)]
    columns = [[GROUP * y + x for y in range(deep)] for x in range(GROUP)]
    row = (lax.axis_index("seq") // GROUP).reshape(1)

    qkv, own = call(
        pack_weights,
        [((GROUP, 3, 32, 256), BF16), ((GROUP, 1, 32, 256), BF16)],
        (w_query[0], w_key[0], w_value[0], w_out[0]),
        "pack_weights",
        in_specs=[HBM] * 4,
        scratch=(pltpu.SemaphoreType.DMA((GROUP, 4)),),
        mib=63,
    )
    qkv = lax.all_to_all(qkv, "seq", 0, 0, axis_index_groups=row_groups, tiled=True)
    own = lax.ppermute(own, "seq", [(s, GROUP * (s % deep) + s // deep) for s in range(seqs)])
    tokens, = call(
        pack_tokens,
        [((GROUP, 3, 64, 1024), BF16)],
        (fwd_input[0], bwd_input[0], bwd_grad[0]),
        "pack_tokens",
        in_specs=[HBM] * 3,
        scratch=(
            pltpu.VMEM((64, 1024), F32),
            pltpu.SemaphoreType.DMA((GROUP, 2)),
            pltpu.SemaphoreType.DMA,
        ),
        mib=63,
    )
    mine = qkv
    qkv = lax.all_gather(qkv, "seq", axis_index_groups=columns)
    _, own, tokens = lax.optimization_barrier((mine, own, tokens))
    tokens = lax.all_to_all(tokens, "seq", 0, 0, axis_index_groups=row_groups, tiled=True)
    def up(value, steps):
        return lax.ppermute(
            value, "seq", [(s, (s - steps * GROUP) % seqs) for s in range(seqs)]
        )

    own = own.reshape(1, GROUP, 32, 256)
    pieces = [jnp.concatenate((own, up(own, 1)))]
    for step in range(2, deep, 2):
        pieces.append(up(pieces[-1], 2))
        if step == 4:
            pieces[-1], tokens = lax.optimization_barrier((pieces[-1], tokens))

    normed, inv, bias = call(
        prepare,
        [((2, 256, 1024), BF16), ((256, 128), F32), ((HEADS, 256, 256), F32)],
        (tokens, norm_gain),
        "prepare",
    )
    parts, = call(
        layer,
        [((GROUP, 2, 64, 1024), BF16)],
        (row, tokens, normed, inv, bias, norm_gain, qkv, *pieces),
        "layer",
        in_specs=[SMEM] + [VMEM] * (6 + deep // 2),
        scratch=(pltpu.VMEM((deep, GROUP, 32, 256), BF16),),
        flops=15 * 10**8,
    )
    parts = lax.all_to_all(parts, "seq", 0, 0, axis_index_groups=row_groups, tiled=True)
    layer_out, input_grad = call(
        finish,
        [((64, 1024), BF16)] * 2,
        (parts, fwd_input[0], bwd_grad[0]),
        "finish",
    )
    ring = [(c, (c + 1) % sections) for c in range(sections)]
    next_input = lax.ppermute(layer_out, "section", ring)
    prev_grad = lax.ppermute(input_grad, "section", [(b, a) for a, b in ring])
    return next_input[None], prev_grad.astype(F32)[None]


def solution(mesh):
    placed = (
        P("section", "seq", None),
        P("section", "seq", None),
        P("section", "seq", None),
        P("section", None),
        P("section", "seq", None),
        P("section", "seq", None),
        P("section", "seq", None),
        P("section", "seq", None),
    )
    return jax.shard_map(
        per_device,
        mesh=mesh,
        in_specs=placed,
        out_specs=(P("section", "seq", None), P("section", "seq", None)),
        check_vma=False,
    )
```

time: 115 us -> 117 us (1.017)
  starting transfers between devices: 29.6 us -> 43.7 us
  waiting for transfers between devices: 30.2 us -> 19.5 us
  blocking collectives: 26.5 us -> 23.3 us
  local copies, waits for them, and re-layouts: 1.58 us -> 4.28 us
    ppermute x3 -> x4, starting transfers between devices: 7.75 us -> 23 us  [up(): lax.ppermute(value, 'seq', [(s, (s - steps * GROUP) % seqs) for s in rang...]
    all_gather x1, waiting for transfers between devices: 11.6 us -> 0.01 us  [per_device(): qkv = lax.all_gather(qkv, 'seq', axis_index_groups=columns)]
    all_to_all x1, starting transfers between devices: 14.7 us -> 9.39 us  [per_device(): lax.all_to_all(tokens, 'seq', 0, 0, axis_index_groups=row_groups, tiled=T...]
    unnamed x15 -> x13, local copies, waits for them, and re-layouts: 0.69 us -> 4.28 us
    ppermute x1, starting transfers between devices: 5.68 us -> 8.87 us  [per_device(): next_input = lax.ppermute(layer_out, 'section', ring)]
    all_to_all x1, blocking collectives: 16.3 us -> 13.1 us  [per_device(): lax.all_to_all(parts, 'seq', 0, 0, axis_index_groups=row_groups, tiled=True)]
    ppermute x3 -> x4, waiting for transfers between devices: 14.2 us -> 15.6 us  [up(): lax.ppermute(value, 'seq', [(s, (s - steps * GROUP) % seqs) for s in rang...]
    pallas_call x3 -> x5, Pallas kernels: 11.3 us -> 10.4 us  [call(): pl.pallas_call(body, out_shape=[jax.ShapeDtypeStruct(shape, kind) for sha...]
  transfers between devices with their start and end apart: 8 -> 9, of which waited for: 6 -> 6; matrix products, arithmetic and copies ran while one was open for 1% -> 0% of each run, Pallas kernels for 0% -> 3%
where the time goes in v2:
time: 117 us; the launch traced here: 116 us
  starting transfers between devices  43.7 us (37%)
  blocking collectives  23.3 us (20%)
  waiting for transfers between devices  19.5 us (17%)
  between operations  14.2 us (12%)
  Pallas kernels  10.4 us (9%)
  local copies, waits for them, and re-layouts  4.28 us (4%)
    ppermute x4, starting transfers between devices, up(): lax.ppermute(value, 'seq', [(s, (s - steps * GROUP) % seqs) for s in rang...  23 us
    ppermute x4, waiting for transfers between devices, up(): lax.ppermute(value, 'seq', [(s, (s - steps * GROUP) % seqs) for s in rang...  15.6 us
    all_to_all x1, blocking collectives, per_device(): lax.all_to_all(parts, 'seq', 0, 0, axis_index_groups=row_groups, tiled=True)  13.1 us
    pallas_call x5, Pallas kernels, call(): pl.pallas_call(body, out_shape=[jax.ShapeDtypeStruct(shape, kind) for sha...  10.4 us
    all_to_all x1, blocking collectives, per_device(): lax.all_to_all(qkv, 'seq', 0, 0, axis_index_groups=row_groups, tiled=True)  10.1 us
    all_to_all x1, starting transfers between devices, per_device(): lax.all_to_all(tokens, 'seq', 0, 0, axis_index_groups=row_groups, tiled=T...  9.39 us
    ppermute x1, starting transfers between devices, per_device(): next_input = lax.ppermute(layer_out, 'section', ring)  8.87 us
    unnamed x13, local copies, waits for them, and re-layouts  4.28 us
  transfers between devices with their start and end apart: 9, of which 6 were waited for; matrix products, arithmetic and copies ran while one was open for 0% of the time, Pallas kernels for 3%

profile of v2, /device:TPU:1, one launch (start us, length us, event | category | flops | bytes accessed | tf_op | source)
XLA Modules:
  0.0 116.0 jit_solution(13369611192287849193)
XLA Ops:
  7.2 1.7 %pack_weights.1 = (bf16[4,3,32,256]{3,2,1,0:T(8,128)(2,1)}, bf16[4,1,32,256]{3,2,1,0:T(8,128)(2,1)}) custom-call(bf16[32,1024]{1,0:T(8,128)(2,1)} %bitcast.22, bf16[32,1024]{1,0:T(8,128)(2,1)} %bitcast.23, bf16[32,1024]{1,0:T(8,128)(2,1)} %bitcast.24, bf16[32,1024]{1,0:T(8,128)(2,1)} %bitcast.25), custom_call_target="tpu_custom_call" | custom-call | flops 1000000 | bytes 1000000 | tf_op jit(solution)/shard_map/pack_weights/pallas_call | solution.py:181
  8.9 10.1 %all_to_all.15 = bf16[4,3,32,256]{3,2,1,0:T(8,128)(2,1)} all-to-all(bf16[4,3,32,256]{3,2,1,0:T(8,128)(2,1)} %get-tuple-element.13), channel_id=1, replica_groups={{0,16,32,48},{64,80,96,112},{128,144,160,176},{192,208,224,240},{256,27..., dimensions={0} | all-to-all | bytes 393216 | tf_op jit(solution)/shard_map/all_to_all | solution.py:210
  19.1 1.5 %collective-permute-start = (bf16[4,1,32,256]{3,2,0,1:T(8,128)(2,1)}, bf16[4,1,32,256]{3,2,0,1:T(8,128)(2,1)S(1)}, u32[]{:S(2)}, u32[]{:S(2)}) collective-permute-start(bf16[4,1,32,256]{3,2,0,1:T(8,128)(2,1)} %bitcast.28), channel_id=1, source_target_pairs={{0,0},{16,64},{32,128},{48,192},{64,256},{80,320},{96,384},{112,44... | collective-permute-start | bytes 196616 | tf_op jit(solution)/shard_map/ppermute | solution.py:211
  20.6 2.6 %pack_tokens.1 = bf16[4,3,64,1024]{3,2,1,0:T(8,128)(2,1)} custom-call(bf16[64,1024]{1,0:T(8,128)(2,1)} %bitcast.18, bf16[64,1024]{1,0:T(8,128)(2,1)} %bitcast.20, f32[64,1024]{1,0:T(8,128)} %bitcast.16), custom_call_target="tpu_custom_call" | custom-call | flops 1000000 | bytes 1000000 | tf_op jit(solution)/shard_map/pack_tokens/pallas_call | solution.py:181
  23.2 9.4 %all-to-all-start.1 = ((bf16[4,3,64,1024]{3,2,1,0:T(8,128)(2,1)}), bf16[4,3,64,1024]{3,2,1,0:T(8,128)(2,1)S(1)}, u32[]{:S(2)}, u32[]{:S(2)}) async-start(bf16[4,3,64,1024]{3,2,1,0:T(8,128)(2,1)} %pack_tokens.1), calls=%async_computation.1 | async-start | bytes 3145728 | tf_op jit(solution)/shard_map/all_to_all | solution.py:228
  32.6 4.8 %collective-permute-start.1 = (bf16[1,4,32,256]{3,2,1,0:T(8,128)(2,1)S(1)}, bf16[1,4,32,256]{3,2,1,0:T(8,128)(2,1)S(1)}, u32[]{:S(2)}, u32[]{:S(2)}) collective-permute-start(bf16[1,4,32,256]{3,2,1,0:T(8,128)(2,1)S(1)} %bitcast.26), channel_id=1, source_target_pairs={{0,448},{16,464},{32,480},{48,496},{64,0},{80,16},{96,32},{112,48}... | collective-permute-start | bytes 196616 | tf_op jit(solution)/shard_map/ppermute | solution.py:230
  37.4 1.7 %collective-permute-done.1 = bf16[1,4,32,256]{3,2,1,0:T(8,128)(2,1)S(1)} collective-permute-done((bf16[1,4,32,256]{3,2,1,0:T(8,128)(2,1)S(1)}, bf16[1,4,32,256]{3,2,1,0:T(8,128)(2,1)S(1)}, u32[]{:S(2)}, u32[]{:S(2)}) %collective-permute-start.1) | collective-permute-done | bytes 65568 | tf_op jit(solution)/shard_map/ppermute | solution.py:230
  39.1 6.4 %collective-permute-start.2 = (bf16[2,4,32,256]{3,2,1,0:T(8,128)(2,1)S(1)}, bf16[2,4,32,256]{3,2,1,0:T(8,128)(2,1)S(1)}, u32[]{:S(2)}, u32[]{:S(2)}) collective-permute-start(bf16[2,4,32,256]{3,2,1,0:T(8,128)(2,1)S(1)} %pad_maximum_fusion.refs_0_), channel_id=1, source_target_pairs={{0,384},{16,400},{32,416},{48,432},{64,448},{80,464},{96,480},{112... | collective-permute-start | bytes 393224 | tf_op jit(solution)/shard_map/ppermute | solution.py:230
  45.5 5.0 %collective-permute-done.2.refs_1_ = bf16[2,4,32,256]{3,2,1,0:T(8,128)(2,1)S(1)} collective-permute-done((bf16[2,4,32,256]{3,2,1,0:T(8,128)(2,1)S(1)}, bf16[2,4,32,256]{3,2,1,0:T(8,128)(2,1)S(1)}, u32[]{:S(2)}, u32[]{:S(2)}) %collective-permute-start.2) | collective-permute-done | bytes 131104 | tf_op jit(solution)/shard_map/ppermute | solution.py:230
  50.5 6.3 %collective-permute-start.3 = (bf16[2,4,32,256]{3,2,1,0:T(8,128)(2,1)S(1)}, bf16[2,4,32,256]{3,2,1,0:T(8,128)(2,1)S(1)}, u32[]{:S(2)}, u32[]{:S(2)}) collective-permute-start(bf16[2,4,32,256]{3,2,1,0:T(8,128)(2,1)S(1)} %collective-permute-done.2.refs_1_), channel_id=1, source_target_pairs={{0,384},{16,400},{32,416},{48,432},{64,448},{80,464},{96,480},{112... | collective-permute-start | bytes 393224 | tf_op jit(solution)/shard_map/ppermute | solution.py:230
  56.8 6.3 %collective-permute-done.3.refs_2_ = bf16[2,4,32,256]{3,2,1,0:T(8,128)(2,1)S(1)} collective-permute-done((bf16[2,4,32,256]{3,2,1,0:T(8,128)(2,1)S(1)}, bf16[2,4,32,256]{3,2,1,0:T(8,128)(2,1)S(1)}, u32[]{:S(2)}, u32[]{:S(2)}) %collective-permute-start.3) | collective-permute-done | bytes 131104 | tf_op jit(solution)/shard_map/ppermute | solution.py:230
  63.1 5.6 %collective-permute-start.4 = (bf16[2,4,32,256]{3,2,1,0:T(8,128)(2,1)S(1)}, bf16[2,4,32,256]{3,2,1,0:T(8,128)(2,1)S(1)}, u32[]{:S(2)}, u32[]{:S(2)}) collective-permute-start(bf16[2,4,32,256]{3,2,1,0:T(8,128)(2,1)S(1)} %collective-permute-done.3.refs_2_), channel_id=1, source_target_pairs={{0,384},{16,400},{32,416},{48,432},{64,448},{80,464},{96,480},{112... | collective-permute-start | bytes 393224 | tf_op jit(solution)/shard_map/ppermute | solution.py:230
  68.8 0.9 prepare.1
  69.7 1.0 copy-done.1
  70.6 2.6 %collective-permute-done.4.refs_3_ = bf16[2,4,32,256]{3,2,1,0:T(8,128)(2,1)S(1)} collective-permute-done((bf16[2,4,32,256]{3,2,1,0:T(8,128)(2,1)S(1)}, bf16[2,4,32,256]{3,2,1,0:T(8,128)(2,1)S(1)}, u32[]{:S(2)}, u32[]{:S(2)}) %collective-permute-start.4) | collective-permute-done | bytes 131104 | tf_op jit(solution)/shard_map/ppermute | solution.py:230
  73.2 1.4 %copy-done = bf16[32,3,32,256]{3,2,1,0:T(8,128)(2,1)S(1)} copy-done((bf16[32,3,32,256]{3,2,1,0:T(8,128)(2,1)S(1)}, bf16[32,3,32,256]{3,2,1,0:T(8,128)(2,1)}, u32[]{:S(2)}) %copy-start) | copy-done | bytes 1572888
  74.7 1.2 %copy-done.2 = f32[4,256,256]{2,1,0:T(8,128)S(1)} copy-done((f32[4,256,256]{2,1,0:T(8,128)S(1)}, f32[4,256,256]{2,1,0:T(8,128)}, u32[]{:S(2)}) %copy-start.2) | copy-done | bytes 1048600
  75.9 5.0 %layer.1 = bf16[4,2,64,1024]{3,2,1,0:T(8,128)(2,1)S(1)} custom-call(s32[1]{0:T(128)} %bitcast.row_ref, bf16[4,3,64,1024]{3,2,1,0:T(8,128)(2,1)S(1)} %all-to-all-done.1.tok_ref, bf16[2,256,1024]{2,1,0:T(8,128)(2,1)S(1)} %get-tuple-element.18.normed_ref, f32[256,128]{1,0:T(8,128)S(1)} %get-tuple-element.19.inv_ref, f32[4,256,256]{2,1,0:T(8,128)S(1)} %copy-done.2, ...), custom_call_target="tpu_custom_call" | custom-call | flops 1500000000 | bytes 1000000 | tf_op jit(solution)/shard_map/layer/pallas_call | solution.py:181
  80.9 13.1 %all_to_all.16.parts_ref = bf16[4,2,64,1024]{3,2,1,0:T(8,128)(2,1)S(1)} all-to-all(bf16[4,2,64,1024]{3,2,1,0:T(8,128)(2,1)S(1)} %layer.1), channel_id=1, replica_groups={{0,16,32,48},{64,80,96,112},{128,144,160,176},{192,208,224,240},{256,27..., dimensions={0} | all-to-all | bytes 2097152 | tf_op jit(solution)/shard_map/all_to_all | solution.py:256
  94.2 8.9 %collective-permute-start.5 = (bf16[64,1024]{1,0:T(8,128)(2,1)S(1)}, bf16[64,1024]{1,0:T(8,128)(2,1)S(1)}, u32[]{:S(2)}, u32[]{:S(2)}) collective-permute-start(bf16[64,1024]{1,0:T(8,128)(2,1)S(1)} %get-tuple-element.22), channel_id=1, source_target_pairs={{0,1},{1,2},{2,3},{3,4},{4,5},{5,6},{6,7},{7,8},{8,9},{9,10},{10,1... | collective-permute-start | bytes 393224 | tf_op jit(solution)/shard_map/ppermute | solution.py:264
  103.1 0.9 collective-permute-start.6
  103.9 1.1 collective-permute-done.5
  105.0 2.7 %collective-permute-done.6 = bf16[64,1024]{1,0:T(8,128)(2,1)S(1)} collective-permute-done((bf16[64,1024]{1,0:T(8,128)(2,1)S(1)}, bf16[64,1024]{1,0:T(8,128)(2,1)S(1)}, u32[]{:S(2)}, u32[]{:S(2)}) %collective-permute-start.6) | collective-permute-done | bytes 131104 | tf_op jit(solution)/shard_map/ppermute | solution.py:265
  107.8 0.7 bitcast_convert_fusion
  (17 shorter events, 0.9 us)
Async XLA Ops:
  7.2 66.1 %all-gather.3.cloned.1.call-start = ((), (), s32[]{:S(2)}) async-start(), calls=%async_computation.3 | async-start | bytes 1769472 | tf_op jit(solution)/shard_map/all_gather | solution.py:226
  19.1 4.1 %collective-permute-start = (bf16[4,1,32,256]{3,2,0,1:T(8,128)(2,1)}, bf16[4,1,32,256]{3,2,0,1:T(8,128)(2,1)S(1)}, u32[]{:S(2)}, u32[]{:S(2)}) collective-permute-start(bf16[4,1,32,256]{3,2,0,1:T(8,128)(2,1)} %bitcast.28), channel_id=1, source_target_pairs={{0,0},{16,64},{32,128},{48,192},{64,256},{80,320},{96,384},{112,44... | collective-permute-start | bytes 196616 | tf_op jit(solution)/shard_map/ppermute | solution.py:211
  23.2 45.5 %copy-start.5 = (f32[1,1024]{1,0:T(1,128)S(1)}, f32[1,1024]{1,0:T(1,128)}, u32[]{:S(2)}) copy-start(f32[1,1024]{1,0:T(1,128)} %gain_ref.3) | copy-start | bytes 12292
  23.2 39.9 %all-to-all-start.1 = ((bf16[4,3,64,1024]{3,2,1,0:T(8,128)(2,1)}), bf16[4,3,64,1024]{3,2,1,0:T(8,128)(2,1)S(1)}, u32[]{:S(2)}, u32[]{:S(2)}) async-start(bf16[4,3,64,1024]{3,2,1,0:T(8,128)(2,1)} %pack_tokens.1), calls=%async_computation.1 | async-start | bytes 3145728 | tf_op jit(solution)/shard_map/all_to_all | solution.py:228
  32.6 6.5 %collective-permute-start.1 = (bf16[1,4,32,256]{3,2,1,0:T(8,128)(2,1)S(1)}, bf16[1,4,32,256]{3,2,1,0:T(8,128)(2,1)S(1)}, u32[]{:S(2)}, u32[]{:S(2)}) collective-permute-start(bf16[1,4,32,256]{3,2,1,0:T(8,128)(2,1)S(1)} %bitcast.26), channel_id=1, source_target_pairs={{0,448},{16,464},{32,480},{48,496},{64,0},{80,16},{96,32},{112,48}... | collective-permute-start | bytes 196616 | tf_op jit(solution)/shard_map/ppermute | solution.py:230
  39.1 11.4 %collective-permute-start.2 = (bf16[2,4,32,256]{3,2,1,0:T(8,128)(2,1)S(1)}, bf16[2,4,32,256]{3,2,1,0:T(8,128)(2,1)S(1)}, u32[]{:S(2)}, u32[]{:S(2)}) collective-permute-start(bf16[2,4,32,256]{3,2,1,0:T(8,128)(2,1)S(1)} %pad_maximum_fusion.refs_0_), channel_id=1, source_target_pairs={{0,384},{16,400},{32,416},{48,432},{64,448},{80,464},{96,480},{112... | collective-permute-start | bytes 393224 | tf_op jit(solution)/shard_map/ppermute | solution.py:230
  50.5 12.6 %collective-permute-start.3 = (bf16[2,4,32,256]{3,2,1,0:T(8,128)(2,1)S(1)}, bf16[2,4,32,256]{3,2,1,0:T(8,128)(2,1)S(1)}, u32[]{:S(2)}, u32[]{:S(2)}) collective-permute-start(bf16[2,4,32,256]{3,2,1,0:T(8,128)(2,1)S(1)} %collective-permute-done.2.refs_1_), channel_id=1, source_target_pairs={{0,384},{16,400},{32,416},{48,432},{64,448},{80,464},{96,480},{112... | collective-permute-start | bytes 393224 | tf_op jit(solution)/shard_map/ppermute | solution.py:230
  63.1 10.1 %collective-permute-start.4 = (bf16[2,4,32,256]{3,2,1,0:T(8,128)(2,1)S(1)}, bf16[2,4,32,256]{3,2,1,0:T(8,128)(2,1)S(1)}, u32[]{:S(2)}, u32[]{:S(2)}) collective-permute-start(bf16[2,4,32,256]{3,2,1,0:T(8,128)(2,1)S(1)} %collective-permute-done.3.refs_2_), channel_id=1, source_target_pairs={{0,384},{16,400},{32,416},{48,432},{64,448},{80,464},{96,480},{112... | collective-permute-start | bytes 393224 | tf_op jit(solution)/shard_map/ppermute | solution.py:230
  69.7 1.0 copy-start.1
  73.2 1.4 %copy-start = (bf16[32,3,32,256]{3,2,1,0:T(8,128)(2,1)S(1)}, bf16[32,3,32,256]{3,2,1,0:T(8,128)(2,1)}, u32[]{:S(2)}) copy-start(bf16[32,3,32,256]{3,2,1,0:T(8,128)(2,1)} %all-gather.3.cloned.1.call-done) | copy-start | bytes 4718596
  74.6 1.2 %copy-start.2 = (f32[4,256,256]{2,1,0:T(8,128)S(1)}, f32[4,256,256]{2,1,0:T(8,128)}, u32[]{:S(2)}) copy-start(f32[4,256,256]{2,1,0:T(8,128)} %copy-done.1) | copy-start | bytes 3145732
  80.9 13.2 %copy-start.3 = (f32[1,64,1024]{2,1,0:T(8,128)S(1)}, f32[1,64,1024]{2,1,0:T(8,128)}, u32[]{:S(2)}) copy-start(f32[1,64,1024]{2,1,0:T(8,128)} %param.10) | copy-start | bytes 786436
  80.9 13.2 %copy-start.4 = (bf16[1,64,1024]{2,1,0:T(8,128)(2,1)S(1)}, bf16[1,64,1024]{2,1,0:T(8,128)(2,1)}, u32[]{:S(2)}) copy-start(bf16[1,64,1024]{2,1,0:T(8,128)(2,1)} %param.8) | copy-start | bytes 393220
  94.2 10.8 %collective-permute-start.5 = (bf16[64,1024]{1,0:T(8,128)(2,1)S(1)}, bf16[64,1024]{1,0:T(8,128)(2,1)S(1)}, u32[]{:S(2)}, u32[]{:S(2)}) collective-permute-start(bf16[64,1024]{1,0:T(8,128)(2,1)S(1)} %get-tuple-element.22), channel_id=1, source_target_pairs={{0,1},{1,2},{2,3},{3,4},{4,5},{5,6},{6,7},{7,8},{8,9},{9,10},{10,1... | collective-permute-start | bytes 393224 | tf_op jit(solution)/shard_map/ppermute | solution.py:264
  103.1 4.7 %collective-permute-start.6 = (bf16[64,1024]{1,0:T(8,128)(2,1)S(1)}, bf16[64,1024]{1,0:T(8,128)(2,1)S(1)}, u32[]{:S(2)}, u32[]{:S(2)}) collective-permute-start(bf16[64,1024]{1,0:T(8,128)(2,1)S(1)} %get-tuple-element.23), channel_id=1, source_target_pairs={{1,0},{2,1},{3,2},{4,3},{5,4},{6,5},{7,6},{8,7},{9,8},{10,9},{11,1... | collective-permute-start | bytes 393224 | tf_op jit(solution)/shard_map/ppermute | solution.py:265
Sparse Core Ops, SparseCore 0:
  19.2 48.1 all-gather.2

commit v3 on v2

--- a/solution.py
+++ b/solution.py
@@ -89,7 +89,7 @@
         out[...] = total.astype(BF16)
 
 
-def prepare(tok_ref, gain_ref, normed_ref, inv_ref, bias_ref):
+def prepare(tok_ref, gain_ref, normed_ref, inv_ref):
     for which in range(2):
         for part in range(GROUP):
             xf = tok_ref[part, which].astype(F32)
@@ -98,24 +98,25 @@
             normed_ref[which, rows, :] = (xf * inv * gain_ref[...]).astype(BF16)
             if which == 1:
                 inv_ref[rows, :] = jnp.broadcast_to(inv, (64, 128))
-    for head, bias in enumerate(pair_bias(GROUP * 64)):
+
+
+def deliver(next_ref, prev_ref, next_out, prev_out):
+    next_out[...] = next_ref[...]
+    prev_out[...] = prev_ref[...].astype(F32)
+
+
+def layer(tok_ref, normed_ref, inv_ref, gain_ref, w_ref, out_ref, bias_ref):
+    rows = GROUP * 64
+    for head, bias in enumerate(pair_bias(rows)):
         bias_ref[head] = bias
-
-
-def layer(row_ref, tok_ref, normed_ref, inv_ref, bias_ref, gain_ref, qkv_ref, *refs):
-    pieces, (out_ref, own_ref) = refs[:-2], refs[-2:]
-    rows = GROUP * 64
-    deep = 2 * len(pieces)
-    for k in range(deep):
-        own_ref[(row_ref[0] + k) % deep] = pieces[k // 2][k % 2]
     heads = head_masks(rows)
     scale = jnp.asarray(HEAD**-0.5, BF16)
 
     def weight(i):
-        return qkv_ref[:, :, i].reshape(1024, 256)
+        return w_ref[:, :, i].reshape(1024, 256)
 
     def out_weight(c):
-        return own_ref[:, c].reshape(256, 256)
+        return w_ref[:, c, 3].reshape(256, 256)
 
     def projected(which):
         normed = normed_ref[which]
@@ -196,7 +197,6 @@
     deep = seqs // GROUP
     row_groups = [[GROUP * y + x for x in range(GROUP)] for y in range(deep)]
     columns = [[GROUP * y + x for y in range(deep)] for x in range(GROUP)]
-    row = (lax.axis_index("seq") // GROUP).reshape(1)
 
     qkv, own = call(
         pack_weights,
@@ -222,35 +222,22 @@
         ),
         mib=63,
     )
-    mine = qkv
-    qkv = lax.all_gather(qkv, "seq", axis_index_groups=columns)
-    _, own, tokens = lax.optimization_barrier((mine, own, tokens))
+    weights = jnp.concatenate((qkv, own), axis=1)
+    weights, tokens = lax.optimization_barrier((weights, tokens))
+    weights = lax.all_gather(weights, "seq", axis_index_groups=columns)
     tokens = lax.all_to_all(tokens, "seq", 0, 0, axis_index_groups=row_groups, tiled=True)
-    def up(value, steps):
-        return lax.ppermute(
-            value, "seq", [(s, (s - steps * GROUP) % seqs) for s in range(seqs)]
-        )
-
-    own = own.reshape(1, GROUP, 32, 256)
-    pieces = [jnp.concatenate((own, up(own, 1)))]
-    for step in range(2, deep, 2):
-        pieces.append(up(pieces[-1], 2))
-        if step == 4:
-            pieces[-1], tokens = lax.optimization_barrier((pieces[-1], tokens))
-
-    normed, inv, bias = call(
+    normed, inv = call(
         prepare,
-        [((2, 256, 1024), BF16), ((256, 128), F32), ((HEADS, 256, 256), F32)],
+        [((2, 256, 1024), BF16), ((256, 128), F32)],
         (tokens, norm_gain),
         "prepare",
     )
     parts, = call(
         layer,
         [((GROUP, 2, 64, 1024), BF16)],
-        (row, tokens, normed, inv, bias, norm_gain, qkv, *pieces),
+        (tokens, normed, inv, norm_gain, weights),
         "layer",
-        in_specs=[SMEM] + [VMEM] * (6 + deep // 2),
-        scratch=(pltpu.VMEM((deep, GROUP, 32, 256), BF16),),
+        scratch=(pltpu.VMEM((HEADS, 256, 256), F32),),
         flops=15 * 10**8,
     )
     parts = lax.all_to_all(parts, "seq", 0, 0, axis_index_groups=row_groups, tiled=True)
@@ -263,7 +250,13 @@
     ring = [(c, (c + 1) % sections) for c in range(sections)]
     next_input = lax.ppermute(layer_out, "section", ring)
     prev_grad = lax.ppermute(input_grad, "section", [(b, a) for a, b in ring])
-    return next_input[None], prev_grad.astype(F32)[None]
+    next_input, prev_grad = call(
+        deliver,
+        [((64, 1024), BF16), ((64, 1024), F32)],
+        (next_input, prev_grad),
+        "deliver",
+    )
+    return next_input[None], prev_grad[None]
 
 
 def solution(mesh):

time: 117 us -> 111 us (0.949)
  starting transfers between devices: 43.7 us -> 13.1 us
  blocking collectives: 23.3 us -> 38.5 us
  waiting for transfers between devices: 19.5 us -> 31.3 us
  local copies, waits for them, and re-layouts: 4.28 us -> 1.61 us
    all_gather x1, waiting for transfers between devices: 0.01 us -> 25.9 us  [per_device(): weights = lax.all_gather(weights, 'seq', axis_index_groups=columns)]
    ppermute x4 -> x0, starting transfers between devices: 23 us -> none  [up(): lax.ppermute(value, 'seq', [(s, (s - steps * GROUP) % seqs) for s in rang...]
    ppermute x4 -> x0, waiting for transfers between devices: 15.6 us -> none  [up(): lax.ppermute(value, 'seq', [(s, (s - steps * GROUP) % seqs) for s in rang...]
    all_to_all x1, blocking collectives: 10.1 us -> 24 us  [per_device(): lax.all_to_all(tokens, 'seq', 0, 0, axis_index_groups=row_groups, tiled=T...]
    all_to_all x1, starting transfers between devices: 9.39 us -> 4.85 us  [per_device(): lax.all_to_all(qkv, 'seq', 0, 0, axis_index_groups=row_groups, tiled=True)]
    unnamed x13 -> x8, local copies, waits for them, and re-layouts: 4.28 us -> 1.61 us
    ppermute x1, starting transfers between devices: 8.87 us -> 6.76 us  [per_device(): next_input = lax.ppermute(layer_out, 'section', ring)]
    all_to_all x1, blocking collectives: 13.1 us -> 14.5 us  [per_device(): lax.all_to_all(parts, 'seq', 0, 0, axis_index_groups=row_groups, tiled=True)]
  transfers between devices with their start and end apart: 9 -> 5, of which waited for: 6 -> 4; matrix products, arithmetic and copies ran while one was open for 0% -> 0% of each run, Pallas kernels for 3% -> 3%
where the time goes in v3:
time: 111 us; the launch traced here: 110 us
  blocking collectives  38.5 us (35%)
  waiting for transfers between devices  31.3 us (28%)
  between operations  14.1 us (13%)
  starting transfers between devices  13.1 us (12%)
  Pallas kernels  10.7 us (10%)
  local copies, waits for them, and re-layouts  1.61 us (1%)
    all_gather x1, waiting for transfers between devices, per_device(): weights = lax.all_gather(weights, 'seq', axis_index_groups=columns)  25.9 us
    all_to_all x1, blocking collectives, per_device(): lax.all_to_all(tokens, 'seq', 0, 0, axis_index_groups=row_groups, tiled=T...  24 us
    all_to_all x1, blocking collectives, per_device(): lax.all_to_all(parts, 'seq', 0, 0, axis_index_groups=row_groups, tiled=True)  14.5 us
    pallas_call x6, Pallas kernels, call(): pl.pallas_call(body, out_shape=[jax.ShapeDtypeStruct(shape, kind) for sha...  10.7 us
    ppermute x1, starting transfers between devices, per_device(): next_input = lax.ppermute(layer_out, 'section', ring)  6.76 us
    all_to_all x1, starting transfers between devices, per_device(): lax.all_to_all(qkv, 'seq', 0, 0, axis_index_groups=row_groups, tiled=True)  4.85 us
    ppermute x1, waiting for transfers between devices, per_device(): prev_grad = lax.ppermute(input_grad, 'section', [(b, a) for a, b in ring])  2.44 us
  transfers between devices with their start and end apart: 5, of which 4 were waited for; matrix products, arithmetic and copies ran while one was open for 0% of the time, Pallas kernels for 3%

profile of v3, /device:TPU:1, one launch (start us, length us, event | category | flops | bytes accessed | tf_op | source)
XLA Modules:
  0.0 110.1 jit_solution(493823803642003781)
XLA Ops:
  7.2 1.7 %pack_weights.1 = (bf16[4,3,32,256]{3,2,1,0:T(8,128)(2,1)}, bf16[4,1,32,256]{3,2,1,0:T(8,128)(2,1)}) custom-call(bf16[32,1024]{1,0:T(8,128)(2,1)} %bitcast.16, bf16[32,1024]{1,0:T(8,128)(2,1)} %bitcast.17, bf16[32,1024]{1,0:T(8,128)(2,1)} %bitcast.18, bf16[32,1024]{1,0:T(8,128)(2,1)} %bitcast.19), custom_call_target="tpu_custom_call" | custom-call | flops 1000000 | bytes 1000000 | tf_op jit(solution)/shard_map/pack_weights/pallas_call | solution.py:182
  8.9 4.9 %all-to-all-start = ((bf16[4,3,32,256]{3,2,1,0:T(8,128)(2,1)}), bf16[4,3,32,256]{3,2,1,0:T(8,128)(2,1)S(1)}, u32[]{:S(2)}, u32[]{:S(2)}) async-start(bf16[4,3,32,256]{3,2,1,0:T(8,128)(2,1)} %get-tuple-element.12), calls=%async_computation | async-start | bytes 393216 | tf_op jit(solution)/shard_map/all_to_all | solution.py:210
  13.8 1.5 %collective-permute-start = (bf16[4,1,32,256]{3,2,1,0:T(8,128)(2,1)}, bf16[4,1,32,256]{3,2,1,0:T(8,128)(2,1)S(1)}, u32[]{:S(2)}, u32[]{:S(2)}) collective-permute-start(bf16[4,1,32,256]{3,2,1,0:T(8,128)(2,1)} %get-tuple-element.13), channel_id=1, source_target_pairs={{0,0},{16,64},{32,128},{48,192},{64,256},{80,320},{96,384},{112,44... | collective-permute-start | bytes 196616 | tf_op jit(solution)/shard_map/ppermute | solution.py:211
  15.2 2.6 %pack_tokens.1 = bf16[4,3,64,1024]{3,2,1,0:T(8,128)(2,1)} custom-call(bf16[64,1024]{1,0:T(8,128)(2,1)} %bitcast.13, bf16[64,1024]{1,0:T(8,128)(2,1)} %bitcast.15, f32[64,1024]{1,0:T(8,128)} %bitcast.11), custom_call_target="tpu_custom_call" | custom-call | flops 1000000 | bytes 1000000 | tf_op jit(solution)/shard_map/pack_tokens/pallas_call | solution.py:182
  17.9 0.0 collective-permute-done
  17.9 1.1 all-to-all-done
  18.9 0.7 pad_maximum_fusion
  19.7 0.0 all-gather.3.cloned.1.call-update
  19.7 0.0 copy-start.3
  19.7 24.0 %all_to_all.15.tok_ref = bf16[4,3,64,1024]{3,2,1,0:T(8,128)(2,1)S(1)} all-to-all(bf16[4,3,64,1024]{3,2,1,0:T(8,128)(2,1)} %pack_tokens.1), channel_id=1, replica_groups={{0,16,32,48},{64,80,96,112},{128,144,160,176},{192,208,224,240},{256,27..., dimensions={0} | all-to-all | bytes 3145728 | tf_op jit(solution)/shard_map/all_to_all | solution.py:228
  43.7 0.4 prepare.1
  44.1 25.9 %all-gather.3.cloned.1.call-done = bf16[32,4,32,256]{3,2,1,0:T(8,128)(2,1)} async-done(((bf16[4,4,32,256]{3,2,1,0:T(8,128)(2,1)}), bf16[32,4,32,256]{3,2,1,0:T(8,128)(2,1)}) %all-gather.3.cloned.1.call-update) | async-done | bytes 2097168 | tf_op jit(solution)/shard_map/all_gather | solution.py:227
  70.0 1.6 %copy-done = bf16[32,4,32,256]{3,2,1,0:T(8,128)(2,1)S(1)} copy-done((bf16[32,4,32,256]{3,2,1,0:T(8,128)(2,1)S(1)}, bf16[32,4,32,256]{3,2,1,0:T(8,128)(2,1)}, u32[]{:S(2)}) %copy-start) | copy-done | bytes 2097176
  71.6 5.1 %layer.1 = bf16[4,2,64,1024]{3,2,1,0:T(8,128)(2,1)S(1)} custom-call(bf16[4,3,64,1024]{3,2,1,0:T(8,128)(2,1)S(1)} %all_to_all.15.tok_ref, bf16[2,256,1024]{2,1,0:T(8,128)(2,1)S(1)} %get-tuple-element.15.normed_ref, f32[256,128]{1,0:T(8,128)S(1)} %get-tuple-element.16.inv_ref, f32[1,1024]{1,0:T(1,128)S(1)} %copy-done.3, bf16[8,4,4,32,256]{4,3,2,1,0:T(8,128)(2,1)S(1)} %bitcast.10), custom_call_target="tpu_custom_call" | custom-call | flops 1500000000 | bytes 1000000 | tf_op jit(solution)/shard_map/layer/pallas_call | solution.py:182
  76.7 0.0 copy-start.1
  76.7 0.0 copy-start.2
  76.7 14.5 %all_to_all.16.parts_ref = bf16[4,2,64,1024]{3,2,1,0:T(8,128)(2,1)S(1)} all-to-all(bf16[4,2,64,1024]{3,2,1,0:T(8,128)(2,1)S(1)} %layer.1), channel_id=1, replica_groups={{0,16,32,48},{64,80,96,112},{128,144,160,176},{192,208,224,240},{256,27..., dimensions={0} | all-to-all | bytes 2097152 | tf_op jit(solution)/shard_map/all_to_all | solution.py:243
  91.1 0.0 copy-done.1
  91.1 0.2 finish.1
  91.3 6.8 %collective-permute-start.1 = (bf16[64,1024]{1,0:T(8,128)(2,1)S(1)}, bf16[64,1024]{1,0:T(8,128)(2,1)S(1)}, u32[]{:S(2)}, u32[]{:S(2)}) collective-permute-start(bf16[64,1024]{1,0:T(8,128)(2,1)S(1)} %get-tuple-element.18), channel_id=1, source_target_pairs={{0,1},{1,2},{2,3},{3,4},{4,5},{5,6},{6,7},{7,8},{8,9},{9,10},{10,1... | collective-permute-start | bytes 393224 | tf_op jit(solution)/shard_map/ppermute | solution.py:251
  98.1 0.0 collective-permute-start.2
  98.1 1.9 %collective-permute-done.1.next_ref = bf16[64,1024]{1,0:T(8,128)(2,1)S(1)} collective-permute-done((bf16[64,1024]{1,0:T(8,128)(2,1)S(1)}, bf16[64,1024]{1,0:T(8,128)(2,1)S(1)}, u32[]{:S(2)}, u32[]{:S(2)}) %collective-permute-start.1) | collective-permute-done | bytes 131104 | tf_op jit(solution)/shard_map/ppermute | solution.py:251
  100.0 2.4 %collective-permute-done.2.prev_ref = bf16[64,1024]{1,0:T(8,128)(2,1)S(1)} collective-permute-done((bf16[64,1024]{1,0:T(8,128)(2,1)S(1)}, bf16[64,1024]{1,0:T(8,128)(2,1)S(1)}, u32[]{:S(2)}, u32[]{:S(2)}) %collective-permute-start.2) | collective-permute-done | bytes 131104 | tf_op jit(solution)/shard_map/ppermute | solution.py:252
  102.5 0.8 deliver.1
  (4 shorter events, 0.0 us)
Async XLA Ops:
  8.9 10.0 %all-to-all-start = ((bf16[4,3,32,256]{3,2,1,0:T(8,128)(2,1)}), bf16[4,3,32,256]{3,2,1,0:T(8,128)(2,1)S(1)}, u32[]{:S(2)}, u32[]{:S(2)}) async-start(bf16[4,3,32,256]{3,2,1,0:T(8,128)(2,1)} %get-tuple-element.12), calls=%async_computation | async-start | bytes 393216 | tf_op jit(solution)/shard_map/all_to_all | solution.py:210
  13.8 56.2 %all-gather.3.cloned.1.call-start = ((), (), s32[]{:S(2)}) async-start(), calls=%async_computation.3 | async-start | bytes 2359296 | tf_op jit(solution)/shard_map/all_gather | solution.py:227
  13.8 4.1 %collective-permute-start = (bf16[4,1,32,256]{3,2,1,0:T(8,128)(2,1)}, bf16[4,1,32,256]{3,2,1,0:T(8,128)(2,1)S(1)}, u32[]{:S(2)}, u32[]{:S(2)}) collective-permute-start(bf16[4,1,32,256]{3,2,1,0:T(8,128)(2,1)} %get-tuple-element.13), channel_id=1, source_target_pairs={{0,0},{16,64},{32,128},{48,192},{64,256},{80,320},{96,384},{112,44... | collective-permute-start | bytes 196616 | tf_op jit(solution)/shard_map/ppermute | solution.py:211
  19.7 24.0 %copy-start.3 = (f32[1,1024]{1,0:T(1,128)S(1)}, f32[1,1024]{1,0:T(1,128)}, u32[]{:S(2)}) copy-start(f32[1,1024]{1,0:T(1,128)} %gain_ref.3) | copy-start | bytes 12292
  70.0 1.6 %copy-start = (bf16[32,4,32,256]{3,2,1,0:T(8,128)(2,1)S(1)}, bf16[32,4,32,256]{3,2,1,0:T(8,128)(2,1)}, u32[]{:S(2)}) copy-start(bf16[32,4,32,256]{3,2,1,0:T(8,128)(2,1)} %all-gather.3.cloned.1.call-done) | copy-start | bytes 6291460
  76.7 14.5 %copy-start.1 = (f32[1,64,1024]{2,1,0:T(8,128)S(1)}, f32[1,64,1024]{2,1,0:T(8,128)}, u32[]{:S(2)}) copy-start(f32[1,64,1024]{2,1,0:T(8,128)} %param.10) | copy-start | bytes 786436
  76.7 14.5 %copy-start.2 = (bf16[1,64,1024]{2,1,0:T(8,128)(2,1)S(1)}, bf16[1,64,1024]{2,1,0:T(8,128)(2,1)}, u32[]{:S(2)}) copy-start(bf16[1,64,1024]{2,1,0:T(8,128)(2,1)} %param.8) | copy-start | bytes 393220
  91.3 8.7 %collective-permute-start.1 = (bf16[64,1024]{1,0:T(8,128)(2,1)S(1)}, bf16[64,1024]{1,0:T(8,128)(2,1)S(1)}, u32[]{:S(2)}, u32[]{:S(2)}) collective-permute-start(bf16[64,1024]{1,0:T(8,128)(2,1)S(1)} %get-tuple-element.18), channel_id=1, source_target_pairs={{0,1},{1,2},{2,3},{3,4},{4,5},{5,6},{6,7},{7,8},{8,9},{9,10},{10,1... | collective-permute-start | bytes 393224 | tf_op jit(solution)/shard_map/ppermute | solution.py:251
  98.1 4.4 %collective-permute-start.2 = (bf16[64,1024]{1,0:T(8,128)(2,1)S(1)}, bf16[64,1024]{1,0:T(8,128)(2,1)S(1)}, u32[]{:S(2)}, u32[]{:S(2)}) collective-permute-start(bf16[64,1024]{1,0:T(8,128)(2,1)S(1)} %get-tuple-element.19), channel_id=1, source_target_pairs={{1,0},{2,1},{3,2},{4,3},{5,4},{6,5},{7,6},{8,7},{9,8},{10,9},{11,1... | collective-permute-start | bytes 393224 | tf_op jit(solution)/shard_map/ppermute | solution.py:252
Sparse Core Ops, SparseCore 0:
  19.8 50.1 all-gather.2

commit v4 on v3

--- a/solution.py
+++ b/solution.py
@@ -54,19 +54,26 @@
     return jnp.where(mask, value, jnp.zeros((), value.dtype))
 
 
-def pack_weights(q_hbm, k_hbm, v_hbm, o_hbm, qkv_out, own_out, sems):
+def pack_weights(q_hbm, k_hbm, v_hbm, out_ref, sems):
     copies = []
     for block in range(GROUP):
         columns = slice(256 * block, 256 * block + 256)
-        for i, ref in enumerate((q_hbm, k_hbm, v_hbm, o_hbm)):
-            target = own_out.at[block, 0] if i == 3 else qkv_out.at[block, i]
-            copies.append(pltpu.make_async_copy(ref.at[:, columns], target, sems.at[block, i]))
+        for i, ref in enumerate((q_hbm, k_hbm, v_hbm)):
+            source, target = ref.at[:, columns], out_ref.at[block, i]
+            copies.append(pltpu.make_async_copy(source, target, sems.at[block, i]))
             copies[-1].start()
     for copy in copies:
         copy.wait()
 
 
-def pack_tokens(fwd_hbm, bwd_hbm, grad_hbm, out_ref, grad_ref, sems, grad_sem):
+def join_weights(qkv_ref, own_ref, out_ref):
+    for block in range(GROUP):
+        out_ref[block, :3] = qkv_ref[block]
+        out_ref[block, 3] = own_ref[:, 256 * block : 256 * block + 256]
+
+
+def pack_tokens(after_hbm, fwd_hbm, bwd_hbm, grad_hbm, out_ref, grad_ref, sems, grad_sem):
+    del after_hbm
     first = pltpu.make_async_copy(grad_hbm, grad_ref, grad_sem)
     first.start()
     copies = []
@@ -89,7 +96,7 @@
         out[...] = total.astype(BF16)
 
 
-def prepare(tok_ref, gain_ref, normed_ref, inv_ref):
+def prepare(tok_ref, gain_ref, normed_ref, inv_ref, bias_ref):
     for which in range(2):
         for part in range(GROUP):
             xf = tok_ref[part, which].astype(F32)
@@ -98,6 +105,8 @@
             normed_ref[which, rows, :] = (xf * inv * gain_ref[...]).astype(BF16)
             if which == 1:
                 inv_ref[rows, :] = jnp.broadcast_to(inv, (64, 128))
+    for head, bias in enumerate(pair_bias(GROUP * 64)):
+        bias_ref[head] = bias
 
 
 def deliver(next_ref, prev_ref, next_out, prev_out):
@@ -105,22 +114,28 @@
     prev_out[...] = prev_ref[...].astype(F32)
 
 
-def layer(tok_ref, normed_ref, inv_ref, gain_ref, w_ref, out_ref, bias_ref):
+def layer(tok_ref, normed_ref, inv_ref, bias_ref, gain_ref, w_hbm, out_ref, w_ref, sems):
     rows = GROUP * 64
-    for head, bias in enumerate(pair_bias(rows)):
-        bias_ref[head] = bias
+    copies = []
+    for i in range(4):
+        copies.append(pltpu.make_async_copy(w_hbm.at[:, :, i], w_ref.at[i], sems.at[i]))
+        copies[-1].start()
     heads = head_masks(rows)
     scale = jnp.asarray(HEAD**-0.5, BF16)
 
     def weight(i):
-        return w_ref[:, :, i].reshape(1024, 256)
+        return w_ref[i].reshape(1024, 256)
 
     def out_weight(c):
-        return w_ref[:, c, 3].reshape(256, 256)
+        return w_ref[3, :, c].reshape(256, 256)
 
     def projected(which):
-        normed = normed_ref[which]
-        q, k, v = [mm(normed, weight(i), NN).astype(BF16) for i in range(3)]
+        results = []
+        for i in range(3):
+            if which == 0:
+                copies[i].wait()
+            results.append(mm(normed_ref[which], weight(i), NN).astype(BF16))
+        q, k, v = results
         return q * scale, k, v
 
     def prob_of(q_head, k, head):
@@ -135,6 +150,7 @@
         p = prob_of(only(heads[head], q), k, head).astype(BF16)
         attended = attended + mm(p, only(heads[head], v), NN)
     attended = attended.astype(BF16)
+    copies[3].wait()
     for c in range(4):
         part = mm(attended, out_weight(c), NN).astype(BF16)
         for to in range(GROUP):
@@ -198,23 +214,27 @@
     row_groups = [[GROUP * y + x for x in range(GROUP)] for y in range(deep)]
     columns = [[GROUP * y + x for y in range(deep)] for x in range(GROUP)]
 
-    qkv, own = call(
+    places = [(s, GROUP * (s % deep) + s // deep) for s in range(seqs)]
+    own = lax.ppermute(w_out[0], "seq", places)
+    qkv, = call(
         pack_weights,
-        [((GROUP, 3, 32, 256), BF16), ((GROUP, 1, 32, 256), BF16)],
-        (w_query[0], w_key[0], w_value[0], w_out[0]),
+        [((GROUP, 3, 32, 256), BF16)],
+        (w_query[0], w_key[0], w_value[0]),
         "pack_weights",
-        in_specs=[HBM] * 4,
-        scratch=(pltpu.SemaphoreType.DMA((GROUP, 4)),),
+        in_specs=[HBM] * 3,
+        scratch=(pltpu.SemaphoreType.DMA((GROUP, 3)),),
         mib=63,
     )
     qkv = lax.all_to_all(qkv, "seq", 0, 0, axis_index_groups=row_groups, tiled=True)
-    own = lax.ppermute(own, "seq", [(s, GROUP * (s % deep) + s // deep) for s in range(seqs)])
+    joined, = call(join_weights, [((GROUP, 4, 32, 256), BF16)], (qkv, own), "join_weights")
+    weights = lax.all_gather(joined, "seq", axis_index_groups=columns)
+
     tokens, = call(
         pack_tokens,
         [((GROUP, 3, 64, 1024), BF16)],
-        (fwd_input[0], bwd_input[0], bwd_grad[0]),
+        (joined, fwd_input[0], bwd_input[0], bwd_grad[0]),
         "pack_tokens",
-        in_specs=[HBM] * 3,
+        in_specs=[HBM] * 4,
         scratch=(
             pltpu.VMEM((64, 1024), F32),
             pltpu.SemaphoreType.DMA((GROUP, 2)),
@@ -222,22 +242,23 @@
         ),
         mib=63,
     )
-    weights = jnp.concatenate((qkv, own), axis=1)
-    weights, tokens = lax.optimization_barrier((weights, tokens))
-    weights = lax.all_gather(weights, "seq", axis_index_groups=columns)
     tokens = lax.all_to_all(tokens, "seq", 0, 0, axis_index_groups=row_groups, tiled=True)
-    normed, inv = call(
+    normed, inv, bias = call(
         prepare,
-        [((2, 256, 1024), BF16), ((256, 128), F32)],
+        [((2, 256, 1024), BF16), ((256, 128), F32), ((HEADS, 256, 256), F32)],
         (tokens, norm_gain),
         "prepare",
     )
     parts, = call(
         layer,
         [((GROUP, 2, 64, 1024), BF16)],
-        (tokens, normed, inv, norm_gain, weights),
+        (tokens, normed, inv, bias, norm_gain, weights),
         "layer",
-        scratch=(pltpu.VMEM((HEADS, 256, 256), F32),),
+        in_specs=[VMEM] * 5 + [HBM],
+        scratch=(
+            pltpu.VMEM((4, deep, GROUP, 32, 256), BF16),
+            pltpu.SemaphoreType.DMA((4,)),
+        ),
         flops=15 * 10**8,
     )
     parts = lax.all_to_all(parts, "seq", 0, 0, axis_index_groups=row_groups, tiled=True)

time: 111 us -> 112 us (level)
  local copies, waits for them, and re-layouts: 1.61 us -> 3.79 us
  Pallas kernels: 10.7 us -> 12.3 us
  waiting for transfers between devices: 31.3 us -> 29.9 us
    all_gather x1, waiting for transfers between devices: 25.9 us -> 21.8 us  [per_device(): weights = lax.all_gather(joined, 'seq', axis_index_groups=columns)]
    all_to_all x1, waiting for transfers between devices: 1.06 us -> 3.68 us  [per_device(): lax.all_to_all(qkv, 'seq', 0, 0, axis_index_groups=row_groups, tiled=True)]
    unnamed x8 -> x12, local copies, waits for them, and re-layouts: 1.61 us -> 3.79 us
    pallas_call x6 -> x7, Pallas kernels: 10.7 us -> 12.3 us  [call(): pl.pallas_call(body, out_shape=[jax.ShapeDtypeStruct(shape, kind) for sha...]
where the time goes in v4:
time: 112 us
  blocking collectives  37.9 us (34%)
  waiting for transfers between devices  29.9 us (27%)
  between operations  14.1 us (13%)
  starting transfers between devices  13.7 us (12%)
  Pallas kernels  12.3 us (11%)
  local copies, waits for them, and re-layouts  3.79 us (3%)
    all_to_all x1, blocking collectives, per_device(): lax.all_to_all(tokens, 'seq', 0, 0, axis_index_groups=row_groups, tiled=T...  24 us
    all_gather x1, waiting for transfers between devices, per_device(): weights = lax.all_gather(joined, 'seq', axis_index_groups=columns)  21.8 us
    all_to_all x1, blocking collectives, per_device(): lax.all_to_all(parts, 'seq', 0, 0, axis_index_groups=row_groups, tiled=True)  13.9 us
    pallas_call x7, Pallas kernels, call(): pl.pallas_call(body, out_shape=[jax.ShapeDtypeStruct(shape, kind) for sha...  12.3 us
    ppermute x1, starting transfers between devices, per_device(): next_input = lax.ppermute(layer_out, 'section', ring)  7.32 us
    all_to_all x1, starting transfers between devices, per_device(): lax.all_to_all(qkv, 'seq', 0, 0, axis_index_groups=row_groups, tiled=True)  4.85 us
    unnamed x12, local copies, waits for them, and re-layouts  3.79 us
    all_to_all x1, waiting for transfers between devices, per_device(): lax.all_to_all(qkv, 'seq', 0, 0, axis_index_groups=row_groups, tiled=True)  3.68 us
  transfers between devices with their start and end apart: 5, of which 4 were waited for; matrix products, arithmetic and copies ran while one was open for 0% of the time, Pallas kernels for 3%

profile of v4, /device:TPU:1, one launch (start us, length us, event | category | flops | bytes accessed | tf_op | source)
XLA Modules:
  0.0 111.7 jit_solution(14717291756340769624)
XLA Ops:
  7.2 1.7 %pack_weights.1 = bf16[4,3,32,256]{3,2,1,0:T(8,128)(2,1)} custom-call(bf16[32,1024]{1,0:T(8,128)(2,1)} %bitcast.16, bf16[32,1024]{1,0:T(8,128)(2,1)} %bitcast.17, bf16[32,1024]{1,0:T(8,128)(2,1)} %bitcast.18), custom_call_target="tpu_custom_call" | custom-call | flops 1000000 | bytes 1000000 | tf_op jit(solution)/shard_map/pack_weights/pallas_call | solution.py:198
  8.8 4.9 %all-to-all-start = ((bf16[4,3,32,256]{3,2,1,0:T(8,128)(2,1)}), bf16[4,3,32,256]{3,2,1,0:T(8,128)(2,1)S(1)}, u32[]{:S(2)}, u32[]{:S(2)}) async-start(bf16[4,3,32,256]{3,2,1,0:T(8,128)(2,1)} %pack_weights.1), calls=%async_computation | async-start | bytes 393216 | tf_op jit(solution)/shard_map/all_to_all | solution.py:228
  13.7 1.5 %collective-permute-start = (bf16[32,1024]{1,0:T(8,128)(2,1)}, bf16[32,1024]{1,0:T(8,128)(2,1)S(1)}, u32[]{:S(2)}, u32[]{:S(2)}) collective-permute-start(bf16[32,1024]{1,0:T(8,128)(2,1)} %bitcast.21), channel_id=1, source_target_pairs={{0,0},{16,64},{32,128},{48,192},{64,256},{80,320},{96,384},{112,44... | collective-permute-start | bytes 196616 | tf_op jit(solution)/shard_map/ppermute | solution.py:218
  15.2 0.0 collective-permute-done.own_ref
  15.2 3.7 %all-to-all-done.qkv_ref = bf16[4,3,32,256]{3,2,1,0:T(8,128)(2,1)S(1)} async-done(((bf16[4,3,32,256]{3,2,1,0:T(8,128)(2,1)}), bf16[4,3,32,256]{3,2,1,0:T(8,128)(2,1)S(1)}, u32[]{:S(2)}, u32[]{:S(2)}) %all-to-all-start) | async-done | bytes 196640 | tf_op jit(solution)/shard_map/all_to_all | solution.py:228
  18.9 0.7 join_weights.1.after_hbm
  19.6 0.0 all-gather.3.cloned.1.call-update
  19.6 2.6 %pack_tokens.1 = bf16[4,3,64,1024]{3,2,1,0:T(8,128)(2,1)} custom-call(bf16[4,4,32,256]{3,2,1,0:T(8,128)(2,1)} %join_weights.1.after_hbm, bf16[64,1024]{1,0:T(8,128)(2,1)} %bitcast.13, bf16[64,1024]{1,0:T(8,128)(2,1)} %bitcast.15, f32[64,1024]{1,0:T(8,128)} %bitcast.11), custom_call_target="tpu_custom_call" | custom-call | flops 1000000 | bytes 1000000 | tf_op jit(solution)/shard_map/pack_tokens/pallas_call | solution.py:198
  22.2 0.0 copy-start.5
  22.2 24.0 %all_to_all.15.tok_ref = bf16[4,3,64,1024]{3,2,1,0:T(8,128)(2,1)S(1)} all-to-all(bf16[4,3,64,1024]{3,2,1,0:T(8,128)(2,1)} %pack_tokens.1), channel_id=1, replica_groups={{0,16,32,48},{64,80,96,112},{128,144,160,176},{192,208,224,240},{256,27..., dimensions={0} | all-to-all | bytes 3145728 | tf_op jit(solution)/shard_map/all_to_all | solution.py:245
  46.3 0.9 prepare.1
  47.2 1.0 copy-done.2
  48.1 21.8 %all-gather.3.cloned.1.call-done = bf16[32,4,32,256]{3,2,1,0:T(8,128)(2,1)} async-done(((bf16[4,4,32,256]{3,2,1,0:T(8,128)(2,1)}), bf16[32,4,32,256]{3,2,1,0:T(8,128)(2,1)}) %all-gather.3.cloned.1.call-update) | async-done | bytes 2097168 | tf_op jit(solution)/shard_map/all_gather | solution.py:230
  69.9 1.6 %copy-done = bf16[32,4,32,256]{3,2,1,0:T(8,128)(2,1)S(1)} copy-done((bf16[32,4,32,256]{3,2,1,0:T(8,128)(2,1)S(1)}, bf16[32,4,32,256]{3,2,1,0:T(8,128)(2,1)}, u32[]{:S(2)}) %copy-start) | copy-done | bytes 2097176
  71.5 1.2 %copy-done.3 = f32[4,256,256]{2,1,0:T(8,128)S(1)} copy-done((f32[4,256,256]{2,1,0:T(8,128)S(1)}, f32[4,256,256]{2,1,0:T(8,128)}, u32[]{:S(2)}) %copy-start.3) | copy-done | bytes 1048600
  72.7 5.5 %layer.1 = bf16[4,2,64,1024]{3,2,1,0:T(8,128)(2,1)S(1)} custom-call(bf16[4,3,64,1024]{3,2,1,0:T(8,128)(2,1)S(1)} %all_to_all.15.tok_ref, bf16[2,256,1024]{2,1,0:T(8,128)(2,1)S(1)} %get-tuple-element.9.normed_ref, f32[256,128]{1,0:T(8,128)S(1)} %get-tuple-element.10.inv_ref, f32[4,256,256]{2,1,0:T(8,128)S(1)} %copy-done.3, f32[1,1024]{1,0:T(1,128)S(1)} %copy-done.5, ...), custom_call_target="tpu_custom_call" | custom-call | flops 1500000000 | bytes 1000000 | tf_op jit(solution)/shard_map/layer/pallas_call | solution.py:198
  78.3 0.0 copy-start.1
  78.3 0.0 copy-start.4
  78.3 13.9 %all_to_all.16.parts_ref = bf16[4,2,64,1024]{3,2,1,0:T(8,128)(2,1)S(1)} all-to-all(bf16[4,2,64,1024]{3,2,1,0:T(8,128)(2,1)S(1)} %layer.1), channel_id=1, replica_groups={{0,16,32,48},{64,80,96,112},{128,144,160,176},{192,208,224,240},{256,27..., dimensions={0} | all-to-all | bytes 2097152 | tf_op jit(solution)/shard_map/all_to_all | solution.py:264
  92.2 0.2 finish.1
  92.4 7.3 %collective-permute-start.1 = (bf16[64,1024]{1,0:T(8,128)(2,1)S(1)}, bf16[64,1024]{1,0:T(8,128)(2,1)S(1)}, u32[]{:S(2)}, u32[]{:S(2)}) collective-permute-start(bf16[64,1024]{1,0:T(8,128)(2,1)S(1)} %get-tuple-element.12), channel_id=1, source_target_pairs={{0,1},{1,2},{2,3},{3,4},{4,5},{5,6},{6,7},{7,8},{8,9},{9,10},{10,1... | collective-permute-start | bytes 393224 | tf_op jit(solution)/shard_map/ppermute | solution.py:272
  99.7 1.9 %collective-permute-done.1.next_ref = bf16[64,1024]{1,0:T(8,128)(2,1)S(1)} collective-permute-done((bf16[64,1024]{1,0:T(8,128)(2,1)S(1)}, bf16[64,1024]{1,0:T(8,128)(2,1)S(1)}, u32[]{:S(2)}, u32[]{:S(2)}) %collective-permute-start.1) | collective-permute-done | bytes 131104 | tf_op jit(solution)/shard_map/ppermute | solution.py:272
  101.6 2.4 %collective-permute-done.2.prev_ref = bf16[64,1024]{1,0:T(8,128)(2,1)S(1)} collective-permute-done((bf16[64,1024]{1,0:T(8,128)(2,1)S(1)}, bf16[64,1024]{1,0:T(8,128)(2,1)S(1)}, u32[]{:S(2)}, u32[]{:S(2)}) %collective-permute-start.2) | collective-permute-done | bytes 131104 | tf_op jit(solution)/shard_map/ppermute | solution.py:273
  104.1 0.8 deliver.1
  (8 shorter events, 0.0 us)
Async XLA Ops:
  8.8 10.0 %all-to-all-start = ((bf16[4,3,32,256]{3,2,1,0:T(8,128)(2,1)}), bf16[4,3,32,256]{3,2,1,0:T(8,128)(2,1)S(1)}, u32[]{:S(2)}, u32[]{:S(2)}) async-start(bf16[4,3,32,256]{3,2,1,0:T(8,128)(2,1)} %pack_weights.1), calls=%async_computation | async-start | bytes 393216 | tf_op jit(solution)/shard_map/all_to_all | solution.py:228
  13.7 56.2 %all-gather.3.cloned.1.call-start = ((), (), s32[]{:S(2)}) async-start(), calls=%async_computation.3 | async-start | bytes 2359296 | tf_op jit(solution)/shard_map/all_gather | solution.py:230
  13.7 1.5 %collective-permute-start = (bf16[32,1024]{1,0:T(8,128)(2,1)}, bf16[32,1024]{1,0:T(8,128)(2,1)S(1)}, u32[]{:S(2)}, u32[]{:S(2)}) collective-permute-start(bf16[32,1024]{1,0:T(8,128)(2,1)} %bitcast.21), channel_id=1, source_target_pairs={{0,0},{16,64},{32,128},{48,192},{64,256},{80,320},{96,384},{112,44... | collective-permute-start | bytes 196616 | tf_op jit(solution)/shard_map/ppermute | solution.py:218
  22.2 24.0 %copy-start.5 = (f32[1,1024]{1,0:T(1,128)S(1)}, f32[1,1024]{1,0:T(1,128)}, u32[]{:S(2)}) copy-start(f32[1,1024]{1,0:T(1,128)} %gain_ref.3) | copy-start | bytes 12292
  47.2 1.0 copy-start.2
  69.9 1.6 %copy-start = (bf16[32,4,32,256]{3,2,1,0:T(8,128)(2,1)S(1)}, bf16[32,4,32,256]{3,2,1,0:T(8,128)(2,1)}, u32[]{:S(2)}) copy-start(bf16[32,4,32,256]{3,2,1,0:T(8,128)(2,1)} %all-gather.3.cloned.1.call-done) | copy-start | bytes 6291460
  71.5 1.2 %copy-start.3 = (f32[4,256,256]{2,1,0:T(8,128)S(1)}, f32[4,256,256]{2,1,0:T(8,128)}, u32[]{:S(2)}) copy-start(f32[4,256,256]{2,1,0:T(8,128)} %copy-done.2) | copy-start | bytes 3145732
  78.3 13.9 %copy-start.1 = (f32[1,64,1024]{2,1,0:T(8,128)S(1)}, f32[1,64,1024]{2,1,0:T(8,128)}, u32[]{:S(2)}) copy-start(f32[1,64,1024]{2,1,0:T(8,128)} %param.10) | copy-start | bytes 786436
  78.3 13.9 %copy-start.4 = (bf16[1,64,1024]{2,1,0:T(8,128)(2,1)S(1)}, bf16[1,64,1024]{2,1,0:T(8,128)(2,1)}, u32[]{:S(2)}) copy-start(bf16[1,64,1024]{2,1,0:T(8,128)(2,1)} %param.8) | copy-start | bytes 393220
  92.4 9.3 %collective-permute-start.1 = (bf16[64,1024]{1,0:T(8,128)(2,1)S(1)}, bf16[64,1024]{1,0:T(8,128)(2,1)S(1)}, u32[]{:S(2)}, u32[]{:S(2)}) collective-permute-start(bf16[64,1024]{1,0:T(8,128)(2,1)S(1)} %get-tuple-element.12), channel_id=1, source_target_pairs={{0,1},{1,2},{2,3},{3,4},{4,5},{5,6},{6,7},{7,8},{8,9},{9,10},{10,1... | collective-permute-start | bytes 393224 | tf_op jit(solution)/shard_map/ppermute | solution.py:272
  99.7 4.4 %collective-permute-start.2 = (bf16[64,1024]{1,0:T(8,128)(2,1)S(1)}, bf16[64,1024]{1,0:T(8,128)(2,1)S(1)}, u32[]{:S(2)}, u32[]{:S(2)}) collective-permute-start(bf16[64,1024]{1,0:T(8,128)(2,1)S(1)} %get-tuple-element.13), channel_id=1, source_target_pairs={{1,0},{2,1},{3,2},{4,3},{5,4},{6,5},{7,6},{8,7},{9,8},{10,9},{11,1... | collective-permute-start | bytes 393224 | tf_op jit(solution)/shard_map/ppermute | solution.py:273
Sparse Core Ops, SparseCore 0:
  19.7 50.1 all-gather.2

commit v5 on v4

--- a/solution.py
+++ b/solution.py
@@ -33,15 +33,15 @@
     one = causal & (apart < 64)
     two = causal & (apart < 128) & ((apart & 1) == 0)
     three = causal & (apart < 256) & ((apart & 3) == 0)
+    all_three = jnp.where(one, math.log(3.0), math.log(2.0))
+    one_more = jnp.where(one, math.log(2.0), 0.0)
+    no_more = jnp.where(one, 0.0, NEG)
     biases = []
     for head in range(HEADS):
-        count = one.astype(jnp.int32)
-        count = count + (two & ((t & 1) == head % 2)).astype(jnp.int32)
-        count = count + (three & ((t & 3) == head)).astype(jnp.int32)
-        bias = jnp.where(count == 1, 0.0, NEG)
-        bias = jnp.where(count == 2, math.log(2.0), bias)
-        bias = jnp.where(count == 3, math.log(3.0), bias)
-        biases.append(bias)
+        second = two & ((t & 1) == head % 2)
+        third = three & ((t & 3) == head)
+        bias = jnp.where(third, one_more, no_more)
+        biases.append(jnp.where(second, jnp.where(third, all_three, one_more), bias))
     return biases
 
 
@@ -96,7 +96,7 @@
         out[...] = total.astype(BF16)
 
 
-def prepare(tok_ref, gain_ref, normed_ref, inv_ref, bias_ref):
+def prepare(tok_ref, gain_ref, normed_ref, inv_ref):
     for which in range(2):
         for part in range(GROUP):
             xf = tok_ref[part, which].astype(F32)
@@ -105,8 +105,6 @@
             normed_ref[which, rows, :] = (xf * inv * gain_ref[...]).astype(BF16)
             if which == 1:
                 inv_ref[rows, :] = jnp.broadcast_to(inv, (64, 128))
-    for head, bias in enumerate(pair_bias(GROUP * 64)):
-        bias_ref[head] = bias
 
 
 def deliver(next_ref, prev_ref, next_out, prev_out):
@@ -114,28 +112,22 @@
     prev_out[...] = prev_ref[...].astype(F32)
 
 
-def layer(tok_ref, normed_ref, inv_ref, bias_ref, gain_ref, w_hbm, out_ref, w_ref, sems):
+def layer(tok_ref, normed_ref, inv_ref, gain_ref, w_ref, out_ref, bias_ref):
     rows = GROUP * 64
-    copies = []
-    for i in range(4):
-        copies.append(pltpu.make_async_copy(w_hbm.at[:, :, i], w_ref.at[i], sems.at[i]))
-        copies[-1].start()
+    for head, bias in enumerate(pair_bias(rows)):
+        bias_ref[head] = bias
     heads = head_masks(rows)
     scale = jnp.asarray(HEAD**-0.5, BF16)
 
     def weight(i):
-        return w_ref[i].reshape(1024, 256)
+        return w_ref[:, :, i].reshape(1024, 256)
 
     def out_weight(c):
-        return w_ref[3, :, c].reshape(256, 256)
+        return w_ref[:, c, 3].reshape(256, 256)
 
     def projected(which):
-        results = []
-        for i in range(3):
-            if which == 0:
-                copies[i].wait()
-            results.append(mm(normed_ref[which], weight(i), NN).astype(BF16))
-        q, k, v = results
+        normed = normed_ref[which]
+        q, k, v = [mm(normed, weight(i), NN).astype(BF16) for i in range(3)]
         return q * scale, k, v
 
     def prob_of(q_head, k, head):
@@ -150,7 +142,6 @@
         p = prob_of(only(heads[head], q), k, head).astype(BF16)
         attended = attended + mm(p, only(heads[head], v), NN)
     attended = attended.astype(BF16)
-    copies[3].wait()
     for c in range(4):
         part = mm(attended, out_weight(c), NN).astype(BF16)
         for to in range(GROUP):
@@ -225,6 +216,7 @@
         scratch=(pltpu.SemaphoreType.DMA((GROUP, 3)),),
         mib=63,
     )
+    qkv, own = lax.optimization_barrier((qkv, own))
     qkv = lax.all_to_all(qkv, "seq", 0, 0, axis_index_groups=row_groups, tiled=True)
     joined, = call(join_weights, [((GROUP, 4, 32, 256), BF16)], (qkv, own), "join_weights")
     weights = lax.all_gather(joined, "seq", axis_index_groups=columns)
@@ -243,22 +235,18 @@
         mib=63,
     )
     tokens = lax.all_to_all(tokens, "seq", 0, 0, axis_index_groups=row_groups, tiled=True)
-    normed, inv, bias = call(
+    normed, inv = call(
         prepare,
-        [((2, 256, 1024), BF16), ((256, 128), F32), ((HEADS, 256, 256), F32)],
+        [((2, 256, 1024), BF16), ((256, 128), F32)],
         (tokens, norm_gain),
         "prepare",
     )
     parts, = call(
         layer,
         [((GROUP, 2, 64, 1024), BF16)],
-        (tokens, normed, inv, bias, norm_gain, weights),
+        (tokens, normed, inv, norm_gain, weights),
         "layer",
-        in_specs=[VMEM] * 5 + [HBM],
-        scratch=(
-            pltpu.VMEM((4, deep, GROUP, 32, 256), BF16),
-            pltpu.SemaphoreType.DMA((4,)),
-        ),
+        scratch=(pltpu.VMEM((HEADS, 256, 256), F32),),
         flops=15 * 10**8,
     )
     parts = lax.all_to_all(parts, "seq", 0, 0, axis_index_groups=row_groups, tiled=True)

time: 112 us -> 113 us (level)
  blocking collectives: 37.9 us -> 53.3 us
  waiting for transfers between devices: 29.9 us -> 23.1 us
  starting transfers between devices: 13.7 us -> 8.84 us
  local copies, waits for them, and re-layouts: 3.79 us -> 1.61 us
    all_to_all x0 -> x1, blocking collectives: none -> 18.4 us  [per_device(): lax.all_to_all(qkv, 'seq', 0, 0, axis_index_groups=row_groups, tiled=True)]
    all_to_all x1 -> x0, starting transfers between devices: 4.85 us -> none  [per_device(): lax.all_to_all(qkv, 'seq', 0, 0, axis_index_groups=row_groups, tiled=True)]
    all_to_all x1 -> x0, waiting for transfers between devices: 3.68 us -> none  [per_device(): lax.all_to_all(qkv, 'seq', 0, 0, axis_index_groups=row_groups, tiled=True)]
    all_gather x1, waiting for transfers between devices: 21.8 us -> 18.7 us  [per_device(): weights = lax.all_gather(joined, 'seq', axis_index_groups=columns)]
    all_to_all x1, blocking collectives: 24 us -> 21 us  [per_device(): lax.all_to_all(tokens, 'seq', 0, 0, axis_index_groups=row_groups, tiled=T...]
    unnamed x12 -> x8, local copies, waits for them, and re-layouts: 3.79 us -> 1.61 us
  transfers between devices with their start and end apart: 5 -> 4, of which waited for: 4 -> 3; matrix products, arithmetic and copies ran while one was open for 0% -> 0% of each run, Pallas kernels for 3% -> 4%
where the time goes in v5:
time: 113 us; the launch traced here: 112 us
  blocking collectives  53.3 us (47%)
  waiting for transfers between devices  23.1 us (20%)
  between operations  14.1 us (12%)
  Pallas kernels  11.3 us (10%)
  starting transfers between devices  8.84 us (8%)
  local copies, waits for them, and re-layouts  1.61 us (1%)
    all_to_all x1, blocking collectives, per_device(): lax.all_to_all(tokens, 'seq', 0, 0, axis_index_groups=row_groups, tiled=T...  21 us
    all_gather x1, waiting for transfers between devices, per_device(): weights = lax.all_gather(joined, 'seq', axis_index_groups=columns)  18.7 us
    all_to_all x1, blocking collectives, per_device(): lax.all_to_all(qkv, 'seq', 0, 0, axis_index_groups=row_groups, tiled=True)  18.4 us
    all_to_all x1, blocking collectives, per_device(): lax.all_to_all(parts, 'seq', 0, 0, axis_index_groups=row_groups, tiled=True)  13.9 us
    pallas_call x7, Pallas kernels, call(): pl.pallas_call(body, out_shape=[jax.ShapeDtypeStruct(shape, kind) for sha...  11.3 us
    ppermute x1, starting transfers between devices, per_device(): next_input = lax.ppermute(layer_out, 'section', ring)  7.3 us
    ppermute x1, waiting for transfers between devices, per_device(): prev_grad = lax.ppermute(input_grad, 'section', [(b, a) for a, b in ring])  2.44 us
  transfers between devices with their start and end apart: 4, of which 3 were waited for; matrix products, arithmetic and copies ran while one was open for 0% of the time, Pallas kernels for 4%

profile of v5, /device:TPU:1, one launch (start us, length us, event | category | flops | bytes accessed | tf_op | source)
XLA Modules:
  0.0 112.3 jit_solution(2782920903837812310)
XLA Ops:
  7.2 0.0 all-gather.3.cloned.1.call-start
  7.2 1.5 %collective-permute-start = (bf16[32,1024]{1,0:T(8,128)(2,1)}, bf16[32,1024]{1,0:T(8,128)(2,1)S(1)}, u32[]{:S(2)}, u32[]{:S(2)}) collective-permute-start(bf16[32,1024]{1,0:T(8,128)(2,1)} %bitcast.21), channel_id=1, source_target_pairs={{0,0},{16,64},{32,128},{48,192},{64,256},{80,320},{96,384},{112,44... | collective-permute-start | bytes 196616 | tf_op jit(solution)/shard_map/ppermute | solution.py:209
  8.7 1.7 %pack_weights.1 = bf16[4,3,32,256]{3,2,1,0:T(8,128)(2,1)} custom-call(bf16[32,1024]{1,0:T(8,128)(2,1)} %bitcast.16, bf16[32,1024]{1,0:T(8,128)(2,1)} %bitcast.17, bf16[32,1024]{1,0:T(8,128)(2,1)} %bitcast.18), custom_call_target="tpu_custom_call" | custom-call | flops 1000000 | bytes 1000000 | tf_op jit(solution)/shard_map/pack_weights/pallas_call | solution.py:189
  10.4 0.0 collective-permute-done.own_ref
  10.4 18.4 %all_to_all.15.qkv_ref = bf16[4,3,32,256]{3,2,1,0:T(8,128)(2,1)S(1)} all-to-all(bf16[4,3,32,256]{3,2,1,0:T(8,128)(2,1)} %pack_weights.1), channel_id=1, replica_groups={{0,16,32,48},{64,80,96,112},{128,144,160,176},{192,208,224,240},{256,27..., dimensions={0} | all-to-all | bytes 393216 | tf_op jit(solution)/shard_map/all_to_all | solution.py:220
  28.8 0.7 join_weights.1.after_hbm
  29.5 0.0 all-gather.3.cloned.1.call-update
  29.5 2.6 %pack_tokens.1 = bf16[4,3,64,1024]{3,2,1,0:T(8,128)(2,1)} custom-call(bf16[4,4,32,256]{3,2,1,0:T(8,128)(2,1)} %join_weights.1.after_hbm, bf16[64,1024]{1,0:T(8,128)(2,1)} %bitcast.13, bf16[64,1024]{1,0:T(8,128)(2,1)} %bitcast.15, f32[64,1024]{1,0:T(8,128)} %bitcast.11), custom_call_target="tpu_custom_call" | custom-call | flops 1000000 | bytes 1000000 | tf_op jit(solution)/shard_map/pack_tokens/pallas_call | solution.py:189
  32.1 0.0 copy-start.3
  32.1 21.0 %all_to_all.16.tok_ref = bf16[4,3,64,1024]{3,2,1,0:T(8,128)(2,1)S(1)} all-to-all(bf16[4,3,64,1024]{3,2,1,0:T(8,128)(2,1)} %pack_tokens.1), channel_id=1, replica_groups={{0,16,32,48},{64,80,96,112},{128,144,160,176},{192,208,224,240},{256,27..., dimensions={0} | all-to-all | bytes 3145728 | tf_op jit(solution)/shard_map/all_to_all | solution.py:237
  53.2 0.0 copy-done.3
  53.2 0.4 prepare.1
  53.6 18.7 %all-gather.3.cloned.1.call-done = bf16[32,4,32,256]{3,2,1,0:T(8,128)(2,1)} async-done(((bf16[4,4,32,256]{3,2,1,0:T(8,128)(2,1)}), bf16[32,4,32,256]{3,2,1,0:T(8,128)(2,1)}) %all-gather.3.cloned.1.call-update) | async-done | bytes 2097168 | tf_op jit(solution)/shard_map/all_gather | solution.py:222
  72.3 1.6 %copy-done = bf16[32,4,32,256]{3,2,1,0:T(8,128)(2,1)S(1)} copy-done((bf16[32,4,32,256]{3,2,1,0:T(8,128)(2,1)S(1)}, bf16[32,4,32,256]{3,2,1,0:T(8,128)(2,1)}, u32[]{:S(2)}) %copy-start) | copy-done | bytes 2097176
  73.9 5.0 %layer.1 = bf16[4,2,64,1024]{3,2,1,0:T(8,128)(2,1)S(1)} custom-call(bf16[4,3,64,1024]{3,2,1,0:T(8,128)(2,1)S(1)} %all_to_all.16.tok_ref, bf16[2,256,1024]{2,1,0:T(8,128)(2,1)S(1)} %get-tuple-element.12.normed_ref, f32[256,128]{1,0:T(8,128)S(1)} %get-tuple-element.13.inv_ref, f32[1,1024]{1,0:T(1,128)S(1)} %copy-done.3, bf16[8,4,4,32,256]{4,3,2,1,0:T(8,128)(2,1)S(1)} %bitcast.10), custom_call_target="tpu_custom_call" | custom-call | flops 1500000000 | bytes 1000000 | tf_op jit(solution)/shard_map/layer/pallas_call | solution.py:189
  78.9 0.0 copy-start.1
  78.9 0.0 copy-start.2
  78.9 13.9 %all_to_all.17.parts_ref = bf16[4,2,64,1024]{3,2,1,0:T(8,128)(2,1)S(1)} all-to-all(bf16[4,2,64,1024]{3,2,1,0:T(8,128)(2,1)S(1)} %layer.1), channel_id=1, replica_groups={{0,16,32,48},{64,80,96,112},{128,144,160,176},{192,208,224,240},{256,27..., dimensions={0} | all-to-all | bytes 2097152 | tf_op jit(solution)/shard_map/all_to_all | solution.py:252
  92.9 0.2 finish.1
  93.0 7.3 %collective-permute-start.1 = (bf16[64,1024]{1,0:T(8,128)(2,1)S(1)}, bf16[64,1024]{1,0:T(8,128)(2,1)S(1)}, u32[]{:S(2)}, u32[]{:S(2)}) collective-permute-start(bf16[64,1024]{1,0:T(8,128)(2,1)S(1)} %get-tuple-element.14), channel_id=1, source_target_pairs={{0,1},{1,2},{2,3},{3,4},{4,5},{5,6},{6,7},{7,8},{8,9},{9,10},{10,1... | collective-permute-start | bytes 393224 | tf_op jit(solution)/shard_map/ppermute | solution.py:260
  100.3 0.0 collective-permute-start.2
  100.3 1.9 %collective-permute-done.1.next_ref = bf16[64,1024]{1,0:T(8,128)(2,1)S(1)} collective-permute-done((bf16[64,1024]{1,0:T(8,128)(2,1)S(1)}, bf16[64,1024]{1,0:T(8,128)(2,1)S(1)}, u32[]{:S(2)}, u32[]{:S(2)}) %collective-permute-start.1) | collective-permute-done | bytes 131104 | tf_op jit(solution)/shard_map/ppermute | solution.py:260
  102.3 2.4 %collective-permute-done.2.prev_ref = bf16[64,1024]{1,0:T(8,128)(2,1)S(1)} collective-permute-done((bf16[64,1024]{1,0:T(8,128)(2,1)S(1)}, bf16[64,1024]{1,0:T(8,128)(2,1)S(1)}, u32[]{:S(2)}, u32[]{:S(2)}) %collective-permute-start.2) | collective-permute-done | bytes 131104 | tf_op jit(solution)/shard_map/ppermute | solution.py:261
  104.7 0.8 deliver.1
  (3 shorter events, 0.0 us)
Async XLA Ops:
  7.2 65.1 %all-gather.3.cloned.1.call-start = ((), (), s32[]{:S(2)}) async-start(), calls=%async_computation.3 | async-start | bytes 2359296 | tf_op jit(solution)/shard_map/all_gather | solution.py:222
  7.2 3.2 %collective-permute-start = (bf16[32,1024]{1,0:T(8,128)(2,1)}, bf16[32,1024]{1,0:T(8,128)(2,1)S(1)}, u32[]{:S(2)}, u32[]{:S(2)}) collective-permute-start(bf16[32,1024]{1,0:T(8,128)(2,1)} %bitcast.21), channel_id=1, source_target_pairs={{0,0},{16,64},{32,128},{48,192},{64,256},{80,320},{96,384},{112,44... | collective-permute-start | bytes 196616 | tf_op jit(solution)/shard_map/ppermute | solution.py:209
  32.1 21.0 %copy-start.3 = (f32[1,1024]{1,0:T(1,128)S(1)}, f32[1,1024]{1,0:T(1,128)}, u32[]{:S(2)}) copy-start(f32[1,1024]{1,0:T(1,128)} %gain_ref.3) | copy-start | bytes 12292
  72.3 1.6 %copy-start = (bf16[32,4,32,256]{3,2,1,0:T(8,128)(2,1)S(1)}, bf16[32,4,32,256]{3,2,1,0:T(8,128)(2,1)}, u32[]{:S(2)}) copy-start(bf16[32,4,32,256]{3,2,1,0:T(8,128)(2,1)} %all-gather.3.cloned.1.call-done) | copy-start | bytes 6291460
  78.9 13.9 %copy-start.1 = (f32[1,64,1024]{2,1,0:T(8,128)S(1)}, f32[1,64,1024]{2,1,0:T(8,128)}, u32[]{:S(2)}) copy-start(f32[1,64,1024]{2,1,0:T(8,128)} %param.10) | copy-start | bytes 786436
  78.9 13.9 %copy-start.2 = (bf16[1,64,1024]{2,1,0:T(8,128)(2,1)S(1)}, bf16[1,64,1024]{2,1,0:T(8,128)(2,1)}, u32[]{:S(2)}) copy-start(bf16[1,64,1024]{2,1,0:T(8,128)(2,1)} %param.8) | copy-start | bytes 393220
  93.0 9.3 %collective-permute-start.1 = (bf16[64,1024]{1,0:T(8,128)(2,1)S(1)}, bf16[64,1024]{1,0:T(8,128)(2,1)S(1)}, u32[]{:S(2)}, u32[]{:S(2)}) collective-permute-start(bf16[64,1024]{1,0:T(8,128)(2,1)S(1)} %get-tuple-element.14), channel_id=1, source_target_pairs={{0,1},{1,2},{2,3},{3,4},{4,5},{5,6},{6,7},{7,8},{8,9},{9,10},{10,1... | collective-permute-start | bytes 393224 | tf_op jit(solution)/shard_map/ppermute | solution.py:260
  100.3 4.4 %collective-permute-start.2 = (bf16[64,1024]{1,0:T(8,128)(2,1)S(1)}, bf16[64,1024]{1,0:T(8,128)(2,1)S(1)}, u32[]{:S(2)}, u32[]{:S(2)}) collective-permute-start(bf16[64,1024]{1,0:T(8,128)(2,1)S(1)} %get-tuple-element.15), channel_id=1, source_target_pairs={{1,0},{2,1},{3,2},{4,3},{5,4},{6,5},{7,6},{8,7},{9,8},{10,9},{11,1... | collective-permute-start | bytes 393224 | tf_op jit(solution)/shard_map/ppermute | solution.py:261
Sparse Core Ops, SparseCore 0:
  29.6 42.6 all-gather.2

commit v6 on v5

--- a/solution.py
+++ b/solution.py
@@ -54,22 +54,25 @@
     return jnp.where(mask, value, jnp.zeros((), value.dtype))
 
 
-def pack_weights(q_hbm, k_hbm, v_hbm, out_ref, sems):
+def pack_weights(me_ref, q_hbm, k_hbm, v_hbm, out_ref, self_ref, sems):
+    mine = pl.ds(pl.multiple_of(me_ref[0] * 256, 256), 256)
     copies = []
-    for block in range(GROUP):
-        columns = slice(256 * block, 256 * block + 256)
-        for i, ref in enumerate((q_hbm, k_hbm, v_hbm)):
-            source, target = ref.at[:, columns], out_ref.at[block, i]
+    for i, ref in enumerate((q_hbm, k_hbm, v_hbm)):
+        copies.append(pltpu.make_async_copy(ref.at[:, mine], self_ref.at[i], sems.at[GROUP, i]))
+        for block in range(GROUP):
+            source, target = ref.at[:, 256 * block : 256 * block + 256], out_ref.at[block, i]
             copies.append(pltpu.make_async_copy(source, target, sems.at[block, i]))
-            copies[-1].start()
+    for copy in copies:
+        copy.start()
     for copy in copies:
         copy.wait()
 
 
-def join_weights(qkv_ref, own_ref, out_ref):
+def join_weights(me_ref, qkv_ref, own_ref, out_ref):
+    for k in range(1, GROUP):
+        out_ref[3 * k - 3 : 3 * k] = qkv_ref[(me_ref[0] + k) % GROUP]
     for block in range(GROUP):
-        out_ref[block, :3] = qkv_ref[block]
-        out_ref[block, 3] = own_ref[:, 256 * block : 256 * block + 256]
+        out_ref[9 + block] = own_ref[:, 256 * block : 256 * block + 256]
 
 
 def pack_tokens(after_hbm, fwd_hbm, bwd_hbm, grad_hbm, out_ref, grad_ref, sems, grad_sem):
@@ -112,18 +115,23 @@
     prev_out[...] = prev_ref[...].astype(F32)
 
 
-def layer(tok_ref, normed_ref, inv_ref, gain_ref, w_ref, out_ref, bias_ref):
+def layer(me_ref, tok_ref, normed_ref, inv_ref, gain_ref, self_ref, rest_ref, *refs):
+    out_ref, bias_ref, w_ref = refs
     rows = GROUP * 64
+    for i in range(3):
+        w_ref[i, :, me_ref[0]] = self_ref[:, i]
+        for k in range(1, GROUP):
+            w_ref[i, :, (me_ref[0] + k) % GROUP] = rest_ref[:, 3 * k - 3 + i]
     for head, bias in enumerate(pair_bias(rows)):
         bias_ref[head] = bias
     heads = head_masks(rows)
     scale = jnp.asarray(HEAD**-0.5, BF16)
 
     def weight(i):
-        return w_ref[:, :, i].reshape(1024, 256)
+        return w_ref[i].reshape(1024, 256)
 
     def out_weight(c):
-        return w_ref[:, c, 3].reshape(256, 256)
+        return rest_ref[:, 9 + c].reshape(256, 256)
 
     def projected(which):
         normed = normed_ref[which]
@@ -205,21 +213,29 @@
     row_groups = [[GROUP * y + x for x in range(GROUP)] for y in range(deep)]
     columns = [[GROUP * y + x for y in range(deep)] for x in range(GROUP)]
 
+    me = (lax.axis_index("seq") % GROUP).reshape(1)
+
+    qkv, self_part = call(
+        pack_weights,
+        [((GROUP, 3, 32, 256), BF16), ((3, 32, 256), BF16)],
+        (me, w_query[0], w_key[0], w_value[0]),
+        "pack_weights",
+        in_specs=[SMEM] + [HBM] * 3,
+        scratch=(pltpu.SemaphoreType.DMA((GROUP + 1, 3)),),
+        mib=63,
+    )
+    self_part = lax.all_gather(self_part, "seq", axis_index_groups=columns)
     places = [(s, GROUP * (s % deep) + s // deep) for s in range(seqs)]
     own = lax.ppermute(w_out[0], "seq", places)
-    qkv, = call(
-        pack_weights,
-        [((GROUP, 3, 32, 256), BF16)],
-        (w_query[0], w_key[0], w_value[0]),
-        "pack_weights",
-        in_specs=[HBM] * 3,
-        scratch=(pltpu.SemaphoreType.DMA((GROUP, 3)),),
-        mib=63,
-    )
-    qkv, own = lax.optimization_barrier((qkv, own))
     qkv = lax.all_to_all(qkv, "seq", 0, 0, axis_index_groups=row_groups, tiled=True)
-    joined, = call(join_weights, [((GROUP, 4, 32, 256), BF16)], (qkv, own), "join_weights")
-    weights = lax.all_gather(joined, "seq", axis_index_groups=columns)
+    joined, = call(
+        join_weights,
+        [((13, 32, 256), BF16)],
+        (me, qkv, own),
+        "join_weights",
+        in_specs=[SMEM, VMEM, VMEM],
+    )
+    rest = lax.all_gather(joined, "seq", axis_index_groups=columns)
 
     tokens, = call(
         pack_tokens,
@@ -244,9 +260,13 @@
     parts, = call(
         layer,
         [((GROUP, 2, 64, 1024), BF16)],
-        (tokens, normed, inv, norm_gain, weights),
+        (me, tokens, normed, inv, norm_gain, self_part, rest),
         "layer",
-        scratch=(pltpu.VMEM((HEADS, 256, 256), F32),),
+        in_specs=[SMEM] + [VMEM] * 6,
+        scratch=(
+            pltpu.VMEM((HEADS, 256, 256), F32),
+            pltpu.VMEM((3, deep, GROUP, 32, 256), BF16),
+        ),
         flops=15 * 10**8,
     )
     parts = lax.all_to_all(parts, "seq", 0, 0, axis_index_groups=row_groups, tiled=True)

time: 113 us -> 110 us (0.973)
  blocking collectives: 53.3 us -> 34.8 us
  starting transfers between devices: 8.84 us -> 23.4 us
    all_to_all x2 -> x0, blocking collectives: 39.4 us -> none  [the longest x1 21 us: per_device(): lax.all_to_all(tokens, 'seq', 0, 0, axis_index_groups=row_groups, tiled=T...]
    all_gather x0 -> x1, blocking collectives: none -> 20.1 us  [per_device(): self_part = lax.all_gather(self_part, 'seq', axis_index_groups=columns)]
    all_to_all x0 -> x2, starting transfers between devices: none -> 15.6 us  [the longest x1 10.7 us: per_device(): lax.all_to_all(tokens, 'seq', 0, 0, axis_index_groups=row_groups, tiled=T...]
    all_to_all x0 -> x2, waiting for transfers between devices: none -> 3.69 us  [the longest x1 3.68 us: per_device(): lax.all_to_all(qkv, 'seq', 0, 0, axis_index_groups=row_groups, tiled=True)]
    all_gather x1, waiting for transfers between devices: 18.7 us -> 16 us  [per_device(): rest = lax.all_gather(joined, 'seq', axis_index_groups=columns)]
  transfers between devices with their start and end apart: 4 -> 6, of which waited for: 3 -> 4; matrix products, arithmetic and copies ran while one was open for 0% -> 0% of each run, Pallas kernels for 4% -> 3%
where the time goes in v6:
time: 110 us; the launch traced here: 109 us
  blocking collectives  34.8 us (32%)
  waiting for transfers between devices  24.1 us (22%)
  starting transfers between devices  23.4 us (21%)
  between operations  14.1 us (13%)
  Pallas kernels  11.5 us (10%)
  local copies, waits for them, and re-layouts  1.48 us (1%)
    all_gather x1, blocking collectives, per_device(): self_part = lax.all_gather(self_part, 'seq', axis_index_groups=columns)  20.1 us
    all_gather x1, waiting for transfers between devices, per_device(): rest = lax.all_gather(joined, 'seq', axis_index_groups=columns)  16 us
    all_to_all x1, blocking collectives, per_device(): lax.all_to_all(parts, 'seq', 0, 0, axis_index_groups=row_groups, tiled=True)  14.7 us
    pallas_call x7, Pallas kernels, call(): pl.pallas_call(body, out_shape=[jax.ShapeDtypeStruct(shape, kind) for sha...  11.5 us
    all_to_all x1, starting transfers between devices, per_device(): lax.all_to_all(tokens, 'seq', 0, 0, axis_index_groups=row_groups, tiled=T...  10.7 us
    ppermute x1, starting transfers between devices, per_device(): next_input = lax.ppermute(layer_out, 'section', ring)  6.34 us
    all_to_all x1, starting transfers between devices, per_device(): lax.all_to_all(qkv, 'seq', 0, 0, axis_index_groups=row_groups, tiled=True)  4.83 us
    all_to_all x1, waiting for transfers between devices, per_device(): lax.all_to_all(qkv, 'seq', 0, 0, axis_index_groups=row_groups, tiled=True)  3.68 us
  transfers between devices with their start and end apart: 6, of which 4 were waited for; matrix products, arithmetic and copies ran while one was open for 0% of the time, Pallas kernels for 3%

profile of v6, /device:TPU:1, one launch (start us, length us, event | category | flops | bytes accessed | tf_op | source)
XLA Modules:
  0.0 109.4 jit_solution(12332367419668910314)
XLA Ops:
  7.2 1.7 %pack_weights.1 = (bf16[4,3,32,256]{3,2,1,0:T(8,128)(2,1)}, bf16[3,32,256]{2,1,0:T(8,128)(2,1)}) custom-call(s32[1]{0:T(128)} %bitcast.me_ref, bf16[32,1024]{1,0:T(8,128)(2,1)} %bitcast.19, bf16[32,1024]{1,0:T(8,128)(2,1)} %bitcast.20, bf16[32,1024]{1,0:T(8,128)(2,1)} %bitcast.21), custom_call_target="tpu_custom_call" | custom-call | flops 1000000 | bytes 1000000 | tf_op jit(solution)/shard_map/pack_weights/pallas_call | solution.py:197
  8.9 4.8 %all-to-all-start = ((bf16[4,3,32,256]{3,2,1,0:T(8,128)(2,1)}), bf16[4,3,32,256]{3,2,1,0:T(8,128)(2,1)S(1)}, u32[]{:S(2)}, u32[]{:S(2)}) async-start(bf16[4,3,32,256]{3,2,1,0:T(8,128)(2,1)} %get-tuple-element.10), calls=%async_computation | async-start | bytes 393216 | tf_op jit(solution)/shard_map/all_to_all | solution.py:230
  13.8 1.5 %collective-permute-start = (bf16[32,1024]{1,0:T(8,128)(2,1)}, bf16[32,1024]{1,0:T(8,128)(2,1)S(1)}, u32[]{:S(2)}, u32[]{:S(2)}) collective-permute-start(bf16[32,1024]{1,0:T(8,128)(2,1)} %bitcast.24), channel_id=1, source_target_pairs={{0,0},{16,64},{32,128},{48,192},{64,256},{80,320},{96,384},{112,44... | collective-permute-start | bytes 196616 | tf_op jit(solution)/shard_map/ppermute | solution.py:229
  15.2 3.7 %all-to-all-done.qkv_ref = bf16[4,3,32,256]{3,2,1,0:T(8,128)(2,1)S(1)} async-done(((bf16[4,3,32,256]{3,2,1,0:T(8,128)(2,1)}), bf16[4,3,32,256]{3,2,1,0:T(8,128)(2,1)S(1)}, u32[]{:S(2)}, u32[]{:S(2)}) %all-to-all-start) | async-done | bytes 196640 | tf_op jit(solution)/shard_map/all_to_all | solution.py:230
  18.9 0.7 join_weights.1.after_hbm
  19.6 0.0 all-gather.4.cloned.1.call-update
  19.6 2.6 %pack_tokens.1 = bf16[4,3,64,1024]{3,2,1,0:T(8,128)(2,1)} custom-call(bf16[13,32,256]{2,1,0:T(8,128)(2,1)} %join_weights.1.after_hbm, bf16[64,1024]{1,0:T(8,128)(2,1)} %bitcast.16, bf16[64,1024]{1,0:T(8,128)(2,1)} %bitcast.18, f32[64,1024]{1,0:T(8,128)} %bitcast.14), custom_call_target="tpu_custom_call" | custom-call | flops 1000000 | bytes 1000000 | tf_op jit(solution)/shard_map/pack_tokens/pallas_call | solution.py:197
  22.3 0.0 copy-start.4
  22.3 0.0 copy-start.3
  22.3 10.7 %all-to-all-start.1 = ((bf16[4,3,64,1024]{3,2,1,0:T(8,128)(2,1)}), bf16[4,3,64,1024]{3,2,1,0:T(8,128)(2,1)S(1)}, u32[]{:S(2)}, u32[]{:S(2)}) async-start(bf16[4,3,64,1024]{3,2,1,0:T(8,128)(2,1)} %pack_tokens.1), calls=%async_computation.1 | async-start | bytes 3145728 | tf_op jit(solution)/shard_map/all_to_all | solution.py:253
  33.0 20.1 %all-gather = bf16[24,32,256]{2,1,0:T(8,128)(2,1)S(1)} all-gather(bf16[3,32,256]{2,1,0:T(8,128)(2,1)S(1)} %copy-done.4), channel_id=2, replica_groups={{0,64,128,192,256,320,384,448},{16,80,144,208,272,336,400,464},{32,96,1..., dimensions={0}, use_global_device_ids=true | all-gather | bytes 442368 | tf_op jit(solution)/shard_map/all_gather | solution.py:227
  53.1 0.4 prepare.1
  53.5 16.0 %all-gather.4.cloned.1.call-done = bf16[104,32,256]{2,1,0:T(8,128)(2,1)} async-done(((bf16[13,32,256]{2,1,0:T(8,128)(2,1)}), bf16[104,32,256]{2,1,0:T(8,128)(2,1)}) %all-gather.4.cloned.1.call-update) | async-done | bytes 1703952 | tf_op jit(solution)/shard_map/all_gather | solution.py:238
  69.6 1.5 %copy-done = bf16[104,32,256]{2,1,0:T(8,128)(2,1)S(1)} copy-done((bf16[104,32,256]{2,1,0:T(8,128)(2,1)S(1)}, bf16[104,32,256]{2,1,0:T(8,128)(2,1)}, u32[]{:S(2)}) %copy-start) | copy-done | bytes 1703960
  71.0 5.2 %layer.1 = bf16[4,2,64,1024]{3,2,1,0:T(8,128)(2,1)S(1)} custom-call(s32[1]{0:T(128)} %bitcast.me_ref, bf16[4,3,64,1024]{3,2,1,0:T(8,128)(2,1)S(1)} %all-to-all-done.1.tok_ref, bf16[2,256,1024]{2,1,0:T(8,128)(2,1)S(1)} %get-tuple-element.11.normed_ref, f32[256,128]{1,0:T(8,128)S(1)} %get-tuple-element.12.inv_ref, f32[1,1024]{1,0:T(1,128)S(1)} %copy-done.3, ...), custom_call_target="tpu_custom_call" | custom-call | flops 1500000000 | bytes 1000000 | tf_op jit(solution)/shard_map/layer/pallas_call | solution.py:197
  76.2 0.0 copy-start.1
  76.2 0.0 copy-start.2
  76.2 14.7 %all_to_all.15.parts_ref = bf16[4,2,64,1024]{3,2,1,0:T(8,128)(2,1)S(1)} all-to-all(bf16[4,2,64,1024]{3,2,1,0:T(8,128)(2,1)S(1)} %layer.1), channel_id=1, replica_groups={{0,16,32,48},{64,80,96,112},{128,144,160,176},{192,208,224,240},{256,27..., dimensions={0} | all-to-all | bytes 2097152 | tf_op jit(solution)/shard_map/all_to_all | solution.py:272
  90.9 0.2 finish.1
  91.1 6.3 %collective-permute-start.1 = (bf16[64,1024]{1,0:T(8,128)(2,1)S(1)}, bf16[64,1024]{1,0:T(8,128)(2,1)S(1)}, u32[]{:S(2)}, u32[]{:S(2)}) collective-permute-start(bf16[64,1024]{1,0:T(8,128)(2,1)S(1)} %get-tuple-element.14), channel_id=1, source_target_pairs={{0,1},{1,2},{2,3},{3,4},{4,5},{5,6},{6,7},{7,8},{8,9},{9,10},{10,1... | collective-permute-start | bytes 393224 | tf_op jit(solution)/shard_map/ppermute | solution.py:280
  97.4 0.0 collective-permute-start.2
  97.4 1.9 %collective-permute-done.1.next_ref = bf16[64,1024]{1,0:T(8,128)(2,1)S(1)} collective-permute-done((bf16[64,1024]{1,0:T(8,128)(2,1)S(1)}, bf16[64,1024]{1,0:T(8,128)(2,1)S(1)}, u32[]{:S(2)}, u32[]{:S(2)}) %collective-permute-start.1) | collective-permute-done | bytes 131104 | tf_op jit(solution)/shard_map/ppermute | solution.py:280
  99.4 2.4 %collective-permute-done.2.prev_ref = bf16[64,1024]{1,0:T(8,128)(2,1)S(1)} collective-permute-done((bf16[64,1024]{1,0:T(8,128)(2,1)S(1)}, bf16[64,1024]{1,0:T(8,128)(2,1)S(1)}, u32[]{:S(2)}, u32[]{:S(2)}) %collective-permute-start.2) | collective-permute-done | bytes 131104 | tf_op jit(solution)/shard_map/ppermute | solution.py:281
  101.8 0.8 deliver.1
  (8 shorter events, 0.0 us)
Async XLA Ops:
  8.9 10.0 %all-to-all-start = ((bf16[4,3,32,256]{3,2,1,0:T(8,128)(2,1)}), bf16[4,3,32,256]{3,2,1,0:T(8,128)(2,1)S(1)}, u32[]{:S(2)}, u32[]{:S(2)}) async-start(bf16[4,3,32,256]{3,2,1,0:T(8,128)(2,1)} %get-tuple-element.10), calls=%async_computation | async-start | bytes 393216 | tf_op jit(solution)/shard_map/all_to_all | solution.py:230
  13.7 55.8 %all-gather.4.cloned.1.call-start = ((), (), s32[]{:S(2)}) async-start(), calls=%async_computation.3 | async-start | bytes 1916928 | tf_op jit(solution)/shard_map/all_gather | solution.py:238
  13.8 1.5 %collective-permute-start = (bf16[32,1024]{1,0:T(8,128)(2,1)}, bf16[32,1024]{1,0:T(8,128)(2,1)S(1)}, u32[]{:S(2)}, u32[]{:S(2)}) collective-permute-start(bf16[32,1024]{1,0:T(8,128)(2,1)} %bitcast.24), channel_id=1, source_target_pairs={{0,0},{16,64},{32,128},{48,192},{64,256},{80,320},{96,384},{112,44... | collective-permute-start | bytes 196616 | tf_op jit(solution)/shard_map/ppermute | solution.py:229
  22.3 10.8 %copy-start.4 = (bf16[3,32,256]{2,1,0:T(8,128)(2,1)S(1)}, bf16[3,32,256]{2,1,0:T(8,128)(2,1)}, u32[]{:S(2)}) copy-start(bf16[3,32,256]{2,1,0:T(8,128)(2,1)} %get-tuple-element.13) | copy-start | bytes 147460
  22.3 30.9 %copy-start.3 = (f32[1,1024]{1,0:T(1,128)S(1)}, f32[1,1024]{1,0:T(1,128)}, u32[]{:S(2)}) copy-start(f32[1,1024]{1,0:T(1,128)} %gain_ref.3) | copy-start | bytes 12292
  22.3 30.9 %all-to-all-start.1 = ((bf16[4,3,64,1024]{3,2,1,0:T(8,128)(2,1)}), bf16[4,3,64,1024]{3,2,1,0:T(8,128)(2,1)S(1)}, u32[]{:S(2)}, u32[]{:S(2)}) async-start(bf16[4,3,64,1024]{3,2,1,0:T(8,128)(2,1)} %pack_tokens.1), calls=%async_computation.1 | async-start | bytes 3145728 | tf_op jit(solution)/shard_map/all_to_all | solution.py:253
  69.6 1.5 %copy-start = (bf16[104,32,256]{2,1,0:T(8,128)(2,1)S(1)}, bf16[104,32,256]{2,1,0:T(8,128)(2,1)}, u32[]{:S(2)}) copy-start(bf16[104,32,256]{2,1,0:T(8,128)(2,1)} %all-gather.4.cloned.1.call-done) | copy-start | bytes 5111812
  76.2 14.7 %copy-start.1 = (f32[1,64,1024]{2,1,0:T(8,128)S(1)}, f32[1,64,1024]{2,1,0:T(8,128)}, u32[]{:S(2)}) copy-start(f32[1,64,1024]{2,1,0:T(8,128)} %param.10) | copy-start | bytes 786436
  76.2 14.7 %copy-start.2 = (bf16[1,64,1024]{2,1,0:T(8,128)(2,1)S(1)}, bf16[1,64,1024]{2,1,0:T(8,128)(2,1)}, u32[]{:S(2)}) copy-start(bf16[1,64,1024]{2,1,0:T(8,128)(2,1)} %param.8) | copy-start | bytes 393220
  91.1 8.3 %collective-permute-start.1 = (bf16[64,1024]{1,0:T(8,128)(2,1)S(1)}, bf16[64,1024]{1,0:T(8,128)(2,1)S(1)}, u32[]{:S(2)}, u32[]{:S(2)}) collective-permute-start(bf16[64,1024]{1,0:T(8,128)(2,1)S(1)} %get-tuple-element.14), channel_id=1, source_target_pairs={{0,1},{1,2},{2,3},{3,4},{4,5},{5,6},{6,7},{7,8},{8,9},{9,10},{10,1... | collective-permute-start | bytes 393224 | tf_op jit(solution)/shard_map/ppermute | solution.py:280
  97.4 4.4 %collective-permute-start.2 = (bf16[64,1024]{1,0:T(8,128)(2,1)S(1)}, bf16[64,1024]{1,0:T(8,128)(2,1)S(1)}, u32[]{:S(2)}, u32[]{:S(2)}) collective-permute-start(bf16[64,1024]{1,0:T(8,128)(2,1)S(1)} %get-tuple-element.15), channel_id=1, source_target_pairs={{1,0},{2,1},{3,2},{4,3},{5,4},{6,5},{7,6},{8,7},{9,8},{10,9},{11,1... | collective-permute-start | bytes 393224 | tf_op jit(solution)/shard_map/ppermute | solution.py:281
Sparse Core Ops, SparseCore 0:
  19.8 49.7 all-gather.3

commit v7 on v5

--- a/solution.py
+++ b/solution.py
@@ -66,12 +66,6 @@
         copy.wait()
 
 
-def join_weights(qkv_ref, own_ref, out_ref):
-    for block in range(GROUP):
-        out_ref[block, :3] = qkv_ref[block]
-        out_ref[block, 3] = own_ref[:, 256 * block : 256 * block + 256]
-
-
 def pack_tokens(after_hbm, fwd_hbm, bwd_hbm, grad_hbm, out_ref, grad_ref, sems, grad_sem):
     del after_hbm
     first = pltpu.make_async_copy(grad_hbm, grad_ref, grad_sem)
@@ -112,7 +106,7 @@
     prev_out[...] = prev_ref[...].astype(F32)
 
 
-def layer(tok_ref, normed_ref, inv_ref, gain_ref, w_ref, out_ref, bias_ref):
+def layer(tok_ref, normed_ref, inv_ref, gain_ref, w_ref, own_ref, out_ref, bias_ref):
     rows = GROUP * 64
     for head, bias in enumerate(pair_bias(rows)):
         bias_ref[head] = bias
@@ -123,7 +117,7 @@
         return w_ref[:, :, i].reshape(1024, 256)
 
     def out_weight(c):
-        return w_ref[:, c, 3].reshape(256, 256)
+        return own_ref[:, :, 256 * c : 256 * c + 256].reshape(256, 256)
 
     def projected(which):
         normed = normed_ref[which]
@@ -216,15 +210,13 @@
         scratch=(pltpu.SemaphoreType.DMA((GROUP, 3)),),
         mib=63,
     )
-    qkv, own = lax.optimization_barrier((qkv, own))
     qkv = lax.all_to_all(qkv, "seq", 0, 0, axis_index_groups=row_groups, tiled=True)
-    joined, = call(join_weights, [((GROUP, 4, 32, 256), BF16)], (qkv, own), "join_weights")
-    weights = lax.all_gather(joined, "seq", axis_index_groups=columns)
+    weights = lax.all_gather(qkv, "seq", axis_index_groups=columns)
 
     tokens, = call(
         pack_tokens,
         [((GROUP, 3, 64, 1024), BF16)],
-        (joined, fwd_input[0], bwd_input[0], bwd_grad[0]),
+        (qkv, fwd_input[0], bwd_input[0], bwd_grad[0]),
         "pack_tokens",
         in_specs=[HBM] * 4,
         scratch=(
@@ -234,6 +226,8 @@
         ),
         mib=63,
     )
+    own, tokens = lax.optimization_barrier((own, tokens))
+    own = lax.all_gather(own, "seq", axis_index_groups=columns)
     tokens = lax.all_to_all(tokens, "seq", 0, 0, axis_index_groups=row_groups, tiled=True)
     normed, inv = call(
         prepare,
@@ -244,7 +238,7 @@
     parts, = call(
         layer,
         [((GROUP, 2, 64, 1024), BF16)],
-        (tokens, normed, inv, norm_gain, weights),
+        (tokens, normed, inv, norm_gain, weights, own),
         "layer",
         scratch=(pltpu.VMEM((HEADS, 256, 256), F32),),
         flops=15 * 10**8,

time: 113 us -> 104 us (0.920)
  waiting for transfers between devices: 23.1 us -> 11 us
  starting transfers between devices: 8.84 us -> 18.2 us
  blocking collectives: 53.3 us -> 48.1 us
    all_gather x0 -> x1, blocking collectives: none -> 24 us  [per_device(): own = lax.all_gather(own, 'seq', axis_index_groups=columns)]
    all_to_all x1 -> x0, blocking collectives: 21 us -> none  [per_device(): lax.all_to_all(tokens, 'seq', 0, 0, axis_index_groups=row_groups, tiled=T...]
    all_gather x1, waiting for transfers between devices: 18.7 us -> 6.55 us  [per_device(): weights = lax.all_gather(qkv, 'seq', axis_index_groups=columns)]
    all_to_all x0 -> x1, starting transfers between devices: none -> 9.4 us  [per_device(): lax.all_to_all(tokens, 'seq', 0, 0, axis_index_groups=row_groups, tiled=T...]
    all_to_all x1, blocking collectives: 18.4 us -> 10.1 us  [per_device(): lax.all_to_all(qkv, 'seq', 0, 0, axis_index_groups=row_groups, tiled=True)]
    pallas_call x7 -> x6, Pallas kernels: 11.3 us -> 10.6 us  [call(): pl.pallas_call(body, out_shape=[jax.ShapeDtypeStruct(shape, kind) for sha...]
  transfers between devices with their start and end apart: 4 -> 5, of which waited for: 3 -> 3; matrix products, arithmetic and copies ran while one was open for 0% -> 0% of each run, Pallas kernels for 4% -> 3%
where the time goes in v7:
time: 104 us; the launch traced here: 103 us
  blocking collectives  48.1 us (46%)
  starting transfers between devices  18.2 us (18%)
  between operations  14.1 us (14%)
  waiting for transfers between devices  11 us (11%)
  Pallas kernels  10.6 us (10%)
  local copies, waits for them, and re-layouts  1.43 us (1%)
    all_gather x1, blocking collectives, per_device(): own = lax.all_gather(own, 'seq', axis_index_groups=columns)  24 us
    all_to_all x1, blocking collectives, per_device(): lax.all_to_all(parts, 'seq', 0, 0, axis_index_groups=row_groups, tiled=True)  13.9 us
    pallas_call x6, Pallas kernels, call(): pl.pallas_call(body, out_shape=[jax.ShapeDtypeStruct(shape, kind) for sha...  10.6 us
    all_to_all x1, blocking collectives, per_device(): lax.all_to_all(qkv, 'seq', 0, 0, axis_index_groups=row_groups, tiled=True)  10.1 us
    all_to_all x1, starting transfers between devices, per_device(): lax.all_to_all(tokens, 'seq', 0, 0, axis_index_groups=row_groups, tiled=T...  9.4 us
    ppermute x1, starting transfers between devices, per_device(): next_input = lax.ppermute(layer_out, 'section', ring)  7.26 us
    all_gather x1, waiting for transfers between devices, per_device(): weights = lax.all_gather(qkv, 'seq', axis_index_groups=columns)  6.55 us
    ppermute x1, waiting for transfers between devices, per_device(): prev_grad = lax.ppermute(input_grad, 'section', [(b, a) for a, b in ring])  2.44 us
  transfers between devices with their start and end apart: 5, of which 3 were waited for; matrix products, arithmetic and copies ran while one was open for 0% of the time, Pallas kernels for 3%

profile of v7, /device:TPU:1, one launch (start us, length us, event | category | flops | bytes accessed | tf_op | source)
XLA Modules:
  0.0 103.4 jit_solution(13487529795116023104)
XLA Ops:
  7.2 0.0 all-gather.4.cloned.1.call-start
  7.2 1.7 %pack_weights.1 = bf16[4,3,32,256]{3,2,1,0:T(8,128)(2,1)} custom-call(bf16[32,1024]{1,0:T(8,128)(2,1)} %bitcast.18, bf16[32,1024]{1,0:T(8,128)(2,1)} %bitcast.19, bf16[32,1024]{1,0:T(8,128)(2,1)} %bitcast.20), custom_call_target="tpu_custom_call" | custom-call | flops 1000000 | bytes 1000000 | tf_op jit(solution)/shard_map/pack_weights/pallas_call | solution.py:183
  8.9 10.1 %all_to_all.15.after_hbm = bf16[4,3,32,256]{3,2,1,0:T(8,128)(2,1)} all-to-all(bf16[4,3,32,256]{3,2,1,0:T(8,128)(2,1)} %pack_weights.1), channel_id=1, replica_groups={{0,16,32,48},{64,80,96,112},{128,144,160,176},{192,208,224,240},{256,27..., dimensions={0} | all-to-all | bytes 393216 | tf_op jit(solution)/shard_map/all_to_all | solution.py:213
  19.0 0.0 all-gather.4.cloned.1.call-update
  19.0 1.5 %collective-permute-start = (bf16[32,1024]{1,0:T(8,128)(2,1)}, bf16[32,1024]{1,0:T(8,128)(2,1)S(1)}, u32[]{:S(2)}, u32[]{:S(2)}) collective-permute-start(bf16[32,1024]{1,0:T(8,128)(2,1)} %bitcast.23), channel_id=1, source_target_pairs={{0,0},{16,64},{32,128},{48,192},{64,256},{80,320},{96,384},{112,44... | collective-permute-start | bytes 196616 | tf_op jit(solution)/shard_map/ppermute | solution.py:203
  20.5 2.6 %pack_tokens.1 = bf16[4,3,64,1024]{3,2,1,0:T(8,128)(2,1)} custom-call(bf16[4,3,32,256]{3,2,1,0:T(8,128)(2,1)} %all_to_all.15.after_hbm, bf16[64,1024]{1,0:T(8,128)(2,1)} %bitcast.15, bf16[64,1024]{1,0:T(8,128)(2,1)} %bitcast.17, f32[64,1024]{1,0:T(8,128)} %bitcast.13), custom_call_target="tpu_custom_call" | custom-call | flops 1000000 | bytes 1000000 | tf_op jit(solution)/shard_map/pack_tokens/pallas_call | solution.py:183
  23.1 0.0 copy-start.3
  23.1 0.0 collective-permute-done
  23.2 9.4 %all-to-all-start.1 = ((bf16[4,3,64,1024]{3,2,1,0:T(8,128)(2,1)}), bf16[4,3,64,1024]{3,2,1,0:T(8,128)(2,1)S(1)}, u32[]{:S(2)}, u32[]{:S(2)}) async-start(bf16[4,3,64,1024]{3,2,1,0:T(8,128)(2,1)} %pack_tokens.1), calls=%async_computation.1 | async-start | bytes 3145728 | tf_op jit(solution)/shard_map/all_to_all | solution.py:231
  32.6 24.0 %all-gather.1 = bf16[256,1024]{1,0:T(8,128)(2,1)S(1)} all-gather(bf16[32,1024]{1,0:T(8,128)(2,1)S(1)} %collective-permute-done), channel_id=3, replica_groups={{0,64,128,192,256,320,384,448},{16,80,144,208,272,336,400,464},{32,96,1..., dimensions={0}, use_global_device_ids=true | all-gather | bytes 589824 | tf_op jit(solution)/shard_map/all_gather | solution.py:230
  56.5 0.0 all-to-all-done.1.tok_ref
  56.5 0.4 prepare.1
  56.9 6.6 %all-gather.4.cloned.1.call-done = bf16[32,3,32,256]{3,2,1,0:T(8,128)(2,1)} async-done(((bf16[4,3,32,256]{3,2,1,0:T(8,128)(2,1)}), bf16[32,3,32,256]{3,2,1,0:T(8,128)(2,1)}) %all-gather.4.cloned.1.call-update) | async-done | bytes 1572880 | tf_op jit(solution)/shard_map/all_gather | solution.py:214
  63.5 1.4 %copy-done = bf16[32,3,32,256]{3,2,1,0:T(8,128)(2,1)S(1)} copy-done((bf16[32,3,32,256]{3,2,1,0:T(8,128)(2,1)S(1)}, bf16[32,3,32,256]{3,2,1,0:T(8,128)(2,1)}, u32[]{:S(2)}) %copy-start) | copy-done | bytes 1572888
  64.9 5.1 %layer.1 = bf16[4,2,64,1024]{3,2,1,0:T(8,128)(2,1)S(1)} custom-call(bf16[4,3,64,1024]{3,2,1,0:T(8,128)(2,1)S(1)} %all-to-all-done.1.tok_ref, bf16[2,256,1024]{2,1,0:T(8,128)(2,1)S(1)} %get-tuple-element.11.normed_ref, f32[256,128]{1,0:T(8,128)S(1)} %get-tuple-element.12.inv_ref, f32[1,1024]{1,0:T(1,128)S(1)} %copy-done.3, ...), custom_call_target="tpu_custom_call" | custom-call | flops 1500000000 | bytes 1000000 | tf_op jit(solution)/shard_map/layer/pallas_call | solution.py:183
  70.0 0.0 copy-start.1
  70.0 0.0 copy-start.2
  70.0 13.9 %all_to_all.16.parts_ref = bf16[4,2,64,1024]{3,2,1,0:T(8,128)(2,1)S(1)} all-to-all(bf16[4,2,64,1024]{3,2,1,0:T(8,128)(2,1)S(1)} %layer.1), channel_id=1, replica_groups={{0,16,32,48},{64,80,96,112},{128,144,160,176},{192,208,224,240},{256,27..., dimensions={0} | all-to-all | bytes 2097152 | tf_op jit(solution)/shard_map/all_to_all | solution.py:246
  83.9 0.2 finish.1
  84.1 7.3 %collective-permute-start.1 = (bf16[64,1024]{1,0:T(8,128)(2,1)S(1)}, bf16[64,1024]{1,0:T(8,128)(2,1)S(1)}, u32[]{:S(2)}, u32[]{:S(2)}) collective-permute-start(bf16[64,1024]{1,0:T(8,128)(2,1)S(1)} %get-tuple-element.14), channel_id=1, source_target_pairs={{0,1},{1,2},{2,3},{3,4},{4,5},{5,6},{6,7},{7,8},{8,9},{9,10},{10,1... | collective-permute-start | bytes 393224 | tf_op jit(solution)/shard_map/ppermute | solution.py:254
  91.4 0.0 collective-permute-start.2
  91.4 1.9 %collective-permute-done.1.next_ref = bf16[64,1024]{1,0:T(8,128)(2,1)S(1)} collective-permute-done((bf16[64,1024]{1,0:T(8,128)(2,1)S(1)}, bf16[64,1024]{1,0:T(8,128)(2,1)S(1)}, u32[]{:S(2)}, u32[]{:S(2)}) %collective-permute-start.1) | collective-permute-done | bytes 131104 | tf_op jit(solution)/shard_map/ppermute | solution.py:254
  93.3 2.4 %collective-permute-done.2.prev_ref = bf16[64,1024]{1,0:T(8,128)(2,1)S(1)} collective-permute-done((bf16[64,1024]{1,0:T(8,128)(2,1)S(1)}, bf16[64,1024]{1,0:T(8,128)(2,1)S(1)}, u32[]{:S(2)}, u32[]{:S(2)}) %collective-permute-start.2) | collective-permute-done | bytes 131104 | tf_op jit(solution)/shard_map/ppermute | solution.py:255
  95.7 0.8 deliver.1
  (4 shorter events, 0.0 us)
Async XLA Ops:
  7.2 56.3 %all-gather.4.cloned.1.call-start = ((), (), s32[]{:S(2)}) async-start(), calls=%async_computation.3 | async-start | bytes 1769472 | tf_op jit(solution)/shard_map/all_gather | solution.py:214
  19.0 4.1 %collective-permute-start = (bf16[32,1024]{1,0:T(8,128)(2,1)}, bf16[32,1024]{1,0:T(8,128)(2,1)S(1)}, u32[]{:S(2)}, u32[]{:S(2)}) collective-permute-start(bf16[32,1024]{1,0:T(8,128)(2,1)} %bitcast.23), channel_id=1, source_target_pairs={{0,0},{16,64},{32,128},{48,192},{64,256},{80,320},{96,384},{112,44... | collective-permute-start | bytes 196616 | tf_op jit(solution)/shard_map/ppermute | solution.py:203
  23.1 33.4 %copy-start.3 = (f32[1,1024]{1,0:T(1,128)S(1)}, f32[1,1024]{1,0:T(1,128)}, u32[]{:S(2)}) copy-start(f32[1,1024]{1,0:T(1,128)} %gain_ref.3) | copy-start | bytes 12292
  23.2 33.4 %all-to-all-start.1 = ((bf16[4,3,64,1024]{3,2,1,0:T(8,128)(2,1)}), bf16[4,3,64,1024]{3,2,1,0:T(8,128)(2,1)S(1)}, u32[]{:S(2)}, u32[]{:S(2)}) async-start(bf16[4,3,64,1024]{3,2,1,0:T(8,128)(2,1)} %pack_tokens.1), calls=%async_computation.1 | async-start | bytes 3145728 | tf_op jit(solution)/shard_map/all_to_all | solution.py:231
  63.5 1.4 %copy-start = (bf16[32,3,32,256]{3,2,1,0:T(8,128)(2,1)S(1)}, bf16[32,3,32,256]{3,2,1,0:T(8,128)(2,1)}, u32[]{:S(2)}) copy-start(bf16[32,3,32,256]{3,2,1,0:T(8,128)(2,1)} %all-gather.4.cloned.1.call-done) | copy-start | bytes 4718596
  70.0 14.0 %copy-start.1 = (f32[1,64,1024]{2,1,0:T(8,128)S(1)}, f32[1,64,1024]{2,1,0:T(8,128)}, u32[]{:S(2)}) copy-start(f32[1,64,1024]{2,1,0:T(8,128)} %param.10) | copy-start | bytes 786436
  70.0 14.0 %copy-start.2 = (bf16[1,64,1024]{2,1,0:T(8,128)(2,1)S(1)}, bf16[1,64,1024]{2,1,0:T(8,128)(2,1)}, u32[]{:S(2)}) copy-start(bf16[1,64,1024]{2,1,0:T(8,128)(2,1)} %param.8) | copy-start | bytes 393220
  84.1 9.2 %collective-permute-start.1 = (bf16[64,1024]{1,0:T(8,128)(2,1)S(1)}, bf16[64,1024]{1,0:T(8,128)(2,1)S(1)}, u32[]{:S(2)}, u32[]{:S(2)}) collective-permute-start(bf16[64,1024]{1,0:T(8,128)(2,1)S(1)} %get-tuple-element.14), channel_id=1, source_target_pairs={{0,1},{1,2},{2,3},{3,4},{4,5},{5,6},{6,7},{7,8},{8,9},{9,10},{10,1... | collective-permute-start | bytes 393224 | tf_op jit(solution)/shard_map/ppermute | solution.py:254
  91.4 4.4 %collective-permute-start.2 = (bf16[64,1024]{1,0:T(8,128)(2,1)S(1)}, bf16[64,1024]{1,0:T(8,128)(2,1)S(1)}, u32[]{:S(2)}, u32[]{:S(2)}) collective-permute-start(bf16[64,1024]{1,0:T(8,128)(2,1)S(1)} %get-tuple-element.15), channel_id=1, source_target_pairs={{1,0},{2,1},{3,2},{4,3},{5,4},{6,5},{7,6},{8,7},{9,8},{10,9},{11,1... | collective-permute-start | bytes 393224 | tf_op jit(solution)/shard_map/ppermute | solution.py:255
Sparse Core Ops, SparseCore 0:
  19.2 44.2 all-gather.3

commit v8 on v7

--- a/solution.py
+++ b/solution.py
@@ -226,7 +226,7 @@
         ),
         mib=63,
     )
-    own, tokens = lax.optimization_barrier((own, tokens))
+    own, _ = lax.optimization_barrier((own, tokens))
     own = lax.all_gather(own, "seq", axis_index_groups=columns)
     tokens = lax.all_to_all(tokens, "seq", 0, 0, axis_index_groups=row_groups, tiled=True)
     normed, inv = call(

time: 104 us -> 111 us (1.067)
  the two profiles are of different devices: /device:TPU:1 before, /device:TPU:201 now
where the time goes in v8:
time: 111 us; the launch traced here: 110 us
  blocking collectives  47.5 us (43%)
  starting transfers between devices  27.5 us (25%)
  between operations  14.1 us (13%)
  Pallas kernels  10.6 us (10%)
  waiting for transfers between devices  8.88 us (8%)
  local copies, waits for them, and re-layouts  1.43 us (1%)
    all_gather x1, blocking collectives, per_device(): own = lax.all_gather(own, 'seq', axis_index_groups=columns)  24.7 us
    ppermute x1, starting transfers between devices, per_device(): next_input = lax.ppermute(layer_out, 'section', ring)  17.4 us
    all_to_all x1, blocking collectives, per_device(): lax.all_to_all(parts, 'seq', 0, 0, axis_index_groups=row_groups, tiled=True)  13.4 us
    pallas_call x6, Pallas kernels, call(): pl.pallas_call(body, out_shape=[jax.ShapeDtypeStruct(shape, kind) for sha...  10.6 us
    all_to_all x1, blocking collectives, per_device(): lax.all_to_all(qkv, 'seq', 0, 0, axis_index_groups=row_groups, tiled=True)  9.31 us
    ppermute x1, starting transfers between devices, per_device(): own = lax.ppermute(w_out[0], 'seq', places)  6.44 us
    all_to_all x1, starting transfers between devices, per_device(): lax.all_to_all(tokens, 'seq', 0, 0, axis_index_groups=row_groups, tiled=T...  3.71 us
    ppermute x1, waiting for transfers between devices, per_device(): prev_grad = lax.ppermute(input_grad, 'section', [(b, a) for a, b in ring])  3.66 us
  transfers between devices with their start and end apart: 5, of which 4 were waited for; matrix products, arithmetic and copies ran while one was open for 0% of the time, Pallas kernels for 3%

profile of v8, /device:TPU:201, one launch (start us, length us, event | category | flops | bytes accessed | tf_op | source)
XLA Modules:
  0.0 110.0 jit_solution(15222329002983155319)
XLA Ops:
  7.2 0.0 all-gather.4.cloned.1.call-start
  7.2 1.7 %pack_weights.1 = bf16[4,3,32,256]{3,2,1,0:T(8,128)(2,1)} custom-call(bf16[32,1024]{1,0:T(8,128)(2,1)} %bitcast.18, bf16[32,1024]{1,0:T(8,128)(2,1)} %bitcast.19, bf16[32,1024]{1,0:T(8,128)(2,1)} %bitcast.20), custom_call_target="tpu_custom_call" | custom-call | flops 1000000 | bytes 1000000 | tf_op jit(solution)/shard_map/pack_weights/pallas_call | solution.py:183
  8.9 9.3 %all_to_all.15.after_hbm = bf16[4,3,32,256]{3,2,1,0:T(8,128)(2,1)} all-to-all(bf16[4,3,32,256]{3,2,1,0:T(8,128)(2,1)} %pack_weights.1), channel_id=1, replica_groups={{0,16,32,48},{64,80,96,112},{128,144,160,176},{192,208,224,240},{256,27..., dimensions={0} | all-to-all | bytes 393216 | tf_op jit(solution)/shard_map/all_to_all | solution.py:213
  18.2 0.0 all-gather.4.cloned.1.call-update
  18.2 2.6 %pack_tokens.1 = bf16[4,3,64,1024]{3,2,1,0:T(8,128)(2,1)} custom-call(bf16[4,3,32,256]{3,2,1,0:T(8,128)(2,1)} %all_to_all.15.after_hbm, bf16[64,1024]{1,0:T(8,128)(2,1)} %bitcast.15, bf16[64,1024]{1,0:T(8,128)(2,1)} %bitcast.17, f32[64,1024]{1,0:T(8,128)} %bitcast.13), custom_call_target="tpu_custom_call" | custom-call | flops 1000000 | bytes 1000000 | tf_op jit(solution)/shard_map/pack_tokens/pallas_call | solution.py:183
  20.8 0.0 copy-start.4
  20.8 0.0 copy-start.3
  20.8 3.7 %all-to-all-start.1 = ((bf16[4,3,64,1024]{3,2,1,0:T(8,128)(2,1)}), bf16[4,3,64,1024]{3,2,1,0:T(8,128)(2,1)S(1)}, u32[]{:S(2)}, u32[]{:S(2)}) async-start(bf16[4,3,64,1024]{3,2,1,0:T(8,128)(2,1)} %pack_tokens.1), calls=%async_computation.1 | async-start | bytes 3145728 | tf_op jit(solution)/shard_map/all_to_all | solution.py:231
  24.6 6.4 %collective-permute-start = (bf16[32,1024]{1,0:T(8,128)(2,1)S(1)}, bf16[32,1024]{1,0:T(8,128)(2,1)S(1)}, u32[]{:S(2)}, u32[]{:S(2)}) collective-permute-start(bf16[32,1024]{1,0:T(8,128)(2,1)S(1)} %bitcast.23), channel_id=1, source_target_pairs={{0,0},{16,64},{32,128},{48,192},{64,256},{80,320},{96,384},{112,44... | collective-permute-start | bytes 196616 | tf_op jit(solution)/shard_map/ppermute | solution.py:203
  31.0 1.3 %collective-permute-done = bf16[32,1024]{1,0:T(8,128)(2,1)S(1)} collective-permute-done((bf16[32,1024]{1,0:T(8,128)(2,1)S(1)}, bf16[32,1024]{1,0:T(8,128)(2,1)S(1)}, u32[]{:S(2)}, u32[]{:S(2)}) %collective-permute-start) | collective-permute-done | bytes 65568 | tf_op jit(solution)/shard_map/ppermute | solution.py:203
  32.3 24.7 %all-gather.1 = bf16[256,1024]{1,0:T(8,128)(2,1)S(1)} all-gather(bf16[32,1024]{1,0:T(8,128)(2,1)S(1)} %collective-permute-done), channel_id=3, replica_groups={{0,64,128,192,256,320,384,448},{16,80,144,208,272,336,400,464},{32,96,1..., dimensions={0}, use_global_device_ids=true | all-gather | bytes 589824 | tf_op jit(solution)/shard_map/all_gather | solution.py:230
  57.1 0.0 all-to-all-done.1.tok_ref
  57.1 0.4 prepare.1
  57.5 1.9 %all-gather.4.cloned.1.call-done = bf16[32,3,32,256]{3,2,1,0:T(8,128)(2,1)} async-done(((bf16[4,3,32,256]{3,2,1,0:T(8,128)(2,1)}), bf16[32,3,32,256]{3,2,1,0:T(8,128)(2,1)}) %all-gather.4.cloned.1.call-update) | async-done | bytes 1572880 | tf_op jit(solution)/shard_map/all_gather | solution.py:214
  59.4 1.4 %copy-done = bf16[32,3,32,256]{3,2,1,0:T(8,128)(2,1)S(1)} copy-done((bf16[32,3,32,256]{3,2,1,0:T(8,128)(2,1)S(1)}, bf16[32,3,32,256]{3,2,1,0:T(8,128)(2,1)}, u32[]{:S(2)}) %copy-start) | copy-done | bytes 1572888
  60.8 5.1 %layer.1 = bf16[4,2,64,1024]{3,2,1,0:T(8,128)(2,1)S(1)} custom-call(bf16[4,3,64,1024]{3,2,1,0:T(8,128)(2,1)S(1)} %all-to-all-done.1.tok_ref, bf16[2,256,1024]{2,1,0:T(8,128)(2,1)S(1)} %get-tuple-element.9.normed_ref, f32[256,128]{1,0:T(8,128)S(1)} %get-tuple-element.10.inv_ref, f32[1,1024]{1,0:T(1,128)S(1)} %copy-done.3, ...), custom_call_target="tpu_custom_call" | custom-call | flops 1500000000 | bytes 1000000 | tf_op jit(solution)/shard_map/layer/pallas_call | solution.py:183
  65.9 0.0 copy-start.1
  65.9 0.0 copy-start.2
  65.9 13.4 %all_to_all.16.parts_ref = bf16[4,2,64,1024]{3,2,1,0:T(8,128)(2,1)S(1)} all-to-all(bf16[4,2,64,1024]{3,2,1,0:T(8,128)(2,1)S(1)} %layer.1), channel_id=1, replica_groups={{0,16,32,48},{64,80,96,112},{128,144,160,176},{192,208,224,240},{256,27..., dimensions={0} | all-to-all | bytes 2097152 | tf_op jit(solution)/shard_map/all_to_all | solution.py:246
  79.3 0.2 finish.1
  79.5 17.4 %collective-permute-start.1 = (bf16[64,1024]{1,0:T(8,128)(2,1)S(1)}, bf16[64,1024]{1,0:T(8,128)(2,1)S(1)}, u32[]{:S(2)}, u32[]{:S(2)}) collective-permute-start(bf16[64,1024]{1,0:T(8,128)(2,1)S(1)} %get-tuple-element.12), channel_id=1, source_target_pairs={{0,1},{1,2},{2,3},{3,4},{4,5},{5,6},{6,7},{7,8},{8,9},{9,10},{10,1... | collective-permute-start | bytes 393224 | tf_op jit(solution)/shard_map/ppermute | solution.py:254
  96.8 1.9 %collective-permute-done.1.next_ref = bf16[64,1024]{1,0:T(8,128)(2,1)S(1)} collective-permute-done((bf16[64,1024]{1,0:T(8,128)(2,1)S(1)}, bf16[64,1024]{1,0:T(8,128)(2,1)S(1)}, u32[]{:S(2)}, u32[]{:S(2)}) %collective-permute-start.1) | collective-permute-done | bytes 131104 | tf_op jit(solution)/shard_map/ppermute | solution.py:254
  98.8 3.7 %collective-permute-done.2.prev_ref = bf16[64,1024]{1,0:T(8,128)(2,1)S(1)} collective-permute-done((bf16[64,1024]{1,0:T(8,128)(2,1)S(1)}, bf16[64,1024]{1,0:T(8,128)(2,1)S(1)}, u32[]{:S(2)}, u32[]{:S(2)}) %collective-permute-start.2) | collective-permute-done | bytes 131104 | tf_op jit(solution)/shard_map/ppermute | solution.py:255
  102.4 0.8 deliver.1
  (6 shorter events, 0.0 us)
Async XLA Ops:
  7.2 52.2 %all-gather.4.cloned.1.call-start = ((), (), s32[]{:S(2)}) async-start(), calls=%async_computation.3 | async-start | bytes 1769472 | tf_op jit(solution)/shard_map/all_gather | solution.py:214
  20.8 3.7 %copy-start.4 = (bf16[1,32,1024]{2,1,0:T(8,128)(2,1)S(1)}, bf16[1,32,1024]{2,1,0:T(8,128)(2,1)}, u32[]{:S(2)}) copy-start(bf16[1,32,1024]{2,1,0:T(8,128)(2,1)} %param.15) | copy-start | bytes 196612
  20.8 36.2 %copy-start.3 = (f32[1,1024]{1,0:T(1,128)S(1)}, f32[1,1024]{1,0:T(1,128)}, u32[]{:S(2)}) copy-start(f32[1,1024]{1,0:T(1,128)} %gain_ref.3) | copy-start | bytes 12292
  20.8 36.2 %all-to-all-start.1 = ((bf16[4,3,64,1024]{3,2,1,0:T(8,128)(2,1)}), bf16[4,3,64,1024]{3,2,1,0:T(8,128)(2,1)S(1)}, u32[]{:S(2)}, u32[]{:S(2)}) async-start(bf16[4,3,64,1024]{3,2,1,0:T(8,128)(2,1)} %pack_tokens.1), calls=%async_computation.1 | async-start | bytes 3145728 | tf_op jit(solution)/shard_map/all_to_all | solution.py:231
  24.6 7.8 %collective-permute-start = (bf16[32,1024]{1,0:T(8,128)(2,1)S(1)}, bf16[32,1024]{1,0:T(8,128)(2,1)S(1)}, u32[]{:S(2)}, u32[]{:S(2)}) collective-permute-start(bf16[32,1024]{1,0:T(8,128)(2,1)S(1)} %bitcast.23), channel_id=1, source_target_pairs={{0,0},{16,64},{32,128},{48,192},{64,256},{80,320},{96,384},{112,44... | collective-permute-start | bytes 196616 | tf_op jit(solution)/shard_map/ppermute | solution.py:203
  59.4 1.4 %copy-start = (bf16[32,3,32,256]{3,2,1,0:T(8,128)(2,1)S(1)}, bf16[32,3,32,256]{3,2,1,0:T(8,128)(2,1)}, u32[]{:S(2)}) copy-start(bf16[32,3,32,256]{3,2,1,0:T(8,128)(2,1)} %all-gather.4.cloned.1.call-done) | copy-start | bytes 4718596
  65.9 13.4 %copy-start.1 = (f32[1,64,1024]{2,1,0:T(8,128)S(1)}, f32[1,64,1024]{2,1,0:T(8,128)}, u32[]{:S(2)}) copy-start(f32[1,64,1024]{2,1,0:T(8,128)} %param.10) | copy-start | bytes 786436
  65.9 13.4 %copy-start.2 = (bf16[1,64,1024]{2,1,0:T(8,128)(2,1)S(1)}, bf16[1,64,1024]{2,1,0:T(8,128)(2,1)}, u32[]{:S(2)}) copy-start(bf16[1,64,1024]{2,1,0:T(8,128)(2,1)} %param.8) | copy-start | bytes 393220
  79.5 19.3 %collective-permute-start.1 = (bf16[64,1024]{1,0:T(8,128)(2,1)S(1)}, bf16[64,1024]{1,0:T(8,128)(2,1)S(1)}, u32[]{:S(2)}, u32[]{:S(2)}) collective-permute-start(bf16[64,1024]{1,0:T(8,128)(2,1)S(1)} %get-tuple-element.12), channel_id=1, source_target_pairs={{0,1},{1,2},{2,3},{3,4},{4,5},{5,6},{6,7},{7,8},{8,9},{9,10},{10,1... | collective-permute-start | bytes 393224 | tf_op jit(solution)/shard_map/ppermute | solution.py:254
  96.8 5.6 %collective-permute-start.2 = (bf16[64,1024]{1,0:T(8,128)(2,1)S(1)}, bf16[64,1024]{1,0:T(8,128)(2,1)S(1)}, u32[]{:S(2)}, u32[]{:S(2)}) collective-permute-start(bf16[64,1024]{1,0:T(8,128)(2,1)S(1)} %get-tuple-element.13), channel_id=1, source_target_pairs={{1,0},{2,1},{3,2},{4,3},{5,4},{6,5},{7,6},{8,7},{9,8},{10,9},{11,1... | collective-permute-start | bytes 393224 | tf_op jit(solution)/shard_map/ppermute | solution.py:255
Sparse Core Ops, SparseCore 0:
  18.3 41.0 all-gather.3

commit v9 on v7

--- a/solution.py
+++ b/solution.py
@@ -66,18 +66,23 @@
         copy.wait()
 
 
-def pack_tokens(after_hbm, fwd_hbm, bwd_hbm, grad_hbm, out_ref, grad_ref, sems, grad_sem):
+def pack_tokens(after_hbm, fwd_hbm, bwd_hbm, grad_hbm, out_hbm, grad_ref, low_ref, sems, in_sems):
     del after_hbm
-    first = pltpu.make_async_copy(grad_hbm, grad_ref, grad_sem)
-    first.start()
+    loads = [
+        pltpu.make_async_copy(fwd_hbm, low_ref.at[0], in_sems.at[0]),
+        pltpu.make_async_copy(bwd_hbm, low_ref.at[1], in_sems.at[1]),
+        pltpu.make_async_copy(grad_hbm, grad_ref, in_sems.at[2]),
+    ]
+    for load in loads:
+        load.start()
     copies = []
-    for to in range(GROUP):
-        for i, ref in enumerate((fwd_hbm, bwd_hbm)):
-            copies.append(pltpu.make_async_copy(ref, out_ref.at[to, i], sems.at[to, i]))
+    for i, load in enumerate(loads):
+        load.wait()
+        if i == 2:
+            low_ref[2] = grad_ref[...].astype(BF16)
+        for to in range(GROUP):
+            copies.append(pltpu.make_async_copy(low_ref.at[i], out_hbm.at[to, i], sems.at[to, i]))
             copies[-1].start()
-    first.wait()
-    for to in range(GROUP):
-        out_ref[to, 2] = grad_ref[...].astype(BF16)
     for copy in copies:
         copy.wait()
 
@@ -221,10 +226,12 @@
         in_specs=[HBM] * 4,
         scratch=(
             pltpu.VMEM((64, 1024), F32),
-            pltpu.SemaphoreType.DMA((GROUP, 2)),
-            pltpu.SemaphoreType.DMA,
+            pltpu.VMEM((3, 64, 1024), BF16),
+            pltpu.SemaphoreType.DMA((GROUP, 3)),
+            pltpu.SemaphoreType.DMA((3,)),
         ),
         mib=63,
+        out=HBM,
     )
     own, tokens = lax.optimization_barrier((own, tokens))
     own = lax.all_gather(own, "seq", axis_index_groups=columns)

time: 104 us -> 104 us (level)
  transfers between devices with their start and end apart: 5 -> 5, of which waited for: 3 -> 3; matrix products, arithmetic and copies ran while one was open for 0% -> 0% of each run, Pallas kernels for 3% -> 2%
where the time goes in v9:
time: 104 us; the launch traced here: 103 us
  blocking collectives  48.9 us (47%)
  starting transfers between devices  18 us (17%)
  between operations  14.1 us (14%)
  waiting for transfers between devices  10.7 us (10%)
  Pallas kernels  10.2 us (10%)
  local copies, waits for them, and re-layouts  1.43 us (1%)
    all_gather x1, blocking collectives, per_device(): own = lax.all_gather(own, 'seq', axis_index_groups=columns)  24.1 us
    all_to_all x1, blocking collectives, per_device(): lax.all_to_all(parts, 'seq', 0, 0, axis_index_groups=row_groups, tiled=True)  14.7 us
    pallas_call x6, Pallas kernels, call(): pl.pallas_call(body, out_shape=[jax.ShapeDtypeStruct(shape, kind) for sha...  10.2 us
    all_to_all x1, blocking collectives, per_device(): lax.all_to_all(qkv, 'seq', 0, 0, axis_index_groups=row_groups, tiled=True)  10.1 us
    all_to_all x1, starting transfers between devices, per_device(): lax.all_to_all(tokens, 'seq', 0, 0, axis_index_groups=row_groups, tiled=T...  9.8 us
    ppermute x1, starting transfers between devices, per_device(): next_input = lax.ppermute(layer_out, 'section', ring)  6.7 us
    all_gather x1, waiting for transfers between devices, per_device(): weights = lax.all_gather(qkv, 'seq', axis_index_groups=columns)  6.25 us
    ppermute x1, waiting for transfers between devices, per_device(): prev_grad = lax.ppermute(input_grad, 'section', [(b, a) for a, b in ring])  2.44 us
  transfers between devices with their start and end apart: 5, of which 3 were waited for; matrix products, arithmetic and copies ran while one was open for 0% of the time, Pallas kernels for 2%

profile of v9, /device:TPU:1, one launch (start us, length us, event | category | flops | bytes accessed | tf_op | source)
XLA Modules:
  0.0 103.4 jit_solution(8857214410369252791)
XLA Ops:
  7.2 0.0 all-gather.4.cloned.1.call-start
  7.2 1.7 %pack_weights.1 = bf16[4,3,32,256]{3,2,1,0:T(8,128)(2,1)} custom-call(bf16[32,1024]{1,0:T(8,128)(2,1)} %bitcast.18, bf16[32,1024]{1,0:T(8,128)(2,1)} %bitcast.19, bf16[32,1024]{1,0:T(8,128)(2,1)} %bitcast.20), custom_call_target="tpu_custom_call" | custom-call | flops 1000000 | bytes 1000000 | tf_op jit(solution)/shard_map/pack_weights/pallas_call | solution.py:188
  8.9 10.1 %all_to_all.15.after_hbm = bf16[4,3,32,256]{3,2,1,0:T(8,128)(2,1)} all-to-all(bf16[4,3,32,256]{3,2,1,0:T(8,128)(2,1)} %pack_weights.1), channel_id=1, replica_groups={{0,16,32,48},{64,80,96,112},{128,144,160,176},{192,208,224,240},{256,27..., dimensions={0} | all-to-all | bytes 393216 | tf_op jit(solution)/shard_map/all_to_all | solution.py:218
  19.0 0.0 all-gather.4.cloned.1.call-update
  19.0 1.5 %collective-permute-start = (bf16[32,1024]{1,0:T(8,128)(2,1)}, bf16[32,1024]{1,0:T(8,128)(2,1)S(1)}, u32[]{:S(2)}, u32[]{:S(2)}) collective-permute-start(bf16[32,1024]{1,0:T(8,128)(2,1)} %bitcast.23), channel_id=1, source_target_pairs={{0,0},{16,64},{32,128},{48,192},{64,256},{80,320},{96,384},{112,44... | collective-permute-start | bytes 196616 | tf_op jit(solution)/shard_map/ppermute | solution.py:208
  20.5 2.2 %pack_tokens.1 = bf16[4,3,64,1024]{3,2,1,0:T(8,128)(2,1)} custom-call(bf16[4,3,32,256]{3,2,1,0:T(8,128)(2,1)} %all_to_all.15.after_hbm, bf16[64,1024]{1,0:T(8,128)(2,1)} %bitcast.15, bf16[64,1024]{1,0:T(8,128)(2,1)} %bitcast.17, f32[64,1024]{1,0:T(8,128)} %bitcast.13), custom_call_target="tpu_custom_call" | custom-call | flops 1000000 | bytes 1000000 | tf_op jit(solution)/shard_map/pack_tokens/pallas_call | solution.py:188
  22.7 0.0 copy-start.3
  22.7 0.0 collective-permute-done
  22.7 9.8 %all-to-all-start.1 = ((bf16[4,3,64,1024]{3,2,1,0:T(8,128)(2,1)}), bf16[4,3,64,1024]{3,2,1,0:T(8,128)(2,1)S(1)}, u32[]{:S(2)}, u32[]{:S(2)}) async-start(bf16[4,3,64,1024]{3,2,1,0:T(8,128)(2,1)} %pack_tokens.1), calls=%async_computation.1 | async-start | bytes 3145728 | tf_op jit(solution)/shard_map/all_to_all | solution.py:238
  32.6 24.1 %all-gather.1 = bf16[256,1024]{1,0:T(8,128)(2,1)S(1)} all-gather(bf16[32,1024]{1,0:T(8,128)(2,1)S(1)} %collective-permute-done), channel_id=3, replica_groups={{0,64,128,192,256,320,384,448},{16,80,144,208,272,336,400,464},{32,96,1..., dimensions={0}, use_global_device_ids=true | all-gather | bytes 589824 | tf_op jit(solution)/shard_map/all_gather | solution.py:237
  56.6 0.0 all-to-all-done.1.tok_ref
  56.7 0.4 prepare.1
  57.1 6.3 %all-gather.4.cloned.1.call-done = bf16[32,3,32,256]{3,2,1,0:T(8,128)(2,1)} async-done(((bf16[4,3,32,256]{3,2,1,0:T(8,128)(2,1)}), bf16[32,3,32,256]{3,2,1,0:T(8,128)(2,1)}) %all-gather.4.cloned.1.call-update) | async-done | bytes 1572880 | tf_op jit(solution)/shard_map/all_gather | solution.py:219
  63.3 1.4 %copy-done = bf16[32,3,32,256]{3,2,1,0:T(8,128)(2,1)S(1)} copy-done((bf16[32,3,32,256]{3,2,1,0:T(8,128)(2,1)S(1)}, bf16[32,3,32,256]{3,2,1,0:T(8,128)(2,1)}, u32[]{:S(2)}) %copy-start) | copy-done | bytes 1572888
  64.7 5.1 %layer.1 = bf16[4,2,64,1024]{3,2,1,0:T(8,128)(2,1)S(1)} custom-call(bf16[4,3,64,1024]{3,2,1,0:T(8,128)(2,1)S(1)} %all-to-all-done.1.tok_ref, bf16[2,256,1024]{2,1,0:T(8,128)(2,1)S(1)} %get-tuple-element.11.normed_ref, f32[256,128]{1,0:T(8,128)S(1)} %get-tuple-element.12.inv_ref, f32[1,1024]{1,0:T(1,128)S(1)} %copy-done.3, ...), custom_call_target="tpu_custom_call" | custom-call | flops 1500000000 | bytes 1000000 | tf_op jit(solution)/shard_map/layer/pallas_call | solution.py:188
  69.8 0.0 copy-start.1
  69.8 0.0 copy-start.2
  69.8 14.7 %all_to_all.16.parts_ref = bf16[4,2,64,1024]{3,2,1,0:T(8,128)(2,1)S(1)} all-to-all(bf16[4,2,64,1024]{3,2,1,0:T(8,128)(2,1)S(1)} %layer.1), channel_id=1, replica_groups={{0,16,32,48},{64,80,96,112},{128,144,160,176},{192,208,224,240},{256,27..., dimensions={0} | all-to-all | bytes 2097152 | tf_op jit(solution)/shard_map/all_to_all | solution.py:253
  84.5 0.2 finish.1
  84.7 6.7 %collective-permute-start.1 = (bf16[64,1024]{1,0:T(8,128)(2,1)S(1)}, bf16[64,1024]{1,0:T(8,128)(2,1)S(1)}, u32[]{:S(2)}, u32[]{:S(2)}) collective-permute-start(bf16[64,1024]{1,0:T(8,128)(2,1)S(1)} %get-tuple-element.14), channel_id=1, source_target_pairs={{0,1},{1,2},{2,3},{3,4},{4,5},{5,6},{6,7},{7,8},{8,9},{9,10},{10,1... | collective-permute-start | bytes 393224 | tf_op jit(solution)/shard_map/ppermute | solution.py:261
  91.4 0.0 collective-permute-start.2
  91.4 1.9 %collective-permute-done.1.next_ref = bf16[64,1024]{1,0:T(8,128)(2,1)S(1)} collective-permute-done((bf16[64,1024]{1,0:T(8,128)(2,1)S(1)}, bf16[64,1024]{1,0:T(8,128)(2,1)S(1)}, u32[]{:S(2)}, u32[]{:S(2)}) %collective-permute-start.1) | collective-permute-done | bytes 131104 | tf_op jit(solution)/shard_map/ppermute | solution.py:261
  93.3 2.4 %collective-permute-done.2.prev_ref = bf16[64,1024]{1,0:T(8,128)(2,1)S(1)} collective-permute-done((bf16[64,1024]{1,0:T(8,128)(2,1)S(1)}, bf16[64,1024]{1,0:T(8,128)(2,1)S(1)}, u32[]{:S(2)}, u32[]{:S(2)}) %collective-permute-start.2) | collective-permute-done | bytes 131104 | tf_op jit(solution)/shard_map/ppermute | solution.py:262
  95.7 0.8 deliver.1
  (4 shorter events, 0.0 us)
Async XLA Ops:
  7.2 56.1 %all-gather.4.cloned.1.call-start = ((), (), s32[]{:S(2)}) async-start(), calls=%async_computation.3 | async-start | bytes 1769472 | tf_op jit(solution)/shard_map/all_gather | solution.py:219
  19.0 3.7 %collective-permute-start = (bf16[32,1024]{1,0:T(8,128)(2,1)}, bf16[32,1024]{1,0:T(8,128)(2,1)S(1)}, u32[]{:S(2)}, u32[]{:S(2)}) collective-permute-start(bf16[32,1024]{1,0:T(8,128)(2,1)} %bitcast.23), channel_id=1, source_target_pairs={{0,0},{16,64},{32,128},{48,192},{64,256},{80,320},{96,384},{112,44... | collective-permute-start | bytes 196616 | tf_op jit(solution)/shard_map/ppermute | solution.py:208
  22.7 33.9 %copy-start.3 = (f32[1,1024]{1,0:T(1,128)S(1)}, f32[1,1024]{1,0:T(1,128)}, u32[]{:S(2)}) copy-start(f32[1,1024]{1,0:T(1,128)} %gain_ref.3) | copy-start | bytes 12292
  22.7 33.9 %all-to-all-start.1 = ((bf16[4,3,64,1024]{3,2,1,0:T(8,128)(2,1)}), bf16[4,3,64,1024]{3,2,1,0:T(8,128)(2,1)S(1)}, u32[]{:S(2)}, u32[]{:S(2)}) async-start(bf16[4,3,64,1024]{3,2,1,0:T(8,128)(2,1)} %pack_tokens.1), calls=%async_computation.1 | async-start | bytes 3145728 | tf_op jit(solution)/shard_map/all_to_all | solution.py:238
  63.3 1.4 %copy-start = (bf16[32,3,32,256]{3,2,1,0:T(8,128)(2,1)S(1)}, bf16[32,3,32,256]{3,2,1,0:T(8,128)(2,1)}, u32[]{:S(2)}) copy-start(bf16[32,3,32,256]{3,2,1,0:T(8,128)(2,1)} %all-gather.4.cloned.1.call-done) | copy-start | bytes 4718596
  69.8 14.7 %copy-start.1 = (f32[1,64,1024]{2,1,0:T(8,128)S(1)}, f32[1,64,1024]{2,1,0:T(8,128)}, u32[]{:S(2)}) copy-start(f32[1,64,1024]{2,1,0:T(8,128)} %param.10) | copy-start | bytes 786436
  69.8 14.7 %copy-start.2 = (bf16[1,64,1024]{2,1,0:T(8,128)(2,1)S(1)}, bf16[1,64,1024]{2,1,0:T(8,128)(2,1)}, u32[]{:S(2)}) copy-start(bf16[1,64,1024]{2,1,0:T(8,128)(2,1)} %param.8) | copy-start | bytes 393220
  84.7 8.6 %collective-permute-start.1 = (bf16[64,1024]{1,0:T(8,128)(2,1)S(1)}, bf16[64,1024]{1,0:T(8,128)(2,1)S(1)}, u32[]{:S(2)}, u32[]{:S(2)}) collective-permute-start(bf16[64,1024]{1,0:T(8,128)(2,1)S(1)} %get-tuple-element.14), channel_id=1, source_target_pairs={{0,1},{1,2},{2,3},{3,4},{4,5},{5,6},{6,7},{7,8},{8,9},{9,10},{10,1... | collective-permute-start | bytes 393224 | tf_op jit(solution)/shard_map/ppermute | solution.py:261
  91.4 4.4 %collective-permute-start.2 = (bf16[64,1024]{1,0:T(8,128)(2,1)S(1)}, bf16[64,1024]{1,0:T(8,128)(2,1)S(1)}, u32[]{:S(2)}, u32[]{:S(2)}) collective-permute-start(bf16[64,1024]{1,0:T(8,128)(2,1)S(1)} %get-tuple-element.15), channel_id=1, source_target_pairs={{1,0},{2,1},{3,2},{4,3},{5,4},{6,5},{7,6},{8,7},{9,8},{10,9},{11,1... | collective-permute-start | bytes 393224 | tf_op jit(solution)/shard_map/ppermute | solution.py:262
Sparse Core Ops, SparseCore 0:
  19.2 44.1 all-gather.3
